TPU v7x, 32 devices: a whole 2x2x4 slice. The times are simulated.
32 devices in a mesh: clip: 8 (over z, x), tm: 4 (over y, core).
Axes of the slice: x: 2, y: 2, z: 4, core: 2. Of those that a mesh axis runs over, the one named last changes fastest.
Arguments:
- inputs: bfloat16 [32768, 512], P(('clip', 'tm')), may hold values from -6 to 6
- codes: int32 [32768, 8], P(('clip', 'tm')), may hold values from 0 to 2047
- levels: int32 [8], P('clip'), may hold values from 1 to 8, as said below
- attention_master: float32 [4, 512, 512], P(None, ('clip', 'tm'))
- attention_first: float32 [4, 512, 512], P(None, ('clip', 'tm'))
- attention_second: float32 [4, 512, 512], P(None, ('clip', 'tm'))
- feedforward_master: float32 [2, 512, 2048], P(None, ('clip', 'tm'))
- feedforward_first: float32 [2, 512, 2048], P(None, ('clip', 'tm'))
- feedforward_second: float32 [2, 512, 2048], P(None, ('clip', 'tm'))
- projection_master: float32 [512, 256], P(('clip', 'tm')), may hold values from -0.25 to 0.25
- projection_first: float32 [512, 256], P(('clip', 'tm'))
- projection_second: float32 [512, 256], P(('clip', 'tm'))
- codebook_master: float32 [8, 2048, 256], P(None, ('clip', 'tm')), may hold values from -3 to 3
- codebook_first: float32 [8, 2048, 256], P(None, ('clip', 'tm'))
- codebook_second: float32 [8, 2048, 256], P(None, ('clip', 'tm'))
- scales_master: float32 [6, 512], P(None, ('clip', 'tm'))
- scales_first: float32 [6, 512], P(None, ('clip', 'tm'))
- scales_second: float32 [6, 512], P(None, ('clip', 'tm'))
Outputs:
- latent: float32 [32768, 256], P(('clip', 'tm'))
- input_gradient: float32 [32768, 512], P(('clip', 'tm'))
- gradient_norm: float32 [], replicated
- attention_momentum: float32 [4, 512, 512], P(None, ('clip', 'tm'))
- attention_variance: float32 [4, 512, 512], P(None, ('clip', 'tm'))
- attention_updated: float32 [4, 512, 512], P(None, ('clip', 'tm'))
- attention_bfloat: bfloat16 [4, 512, 512], P(None, ('clip', 'tm'))
- feedforward_momentum: float32 [2, 512, 2048], P(None, ('clip', 'tm'))
- feedforward_variance: float32 [2, 512, 2048], P(None, ('clip', 'tm'))
- feedforward_updated: float32 [2, 512, 2048], P(None, ('clip', 'tm'))
- feedforward_bfloat: bfloat16 [2, 512, 2048], P(None, ('clip', 'tm'))
- projection_momentum: float32 [512, 256], P(('clip', 'tm'))
- projection_variance: float32 [512, 256], P(('clip', 'tm'))
- projection_updated: float32 [512, 256], P(('clip', 'tm'))
- projection_bfloat: bfloat16 [512, 256], P(('clip', 'tm'))
- codebook_momentum: float32 [8, 2048, 256], P(None, ('clip', 'tm'))
- codebook_variance: float32 [8, 2048, 256], P(None, ('clip', 'tm'))
- codebook_updated: float32 [8, 2048, 256], P(None, ('clip', 'tm'))
- codebook_bfloat: bfloat16 [8, 2048, 256], P(None, ('clip', 'tm'))
- scales_momentum: float32 [6, 512], P(None, ('clip', 'tm'))
- scales_variance: float32 [6, 512], P(None, ('clip', 'tm'))
- scales_updated: float32 [6, 512], P(None, ('clip', 'tm'))
- scales_bfloat: bfloat16 [6, 512], P(None, ('clip', 'tm'))
Inputs may be any that keep to these rules, and one draw needn't show every extreme that they name: Some clip has 8 active levels and some clip has 1.
All inputs are finite; a program needn't handle non-finite values.
Results may differ from a plain program's by a relative error of at most 0.01.
The roundings to bfloat16 on the way count: a program that leaves them out, or rounds other values in their place, can miss the bound.
Values may be sent and summed in bfloat16 or wider, within the bound.
No kernel may reach another device: no remote copies, remote signals or barrier semaphores. Data moves between devices by JAX's collectives and lax.ppermute only.
A program may use at most 192 MiB of HBM per device.

v0:
```python
from functools import partial
import math

import jax
import jax.numpy as jnp
from jax import lax
from jax.sharding import PartitionSpec as P

HEADS = 8
LEVELS = 8
WINDOW = 250
STEP = 10


clip_level = 1.0
beta_first = 0.9
beta_second = 0.95
adam_floor = 1e-08
weight_decay = 0.1
group_rates = (0.05, 0.03, 0.05, 0.5, 0.5)
masked_score = -1e30


def from_behind(block, axis, distance):
    devices = range(lax.axis_size(axis))
    route = [(i - distance, i) for i in devices if i - distance in devices]
    return lax.ppermute(block, axis, route)


def normalize(values, gain, shift):
    centre = jnp.mean(values, axis=-1, keepdims=True)
    centred = values - centre
    spread = jnp.mean(centred * centred, axis=-1, keepdims=True)
    return centred * lax.rsqrt(spread + 1e-05) * gain + shift


def rotary(values, positions, turning):
    half_depth = values.shape[-1] // 2
    freqs_table = jnp.exp(
        -math.log(10000.0) * jnp.arange(half_depth, dtype=jnp.float32) * 2.0 / values.shape[-1]
    )
    angles = positions.astype(jnp.float32)[:, None] * freqs_table[None, :]
    cosine = jnp.cos(angles)[:, None, :]
    sine = turning * jnp.sin(angles)[:, None, :]
    former = values[..., :half_depth]
    latter = values[..., half_depth:]
    return jnp.concatenate(
        [former * cosine - latter * sine, former * sine + latter * cosine], axis=-1
    )


def block_mask(row_start, block_rows, key_span, margin, offset):
    query_place = jnp.arange(block_rows, dtype=jnp.int32)[:, None]
    key_place = jnp.arange(key_span, dtype=jnp.int32)[None, :]
    distance = margin + query_place - key_place
    reach = offset + row_start + key_place - margin
    return (distance >= 0) & (distance <= WINDOW) & (reach >= 0)


def head_forward(query_head, key_head, value_head, allowed, score_scale):
    scores = (
        jnp.einsum("qd,kd->qk", query_head, key_head, preferred_element_type=jnp.float32)
        * score_scale
    )
    scores = jnp.where(allowed, scores, masked_score)
    highest_score = jnp.max(scores, axis=-1, keepdims=True)
    raised = jnp.exp(scores - highest_score)
    totals = jnp.sum(raised, axis=-1, keepdims=True)
    weights = (raised / totals).astype(jnp.bfloat16)
    output = jnp.dot(weights, value_head, preferred_element_type=jnp.float32)
    return (output, highest_score[:, 0] + jnp.log(totals[:, 0]))


def head_backward(query_head, key_head, value_head, grad_head, logsum, allowed, score_scale):
    scores = (
        jnp.einsum("qd,kd->qk", query_head, key_head, preferred_element_type=jnp.float32)
        * score_scale
    )
    scores = jnp.where(allowed, scores, masked_score)
    weights = jnp.exp(scores - logsum[:, None])
    grad_weights = jnp.einsum(
        "qd,kd->qk", grad_head, value_head, preferred_element_type=jnp.float32
    )
    row_inner = jnp.sum(weights * grad_weights, axis=-1, keepdims=True)
    grad_scores = (weights * (grad_weights - row_inner)).astype(jnp.bfloat16)
    grad_query = (
        jnp.einsum("qk,kd->qd", grad_scores, key_head, preferred_element_type=jnp.float32)
        * score_scale
    )
    grad_key = (
        jnp.einsum("qk,qd->kd", grad_scores, query_head, preferred_element_type=jnp.float32)
        * score_scale
    )
    grad_value = jnp.einsum(
        "qk,qd->kd", weights.astype(jnp.bfloat16), grad_head, preferred_element_type=jnp.float32
    )
    return (grad_query, grad_key, grad_value)


def attend_forward(query_heads, key_heads, value_heads, offset):
    frame_count = query_heads.shape[1]
    block_rows = min(512, frame_count)
    margin = key_heads.shape[1] - frame_count
    key_span = block_rows + margin
    score_scale = 1.0 / math.sqrt(query_heads.shape[2])
    outputs = []
    logsums = []
    for block_index in range(frame_count // block_rows):
        row_start = block_index * block_rows
        allowed = block_mask(row_start, block_rows, key_span, margin, offset)

        def per_head(operands):
            return head_forward(operands[0], operands[1], operands[2], allowed, score_scale)

        output, logsum = lax.map(
            per_head,
            (
                query_heads[:, row_start : row_start + block_rows],
                key_heads[:, row_start : row_start + key_span],
                value_heads[:, row_start : row_start + key_span],
            ),
        )
        outputs.append(output)
        logsums.append(logsum)
    return (jnp.concatenate(outputs, axis=1), jnp.concatenate(logsums, axis=1))


def attend_backward(query_heads, key_heads, value_heads, grad_heads, logsums, offset):
    frame_count = query_heads.shape[1]
    block_rows = min(512, frame_count)
    margin = key_heads.shape[1] - frame_count
    key_span = block_rows + margin
    score_scale = 1.0 / math.sqrt(query_heads.shape[2])
    grad_queries = []
    grad_keys = jnp.zeros(key_heads.shape, jnp.float32)
    grad_values = jnp.zeros(value_heads.shape, jnp.float32)
    for block_index in range(frame_count // block_rows):
        row_start = block_index * block_rows
        allowed = block_mask(row_start, block_rows, key_span, margin, offset)

        def per_head(operands):
            return head_backward(
                operands[0],
                operands[1],
                operands[2],
                operands[3],
                operands[4],
                allowed,
                score_scale,
            )

        part_query, part_key, part_value = lax.map(
            per_head,
            (
                query_heads[:, row_start : row_start + block_rows],
                key_heads[:, row_start : row_start + key_span],
                value_heads[:, row_start : row_start + key_span],
                grad_heads[:, row_start : row_start + block_rows],
                logsums[:, row_start : row_start + block_rows],
            ),
        )
        grad_queries.append(part_query)
        grad_keys = grad_keys.at[:, row_start : row_start + key_span].add(part_key)
        grad_values = grad_values.at[:, row_start : row_start + key_span].add(part_value)
    return (jnp.concatenate(grad_queries, axis=1), grad_keys, grad_values)


def adam_update(master, first, second, gradient, factor, rate):
    clipped = gradient * factor
    momentum = beta_first * first + (1.0 - beta_first) * clipped
    variance = beta_second * second + (1.0 - beta_second) * clipped * clipped
    corrected = momentum / (1.0 - beta_first**STEP)
    divisor = jnp.sqrt(variance / (1.0 - beta_second**STEP)) + adam_floor
    updated = master - rate * (corrected / divisor + weight_decay * master)
    return (momentum, variance, updated, updated.astype(jnp.bfloat16))


def body(
    inputs,
    codes,
    levels,
    attention_master,
    attention_first,
    attention_second,
    feedforward_master,
    feedforward_first,
    feedforward_second,
    projection_master,
    projection_first,
    projection_second,
    codebook_master,
    codebook_first,
    codebook_second,
    scales_master,
    scales_first,
    scales_second,
):
    lowered = (
        attention_master.astype(jnp.bfloat16),
        feedforward_master.astype(jnp.bfloat16),
        projection_master.astype(jnp.bfloat16),
        codebook_master.astype(jnp.bfloat16),
        scales_master.astype(jnp.bfloat16),
    )
    attention, feedforward, projection, codebook, scales = (
        lax.all_gather(lowered[0], ("clip", "tm"), axis=1, tiled=True),
        lax.all_gather(lowered[1], ("clip", "tm"), axis=1, tiled=True),
        lax.all_gather(lowered[2], ("clip", "tm"), axis=0, tiled=True),
        lax.all_gather(lowered[3], ("clip", "tm"), axis=1, tiled=True),
        lax.all_gather(lowered[4], ("clip", "tm"), axis=1, tiled=True),
    )
    gain_rows = scales.astype(jnp.float32)
    frame_count, model_width = inputs.shape
    head_count = HEADS
    head_depth = model_width // head_count
    head_shape = (frame_count, head_count, head_depth)
    offset = lax.axis_index("tm") * frame_count
    positions = offset + jnp.arange(frame_count, dtype=jnp.int32)
    frames = inputs.astype(jnp.float32)
    normed_first, norm_pull_first = jax.vjp(normalize, frames, gain_rows[0], gain_rows[1])
    lowered_first = normed_first.astype(jnp.bfloat16)
    projected = jnp.einsum(
        "nd,kde->kne", lowered_first, attention[:3], preferred_element_type=jnp.float32
    )
    queries = rotary(projected[0].reshape(head_shape), positions, 1.0).astype(jnp.bfloat16)
    keyset = rotary(projected[1].reshape(head_shape), positions, 1.0).astype(jnp.bfloat16)
    valueset = projected[2].reshape(head_shape).astype(jnp.bfloat16)
    rim_keys, rim_values = from_behind(
        (keyset[frame_count - WINDOW :], valueset[frame_count - WINDOW :]), "tm", 1
    )
    margin = (WINDOW + 127) // 128 * 128
    filler = jnp.zeros((margin - WINDOW, head_count, head_depth), jnp.bfloat16)
    key_heads = jnp.concatenate([filler, rim_keys, keyset], axis=0).transpose(1, 0, 2)
    value_heads = jnp.concatenate([filler, rim_values, valueset], axis=0).transpose(1, 0, 2)
    query_heads = queries.transpose(1, 0, 2)
    attended, logsums = attend_forward(query_heads, key_heads, value_heads, offset)
    mixed_heads = attended.transpose(1, 0, 2).reshape(frame_count, model_width).astype(jnp.bfloat16)
    branch_first = jnp.dot(mixed_heads, attention[3], preferred_element_type=jnp.float32)
    after_first = frames + gain_rows[4] * branch_first
    normed_second, norm_pull_second = jax.vjp(normalize, after_first, gain_rows[2], gain_rows[3])
    lowered_second = normed_second.astype(jnp.bfloat16)
    pre_gelu = jnp.dot(lowered_second, feedforward[0], preferred_element_type=jnp.float32)
    gelu_value, gelu_pull = jax.vjp(partial(jax.nn.gelu, approximate=False), pre_gelu)
    hidden = gelu_value.astype(jnp.bfloat16)
    branch_second = lax.dot_general(
        hidden, feedforward[1], (((1,), (1,)), ((), ())), preferred_element_type=jnp.float32
    )
    after_second = after_first + gain_rows[5] * branch_second
    lowered_out = after_second.astype(jnp.bfloat16)
    latent = jnp.dot(lowered_out, projection, preferred_element_type=jnp.float32)
    active = levels[0]
    residue = latent
    residues = []
    factors = []
    for level_index in range(LEVELS):
        factor_level = jnp.where(level_index < active, 1.0, 0.0).astype(jnp.float32)
        code_rows = jnp.take(codebook[level_index], codes[:, level_index], axis=0).astype(
            jnp.float32
        )
        residue = residue - factor_level * code_rows
        residues.append(factor_level * residue)
        factors.append(factor_level)
    carried = jnp.zeros_like(latent)
    grad_codebook = jnp.zeros(codebook.shape, jnp.float32)
    for level_index in reversed(range(LEVELS)):
        carried = carried + residues[level_index]
        grad_codebook = grad_codebook.at[level_index, codes[:, level_index]].add(
            -factors[level_index] * carried
        )
    attention, feedforward, projection = (
        lax.all_gather(attention_master.astype(jnp.bfloat16), ("clip", "tm"), axis=1, tiled=True),
        lax.all_gather(feedforward_master.astype(jnp.bfloat16), ("clip", "tm"), axis=1, tiled=True),
        lax.all_gather(projection_master.astype(jnp.bfloat16), ("clip", "tm"), axis=0, tiled=True),
    )
    grad_latent = carried.astype(jnp.bfloat16)
    grad_projection = jnp.einsum(
        "nd,nl->dl", lowered_out, grad_latent, preferred_element_type=jnp.float32
    )
    grad_after = jnp.einsum(
        "nl,dl->nd", grad_latent, projection, preferred_element_type=jnp.float32
    )
    grad_scale_second = jnp.sum(grad_after * branch_second, axis=0)
    grad_branch_second = (grad_after * gain_rows[5]).astype(jnp.bfloat16)
    grad_down = jnp.einsum(
        "nd,nf->df", grad_branch_second, hidden, preferred_element_type=jnp.float32
    )
    grad_hidden = jnp.dot(grad_branch_second, feedforward[1], preferred_element_type=jnp.float32)
    grad_pre = gelu_pull(grad_hidden)[0].astype(jnp.bfloat16)
    grad_up = jnp.einsum("nd,nf->df", lowered_second, grad_pre, preferred_element_type=jnp.float32)
    grad_normed_second = jnp.einsum(
        "nf,df->nd", grad_pre, feedforward[0], preferred_element_type=jnp.float32
    )
    grad_through_norm, grad_gain_second, grad_shift_second = norm_pull_second(grad_normed_second)
    grad_after_first = grad_after + grad_through_norm
    grad_scale_first = jnp.sum(grad_after_first * branch_first, axis=0)
    grad_branch_first = (grad_after_first * gain_rows[4]).astype(jnp.bfloat16)
    grad_output_weight = jnp.einsum(
        "nd,ne->de", mixed_heads, grad_branch_first, preferred_element_type=jnp.float32
    )
    grad_mixed = lax.dot_general(
        grad_branch_first,
        attention[3],
        (((1,), (1,)), ((), ())),
        preferred_element_type=jnp.float32,
    )
    grad_heads = grad_mixed.astype(jnp.bfloat16).reshape(head_shape).transpose(1, 0, 2)
    grad_query_heads, grad_key_heads, grad_value_heads = attend_backward(
        query_heads, key_heads, value_heads, grad_heads, logsums, offset
    )
    rim_start = margin - WINDOW
    rim_grad_keys, rim_grad_values = (
        from_behind(grad_key_heads[:, rim_start:margin].astype(jnp.bfloat16), "tm", -1).astype(
            jnp.float32
        ),
        from_behind(grad_value_heads[:, rim_start:margin].astype(jnp.bfloat16), "tm", -1).astype(
            jnp.float32
        ),
    )
    local_keys = grad_key_heads[:, margin:].at[:, frame_count - WINDOW :].add(rim_grad_keys)
    local_values = grad_value_heads[:, margin:].at[:, frame_count - WINDOW :].add(rim_grad_values)
    grad_query_rows = rotary(grad_query_heads.transpose(1, 0, 2), positions, -1.0).reshape(
        frame_count, model_width
    )
    grad_key_rows = rotary(local_keys.transpose(1, 0, 2), positions, -1.0).reshape(
        frame_count, model_width
    )
    grad_value_rows = local_values.transpose(1, 0, 2).reshape(frame_count, model_width)
    grad_projected = jnp.stack([grad_query_rows, grad_key_rows, grad_value_rows]).astype(
        jnp.bfloat16
    )
    grad_qkv = jnp.einsum(
        "nd,kne->kde", lowered_first, grad_projected, preferred_element_type=jnp.float32
    )
    grad_normed_first = jnp.einsum(
        "kne,kde->nd", grad_projected, attention[:3], preferred_element_type=jnp.float32
    )
    grad_frames, grad_gain_first, grad_shift_first = norm_pull_first(grad_normed_first)
    input_gradient = grad_frames + grad_after_first
    local_gradients = (
        jnp.concatenate([grad_qkv, grad_output_weight[None]], axis=0),
        jnp.stack([grad_up, grad_down]),
        grad_projection,
        grad_codebook,
        jnp.stack(
            [
                grad_gain_first,
                grad_shift_first,
                grad_gain_second,
                grad_shift_second,
                grad_scale_first,
                grad_scale_second,
            ]
        ),
    )
    reduced = (
        lax.psum_scatter(local_gradients[0], ("clip", "tm"), scatter_dimension=1, tiled=True),
        lax.psum_scatter(local_gradients[1], ("clip", "tm"), scatter_dimension=1, tiled=True),
        lax.psum_scatter(local_gradients[2], ("clip", "tm"), scatter_dimension=0, tiled=True),
        lax.psum_scatter(local_gradients[3], ("clip", "tm"), scatter_dimension=1, tiled=True),
        lax.psum_scatter(local_gradients[4], ("clip", "tm"), scatter_dimension=1, tiled=True),
    )
    squares = jnp.zeros((), jnp.float32)
    for reduced_part in reduced:
        squares = squares + jnp.sum(reduced_part * reduced_part)
    total_square = lax.psum(squares, ("clip", "tm"))
    gradient_norm = jnp.sqrt(total_square)
    factor = clip_level / jnp.maximum(gradient_norm, clip_level)
    attention_new = adam_update(
        attention_master, attention_first, attention_second, reduced[0], factor, group_rates[0]
    )
    feedforward_new = adam_update(
        feedforward_master,
        feedforward_first,
        feedforward_second,
        reduced[1],
        factor,
        group_rates[1],
    )
    projection_new = adam_update(
        projection_master, projection_first, projection_second, reduced[2], factor, group_rates[2]
    )
    codebook_new = adam_update(
        codebook_master, codebook_first, codebook_second, reduced[3], factor, group_rates[3]
    )
    scales_new = adam_update(
        scales_master, scales_first, scales_second, reduced[4], factor, group_rates[4]
    )
    return (
        latent,
        input_gradient,
        gradient_norm,
        attention_new[0],
        attention_new[1],
        attention_new[2],
        attention_new[3],
        feedforward_new[0],
        feedforward_new[1],
        feedforward_new[2],
        feedforward_new[3],
        projection_new[0],
        projection_new[1],
        projection_new[2],
        projection_new[3],
        codebook_new[0],
        codebook_new[1],
        codebook_new[2],
        codebook_new[3],
        scales_new[0],
        scales_new[1],
        scales_new[2],
        scales_new[3],
    )


def solution(mesh):
    in_specs = (
        P(("clip", "tm"), None),
        P(("clip", "tm"), None),
        P("clip"),
        P(None, ("clip", "tm"), None),
        P(None, ("clip", "tm"), None),
        P(None, ("clip", "tm"), None),
        P(None, ("clip", "tm"), None),
        P(None, ("clip", "tm"), None),
        P(None, ("clip", "tm"), None),
        P(("clip", "tm"), None),
        P(("clip", "tm"), None),
        P(("clip", "tm"), None),
        P(None, ("clip", "tm"), None),
        P(None, ("clip", "tm"), None),
        P(None, ("clip", "tm"), None),
        P(None, ("clip", "tm")),
        P(None, ("clip", "tm")),
        P(None, ("clip", "tm")),
    )
    out_specs = (
        P(("clip", "tm"), None),
        P(("clip", "tm"), None),
        P(),
        P(None, ("clip", "tm"), None),
        P(None, ("clip", "tm"), None),
        P(None, ("clip", "tm"), None),
        P(None, ("clip", "tm"), None),
        P(None, ("clip", "tm"), None),
        P(None, ("clip", "tm"), None),
        P(None, ("clip", "tm"), None),
        P(None, ("clip", "tm"), None),
        P(("clip", "tm"), None),
        P(("clip", "tm"), None),
        P(("clip", "tm"), None),
        P(("clip", "tm"), None),
        P(None, ("clip", "tm"), None),
        P(None, ("clip", "tm"), None),
        P(None, ("clip", "tm"), None),
        P(None, ("clip", "tm"), None),
        P(None, ("clip", "tm")),
        P(None, ("clip", "tm")),
        P(None, ("clip", "tm")),
        P(None, ("clip", "tm")),
    )
    return jax.shard_map(body, mesh=mesh, in_specs=in_specs, out_specs=out_specs, check_vma=False)
```

profile of v0, /device:TPU:0, one launch (start us, length us, event | category | flops | bytes accessed | tf_op | source)
XLA Modules:
  0.0 1353.2 jit_solution(7570922428538923909)
XLA Ops:
  23.1 43.6 %all-gather = bf16[32,16,6]{1,2,0:T(8,128)(2,1)S(1)} all-gather(bf16[1,16,6]{1,2,0:T(8,128)(2,1)S(1)} %convert_bitcast_fusion), channel_id=1, replica_groups=mesh['clip'=8,'tm'=4] {'clip','tm'}, dimensions={0}, use_global_device_ids=true | all-gather | bytes 6336 | tf_op jit(solution)/shard_map/all_gather | solution.py:210
  69.3 37.4 %all_gather.21 = bf16[512,256]{1,0:T(8,128)(2,1)S(1)} all-gather(bf16[16,256]{1,0:T(8,128)(2,1)S(1)} %convert_element_type.158), channel_id=1, replica_groups=mesh['clip'=8,'tm'=4] {'clip','tm'}, dimensions={0}, use_global_device_ids=true | all-gather | bytes 270336 | tf_op jit(solution)/shard_map/all_gather | solution.py:208
  144.1 9.8 concatenate.70
  157.4 23.2 %while.63 = (s32[]{:T(128)}, bf16[8,512,64]{1,2,0:T(8,128)(2,1)S(1)}, f32[8,512]{1,0:T(8,128)S(1)}, bf16[8,512,64]{2,1,0:T(8,128)(2,1)}, bf16[8,768,64]{2,1,0:T(...) while((s32[]{:T(128)}, ...), condition=%wide.region_9.10_spmd.clone, body=%wide.region_6.9_spmd.clone.sunk | while | flops 105774592 | bytes 5399409 | solution.py:115
  183.6 34.7 %while.62 = (s32[]{:T(128)}, bf16[8,512,64]{1,2,0:T(8,128)(2,1)}, f32[8,512]{1,0:T(8,128)S(1)}, bf16[8,512,64]{2,1,0:T(8,128)(2,1)}, bf16[8,768,64]{2,1,0:T(8,12...) while((s32[]{:T(128)}, bf16[8,512,64]{1,2,0:T(8,128)(2,1)}, ...), condition=%wide.region_5.6_spmd.clone, body=%wide.region_2.5_spmd.clone.sunk | while | flops 105774592 | bytes 5399665 | solution.py:115
  223.1 25.1 %multiply_convert_fusion.2 = (bf16[1024,2048]{1,0:T(8,128)(2,1)S(1)}, f32[1024,2048]{1,0:T(8,128)}, f32[1024,2048]{1,0:T(8,128)}) fusion(bf16[2,512,2048]{2,1,0:T(8,128)(2,1)} %all-gather.7.cloned.1.call-done, f32[1024,512]{0,1:T(8,128)S(1)} %get-tuple-element.819, f32[512]{0:T(512)S(1)} %bitcast.370, f32[512]{0:T(512)S(1)} %bitcast.350, ...), kind=kOutput, calls=%fused_computation.142 | convolution fusion | flops 2286419968 | bytes 25178112 | tf_op jit(solution)/shard_map/dot_general | solution.py:242
  259.7 6.0 slice_bitcast_fusion.10
  312.6 6.0 multiply_add_fusion
  323.2 11.2 add_convert_fusion
  356.9 74.8 %while.64 = (s32[]{:T(128)}, f32[8,512,64]{1,2,0:T(8,128)}, f32[8,768,64]{1,2,0:T(8,128)}, f32[8,768,64]{1,2,0:T(8,128)}, bf16[8,512,64]{2,1,0:T(8,128)(2,1)}, /...) while((s32[]{:T(128)}, f32[8,512,64]{1,2,0:T(8,128)}, ...), condition=%wide.region_16.18_spmd.clone, body=%wide.region_14.17_spmd.clone.sunk | while | flops 257244672 | bytes 13453185 | solution.py:152
  435.4 72.8 %while.65 = (s32[]{:T(128)}, f32[8,512,64]{1,2,0:T(8,128)}, f32[8,768,64]{1,2,0:T(8,128)}, f32[8,768,64]{1,2,0:T(8,128)}, bf16[8,512,64]{2,1,0:T(8,128)(2,1)}, /...) while((s32[]{:T(128)}, f32[8,512,64]{1,2,0:T(8,128)}, ...), condition=%wide.region_19.21_spmd.clone, body=%wide.region_17.20_spmd.clone.sunk | while | flops 257244672 | bytes 13453185 | solution.py:152
  580.6 13.8 %scatter_custom_fusion = f32[16384,256]{1,0:T(8,128)} fusion(s32[1024]{0:T(1024)S(1)} %get-tuple-element.913, f32[]{:T(128)} %constant.392.clone.1, f32[1024,256]{1,0:T(8,128)S(1)} %copy-done.24, f32[]{:T(128)S(6)} %neg.41, f32[]{:T(128)} %bitcast.42, f32[]{:T(128)} %bitcast.23, bf16[1024,256]{1,0:T(8,128)(2,1)S(1)} %copy-done.20, ...), kind=kCustom, calls=%fused_computation.139 | custom fusion | flops 2883584 | bytes 18876432
  594.4 18.9 %scatter_custom_fusion.1 = f32[16384,256]{1,0:T(8,128)} fusion(f32[16384,256]{1,0:T(8,128)} %scatter_custom_fusion, s32[1024]{0:T(1024)S(1)} %get-tuple-element.911, f32[1024,256]{1,0:T(8,128)} %get-tuple-element.814, f32[]{:T(128)S(6)} %neg.42, f32[]{:T(128)} %bitcast.42, f32[]{:T(128)} %bitcast.23, bf16[1024,256]{1,0:T(8,128)(2,1)S(1)} %copy-done.20, ...), kind=kCustom, calls=%fused_computation.228 | custom fusion | flops 3407872 | bytes 18877444
  613.3 17.6 %scatter_custom_fusion.2 = f32[16384,256]{1,0:T(8,128)} fusion(f32[16384,256]{1,0:T(8,128)} %scatter_custom_fusion.1, s32[1024]{0:T(1024)S(1)} %get-tuple-element.912, f32[1024,256]{1,0:T(8,128)S(1)} %copy-done.23, f32[]{:T(128)S(6)} %neg.43), kind=kCustom, calls=%fused_computation.226 | custom fusion | flops 524288 | bytes 17825796
  630.9 18.2 %scatter_custom_fusion.3 = f32[16384,256]{1,0:T(8,128)} fusion(f32[16384,256]{1,0:T(8,128)} %scatter_custom_fusion.2, s32[1024]{0:T(1024)S(1)} %get-tuple-element.910, f32[1024,256]{1,0:T(8,128)S(1)} %copy-done.23, f32[1024,256]{1,0:T(8,128)} %get-tuple-element.815, f32[]{:T(128)S(6)} %neg.44, f32[]{:T(128)} %bitcast.36, ...), kind=kCustom, calls=%fused_computation.224 | custom fusion | flops 2097152 | bytes 19400196
  649.2 17.9 %scatter_custom_fusion.4 = f32[16384,256]{1,0:T(8,128)} fusion(f32[16384,256]{1,0:T(8,128)} %scatter_custom_fusion.3, s32[1024]{0:T(1024)S(1)} %get-tuple-element.909, f32[1024,256]{1,0:T(8,128)S(1)} %copy-done.8, f32[]{:T(128)S(6)} %neg.45), kind=kCustom, calls=%fused_computation.222 | custom fusion | flops 524288 | bytes 17825796
  667.1 19.0 %scatter_custom_fusion.5 = f32[16384,256]{1,0:T(8,128)} fusion(f32[16384,256]{1,0:T(8,128)} %scatter_custom_fusion.4, s32[1024]{0:T(1024)S(1)} %get-tuple-element.908, f32[1024,256]{1,0:T(8,128)S(1)} %copy-done.8, f32[]{:T(128)S(6)} %neg.46, f32[]{:T(128)} %bitcast.30, bf16[1024,256]{1,0:T(8,128)(2,1)S(1)} %copy-done.18, ...), kind=kCustom, calls=%fused_computation.220 | custom fusion | flops 4194304 | bytes 20451844
  686.1 19.2 %scatter_custom_fusion.6 = f32[16384,256]{1,0:T(8,128)} fusion(f32[16384,256]{1,0:T(8,128)} %scatter_custom_fusion.5, s32[1024]{0:T(1024)S(1)} %get-tuple-element.907, f32[]{:T(128)S(6)} %neg.47, f32[1024,256]{1,0:T(8,128)S(1)} %copy-done.8, f32[]{:T(128)} %bitcast.30, f32[]{:T(128)} %bitcast.27, bf16[1024,256]{1,0:T(8,128)(2,1)} %gather_fusion.2, ...), kind=kCustom, calls=%fused_computation.218 | custom fusion | flops 4718592 | bytes 20451844
  705.4 17.6 %scatter_custom_fusion.7 = f32[16384,256]{1,0:T(8,128)} fusion(f32[16384,256]{1,0:T(8,128)} %scatter_custom_fusion.6, s32[1024]{0:T(1024)S(1)} %get-tuple-element.906, f32[1024,256]{1,0:T(8,128)S(1)} %copy-done.10, f32[]{:T(128)S(6)} %neg.48), kind=kCustom, calls=%fused_computation.216 | custom fusion | flops 524288 | bytes 17825796
  729.5 86.3 %reduce-scatter.9.cloned.1.call-done = f32[16,256]{1,0:T(8,128)} async-done(((f32[512,256]{1,0:T(8,128)}), f32[16,256]{1,0:T(8,128)}) %reduce-scatter.9.cloned.1.call-update) | async-done | bytes 16400 | tf_op jit(solution)/shard_map/reduce_scatter | solution.py:358
  817.1 141.8 %all-reduce.13.cloned.1.call-done = f32[4,512,512]{2,0,1:T(4,128)} async-done(((f32[4,512,512]{2,0,1:T(4,128)}), f32[4,512,512]{2,0,1:T(4,128)}) %all-reduce.13.cloned.1.call-update) | async-done | bytes 4194320
  960.5 148.6 %reduce-scatter.7.cloned.1.call-done = f32[2,16,2048]{2,1,0:T(8,128)} async-done(((f32[2,512,2048]{2,1,0:T(8,128)}), f32[2,16,2048]{2,1,0:T(8,128)}) %reduce-scatter.7.cloned.1.call-update) | async-done | bytes 262160 | tf_op jit(solution)/shard_map/reduce_scatter | solution.py:357
  1112.6 177.6 %reduce-scatter.11.cloned.1.call-done = f32[8,64,256]{2,1,0:T(8,128)} async-done(((f32[8,2048,256]{2,1,0:T(8,128)}), f32[8,64,256]{2,1,0:T(8,128)}) %reduce-scatter.11.cloned.1.call-update) | async-done | bytes 524304 | tf_op jit(solution)/shard_map/reduce_scatter | solution.py:359
  1296.5 41.1 %psum.7 = f32[]{:T(128)} all-reduce(f32[]{:T(128)S(6)} %add.445), channel_id=1, replica_groups=mesh['clip'=8,'tm'=4] {'clip','tm'}, use_global_device_ids=true, to_apply=%region_46.48 | all-reduce | flops 1 | bytes 8 | tf_op jit(solution)/shard_map/psum | solution.py:365
  (568 shorter events, 454.0 us)
Async XLA Ops:
  7.2 60.4 %copy-start.37 = (bf16[1024,512]{1,0:T(8,128)(2,1)S(1)}, bf16[1024,512]{1,0:T(8,128)(2,1)}, u32[]{:S(2)}) copy-start(bf16[1024,512]{1,0:T(8,128)(2,1)} %param.40) | copy-start | bytes 3145732
  7.2 100.7 %all-gather.5.cloned.1.call-start = ((), (), s32[]{:S(2)}) async-start(), calls=%async_computation.4 | async-start | bytes 2162688 | tf_op jit(solution)/shard_map/all_gather | solution.py:206
  9.0 213.8 %all-gather.7.cloned.1.call-start = ((), (), s32[]{:S(2)}) async-start(), calls=%async_computation.5 | async-start | bytes 4325376 | tf_op jit(solution)/shard_map/all_gather | solution.py:207
  10.7 249.0 %all-gather.9.cloned.1.call-start = ((), (), s32[]{:S(2)}) async-start(), calls=%async_computation.6 | async-start | bytes 8650752 | tf_op jit(solution)/shard_map/all_gather | solution.py:209
  12.5 715.6 %reduce-scatter.13.cloned.1.call-start = ((), (), s32[]{:S(2)}) async-start(), calls=%async_computation.10 | async-start | bytes 270336
  20.3 48.1 %copy-start.21 = (bf16[8,512,64]{1,2,0:T(8,128)(2,1)}, bf16[8,512,64]{1,2,0:T(8,128)(2,1)S(1)}, u32[]{:S(2)}) copy-start(bf16[8,512,64]{1,2,0:T(8,128)(2,1)S(1)} %fusion.202) | copy-start | bytes 1572868
  68.1 151.9 %copy-start = (bf16[1024,512]{0,1:T(8,128)(2,1)}, bf16[1024,512]{0,1:T(8,128)(2,1)S(1)}, u32[]{:S(2)}) copy-start(bf16[1024,512]{0,1:T(8,128)(2,1)S(1)} %copy.207) | copy-start | bytes 3145732
  116.1 19.5 %collective-permute-start = (bf16[250,8,64]{0,2,1:T(8,128)(2,1)}, bf16[250,8,64]{0,2,1:T(8,128)(2,1)}, u32[]{:S(2)}, u32[]{:S(2)}) collective-permute-start(bf16[250,8,64]{0,2,1:T(8,128)(2,1)} %fusion.153), channel_id=1, source_target_pairs={{0,1},{1,2},{2,3},{4,5},{5,6},{6,7},{8,9},{9,10},{10,11},{12,13},{... | collective-permute-start | bytes 768008 | tf_op jit(solution)/shard_map/ppermute | solution.py:27
  123.5 20.6 %collective-permute-start.1 = (bf16[250,8,64]{2,0,1:T(8,128)(2,1)}, bf16[250,8,64]{2,0,1:T(8,128)(2,1)}, u32[]{:S(2)}, u32[]{:S(2)}) collective-permute-start(bf16[250,8,64]{2,0,1:T(8,128)(2,1)} %copy.213), channel_id=1, source_target_pairs={{0,1},{1,2},{2,3},{4,5},{5,6},{6,7},{8,9},{9,10},{10,11},{12,13},{... | collective-permute-start | bytes 768008 | tf_op jit(solution)/shard_map/ppermute | solution.py:27
  511.9 9.5 collective-permute-start.3
  516.9 8.9 collective-permute-start.2
  551.3 264.5 %reduce-scatter.9.cloned.1.call-start = ((), (), s32[]{:S(2)}) async-start(), calls=%async_computation.8 | async-start | bytes 540672 | tf_op jit(solution)/shard_map/reduce_scatter | solution.py:358
  554.1 404.8 %all-reduce.13.cloned.1.call-start = ((), (), s32[]{:S(2)}) async-start(), calls=%async_computation.11 | async-start | bytes 8388608
  567.0 542.1 %reduce-scatter.7.cloned.1.call-start = ((), (), s32[]{:S(2)}) async-start(), calls=%async_computation.7 | async-start | bytes 8650752 | tf_op jit(solution)/shard_map/reduce_scatter | solution.py:357
  579.0 711.2 %reduce-scatter.11.cloned.1.call-start = ((), (), s32[]{:S(2)}) async-start(), calls=%async_computation.9 | async-start | bytes 17301504 | tf_op jit(solution)/shard_map/reduce_scatter | solution.py:359
  728.9 564.5 %copy-start.60 = (f32[6,16]{1,0:T(8,128)}, f32[6,16]{1,0:T(8,128)S(1)}, u32[]{:S(2)}) copy-start(f32[6,16]{1,0:T(8,128)S(1)} %copy.251) | copy-start | bytes 1156
  1293.4 48.1 %copy-start.35 = (f32[2,16,2048]{2,1,0:T(8,128)S(1)}, f32[2,16,2048]{2,1,0:T(8,128)}, u32[]{:S(2)}) copy-start(f32[2,16,2048]{2,1,0:T(8,128)} %param.46) | copy-start | bytes 786436
  1293.4 48.1 %copy-start.36 = (f32[2,16,2048]{2,1,0:T(8,128)S(1)}, f32[2,16,2048]{2,1,0:T(8,128)}, u32[]{:S(2)}) copy-start(f32[2,16,2048]{2,1,0:T(8,128)} %reduce-scatter.7.cloned.1.call-done) | copy-start | bytes 786436
  1293.4 48.1 %copy-start.45 = (f32[2,16,2048]{2,1,0:T(8,128)S(1)}, f32[2,16,2048]{2,1,0:T(8,128)}, u32[]{:S(2)}) copy-start(f32[2,16,2048]{2,1,0:T(8,128)} %param.48) | copy-start | bytes 786436
  1293.4 48.1 %copy-start.46 = (f32[2,16,2048]{2,1,0:T(8,128)S(1)}, f32[2,16,2048]{2,1,0:T(8,128)}, u32[]{:S(2)}) copy-start(f32[2,16,2048]{2,1,0:T(8,128)} %param.47) | copy-start | bytes 786436
  1296.4 46.8 %copy-start.31 = (f32[8,64,256]{2,1,0:T(8,128)S(1)}, f32[8,64,256]{2,1,0:T(8,128)}, u32[]{:S(2)}) copy-start(f32[8,64,256]{2,1,0:T(8,128)} %param.52) | copy-start | bytes 1572868
  1296.4 46.8 %copy-start.32 = (f32[8,64,256]{2,1,0:T(8,128)S(1)}, f32[8,64,256]{2,1,0:T(8,128)}, u32[]{:S(2)}) copy-start(f32[8,64,256]{2,1,0:T(8,128)} %reduce-scatter.11.cloned.1.call-done) | copy-start | bytes 1572868
  1296.4 46.8 %copy-start.41 = (f32[8,64,256]{2,1,0:T(8,128)S(1)}, f32[8,64,256]{2,1,0:T(8,128)}, u32[]{:S(2)}) copy-start(f32[8,64,256]{2,1,0:T(8,128)} %param.54) | copy-start | bytes 1572868
  1296.4 46.8 %copy-start.42 = (f32[8,64,256]{2,1,0:T(8,128)S(1)}, f32[8,64,256]{2,1,0:T(8,128)}, u32[]{:S(2)}) copy-start(f32[8,64,256]{2,1,0:T(8,128)} %param.53) | copy-start | bytes 1572868
  (89 other events, 679.7 us)
Sparse Core Ops, SparseCore 0:
  11.5 59.1 all-gather.4
  74.2 60.7 all-gather.6
  138.6 80.0 all-gather.8
  551.4 132.5 reduce-scatter.12
  686.2 129.5 reduce-scatter.8
  821.2 137.6 all-reduce.12
  961.2 147.8 reduce-scatter.6
  1111.4 178.8 reduce-scatter.10
where the time goes:
time: 1360 us; the launch traced here: 1350 us
  waiting for transfers between devices  554 us (41%)
  matrix products  266 us (20%)
  other arithmetic  216 us (16%)
  local copies, waits for them, and re-layouts  163 us (12%)
  blocking collectives  122 us (9%)
  between operations  21.7 us (2%)
    reduce_scatter x1, waiting for transfers between devices, body(): lax.psum_scatter(local_gradients[3], ('clip', 'tm'), scatter_dimension=1,...  178 us
    reduce_scatter x1, waiting for transfers between devices, body(): lax.psum_scatter(local_gradients[1], ('clip', 'tm'), scatter_dimension=1,...  149 us
    unnamed x16, other arithmetic  143 us
    unnamed x10, waiting for transfers between devices  142 us
    reduce_scatter x1, waiting for transfers between devices, body(): lax.psum_scatter(local_gradients[2], ('clip', 'tm'), scatter_dimension=0,...  86.3 us
    gather x8, local copies, waits for them, and re-layouts, body(): jnp.take(codebook[level_index], codes[:, level_index], axis=0)  46.7 us
    all_gather x1, blocking collectives, body(): lax.all_gather(lowered[4], ('clip', 'tm'), axis=1, tiled=True)  43.6 us
    psum x1, blocking collectives, body(): total_square = lax.psum(squares, ('clip', 'tm'))  41.1 us
  transfers between devices with their start and end apart: 12, of which 4 were waited for; matrix products, arithmetic and copies ran while one was open for 26% of the time, Pallas kernels for 0%

commit v1 on v0

v1 whole, which is shorter than its diff:
```python
import math

import jax
import jax.numpy as jnp
import numpy as np
from jax import lax
from jax.experimental import pallas as pl
from jax.experimental.pallas import tpu as pltpu
from jax.sharding import PartitionSpec as P

HEADS = 8
LEVELS = 8
WINDOW = 250
STEP = 10
AXES = ("clip", "tm")

clip_level = 1.0
beta_first = 0.9
beta_second = 0.95
adam_floor = 1e-08
weight_decay = 0.1
group_rates = (0.05, 0.03, 0.05, 0.5, 0.5)
masked_score = -1e30

f32 = jnp.float32
bf16 = jnp.bfloat16
MARGIN = (WINDOW + 127) // 128 * 128
QROWS = 128
SPAN = QROWS + MARGIN
ROWS = 256
MIB = 1 << 20


def dot(left, right, contract=((1,), (0,))):
    return lax.dot_general(left, right, (contract, ((), ())), preferred_element_type=f32)


def dot_nt(left, right):
    return dot(left, right, ((1,), (1,)))


def flip(block):
    return block.astype(f32).T.astype(bf16)


def params(mib):
    return pltpu.CompilerParams(vmem_limit_bytes=mib * MIB)


def whole(shape):
    return pl.BlockSpec(tuple(shape), lambda *_: (0,) * len(shape))


def smem():
    return pl.BlockSpec(memory_space=pltpu.SMEM)


def cost(share, length=1):
    return pl.CostEstimate(flops=share * 500000000, bytes_accessed=length * 3 * MIB, transcendentals=0)


def after(value, *earlier):
    return lax.optimization_barrier((value, earlier))[0]


def digit_plan(count, kind):
    bits = count.bit_length() - 1
    if kind == 2:
        plan, shift = [(0, 2)], 1
    else:
        middle = [(shift, 2) for shift in range(1, min(3, bits))]
        plan, shift = [(0, 2)] + (middle[::-1] if kind % 2 else middle), 3
    while shift < bits:
        width = 1 if kind > 2 else min(2, bits - shift)
        plan.append((shift, 1 << width))
        shift += width
    return plan


def swap(block, count, mask):
    return lax.ppermute(block, AXES, [(i, i ^ mask) for i in range(count)])


def gather_swaps(block, count, kind, stage):
    shift, radix = digit_plan(count, kind)[stage]
    return [swap(block, count, k << shift) for k in range(1, radix)]


def join(block, others, axis=0):
    return jnp.concatenate([block] + list(others), axis=axis)


def place_of(device, count, kind):
    place, weight = 0, 1
    for shift, radix in reversed(digit_plan(count, kind)):
        place = place + ((device >> shift) & (radix - 1)) * weight
        weight *= radix
    return place


def device_of_places(count, kind):
    table = np.zeros(count, np.int32)
    for device in range(count):
        table[place_of(device, count, kind)] = device
    return table


def swap_parts(parts, count, kind, stage):
    shift, _ = digit_plan(count, kind)[stage]
    return [swap(part, count, (k + 1) << shift) for k, part in enumerate(parts)]


def reduce_add(keep, parts):
    total = keep.astype(f32)
    for part in parts:
        total = total + part.astype(f32)
    return total


def split_kernel(radix, *refs):
    outs, operands = refs[-radix:], refs[:-radix]
    total = operands[0][...].astype(f32)
    for operand in operands[1:]:
        total = total + operand[...].astype(f32)
    size = total.shape[1] // radix
    for k, out in enumerate(outs):
        out[...] = total[:, k * size : (k + 1) * size, :].astype(out.dtype)


def reduce_split(keep, parts, count, kind, stage):
    _, radix = digit_plan(count, kind)[stage]
    lead, rows, columns = keep.shape
    size = rows // radix
    if lead > 1:
        steps, block, index = lead, (1, rows, columns), lambda i: (i, 0, 0)
    else:
        steps = 2 if columns % 256 == 0 else 1
        block, index = (1, rows, columns // steps), lambda i: (0, 0, i)
    shares = (block[0], size, block[2])
    kinds = [f32] + [bf16] * (radix - 1)
    outs = pl.pallas_call(
        lambda *refs: split_kernel(radix, *refs),
        grid=(steps,),
        in_specs=[pl.BlockSpec(block, index)] * (1 + len(parts)),
        out_specs=[pl.BlockSpec(shares, index)] * radix,
        out_shape=[jax.ShapeDtypeStruct((lead, size, columns), kind) for kind in kinds],
        compiler_params=params(32),
        cost_estimate=cost(0, 1),
        name="split_sums",
    )(keep, *parts)
    return outs[0], swap_parts(outs[1:], count, kind, stage)


def merge_kernel(axis, radix, groups, *refs):
    outs = refs[-radix:]
    base = left = 0
    for size in groups:
        total = refs[base][...].astype(f32)
        for operand in refs[base + 1 : base + size]:
            total = total + operand[...].astype(f32)
        base += size
        rows = total.shape[1] // radix
        for k, out in enumerate(outs):
            share = total[:, k * rows : (k + 1) * rows, :].astype(out.dtype)
            if axis == 0:
                out[left : left + total.shape[0]] = share
            else:
                out[:, :, left : left + total.shape[2]] = share
        left += total.shape[axis]


def merge_split(groups, axis, count, kind, stage, share=0):
    _, radix = digit_plan(count, kind)[stage]
    operands = [array for keep, parts in groups for array in (keep, *parts)]
    shape = list(groups[0][0].shape)
    shape[axis] = sum(keep.shape[axis] for keep, _ in groups)
    shape[1] //= radix
    sizes = [1 + len(parts) for _, parts in groups]
    kinds = [f32] + [bf16] * (radix - 1)
    outs = pl.pallas_call(
        lambda *refs: merge_kernel(axis, radix, sizes, *refs),
        grid=(1,),
        in_specs=[whole(operand.shape) for operand in operands],
        out_specs=[whole(shape)] * radix,
        out_shape=[jax.ShapeDtypeStruct(shape, kind) for kind in kinds],
        compiler_params=params(32),
        cost_estimate=cost(share, 1),
        name="split_sums",
    )(*operands)
    return outs[0], swap_parts(outs[1:], count, kind, stage)


def one_hot_rows(rowmap, size):
    place = lax.broadcasted_iota(jnp.int32, (size, size), 0)
    return jnp.where(place == rowmap, 1.0, 0.0).astype(bf16)


def unpack_rows(starts_ref, rowmap_ref, pieces, out_ref):
    half = pieces[0].shape[0]
    count = starts_ref.shape[0]
    rows = 2 * half // count
    if rows % 16 == 0:
        for place in range(count):
            piece = pieces[place * rows // half]
            inner = place * rows % half
            start = pl.multiple_of(starts_ref[place], rows)
            out_ref[pl.ds(start, rows), :] = piece[inner : inner + rows, :]
    else:
        spread = one_hot_rows(rowmap_ref[0:1, :], 2 * half)
        columns = out_ref.shape[1]
        for left in range(0, columns, 128):
            joined = jnp.concatenate([p[:, left : left + 128] for p in pieces], axis=0)
            out_ref[:, left : left + 128] = dot(spread, joined).astype(bf16)


def pack_rows(starts_ref, rowmap_ref, work_ref, outs):
    size, columns = work_ref.shape
    half = size // 2
    count = starts_ref.shape[0]
    rows = size // count
    if rows % 16 == 0:
        for place in range(count):
            start = pl.multiple_of(starts_ref[place], rows)
            out, inner = outs[place * rows // half], place * rows % half
            out[0, inner : inner + rows, :] = work_ref[pl.ds(start, rows), :]
    else:
        spread = one_hot_rows(rowmap_ref[0:1, :], size)
        for left in range(0, columns, 128):
            lanes = slice(left, left + 128)
            joined = dot(spread, work_ref[:, lanes], ((0,), (0,))).astype(bf16)
            for index, out in enumerate(outs):
                out[0, :, lanes] = joined[index * half : (index + 1) * half]


def centre_rows(values):
    centred = values - jnp.mean(values, axis=-1, keepdims=True)
    spread = jnp.mean(centred * centred, axis=-1, keepdims=True)
    rstd = lax.rsqrt(spread + 1e-05)
    return centred * rstd, rstd


def norm_back(normal, rstd, gain, grad):
    inner = grad * gain
    first = jnp.mean(inner, axis=-1, keepdims=True)
    second = jnp.mean(inner * normal, axis=-1, keepdims=True)
    return rstd * (inner - first - normal * second)


def column_sum(values):
    return jnp.sum(values, axis=0, keepdims=True)


def turn(values, cosine, sine):
    lanes = values.shape[1]
    ahead = pltpu.roll(values, lanes - 32, 1)
    behind = pltpu.roll(values, 32, 1)
    lane = lax.broadcasted_iota(jnp.int32, values.shape, 1)
    partner = jnp.where(lane % 64 < 32, ahead, behind)
    repeats = lanes // cosine.shape[1]
    if repeats > 1:
        cosine = jnp.concatenate([cosine] * repeats, axis=1)
        sine = jnp.concatenate([sine] * repeats, axis=1)
    return values * cosine + partner * sine


def head_columns(flipped):
    zero = jnp.zeros((64, flipped.shape[1]), flipped.dtype)
    return jnp.concatenate(
        [
            jnp.concatenate([flipped[:64], zero], axis=1),
            jnp.concatenate([zero, flipped[64:]], axis=1),
        ],
        axis=0,
    )


def head_rows(block):
    lane = lax.broadcasted_iota(jnp.int32, block.shape, 1)
    zero = jnp.zeros_like(block)
    return jnp.concatenate(
        [jnp.where(lane < 64, block, zero), jnp.where(lane < 64, zero, block)], axis=0
    )


def qkv_kernel(
    starts, rowmap, halo, inputs, piece_a, piece_b, cosine, sine, normed, q, k, v, scales, weights
):
    step = pl.program_id(0)
    width = inputs.shape[1]

    @pl.when(step == 0)
    def _():
        unpack_rows(starts, rowmap, (piece_a, piece_b), weights)
        scales[...] = weights[:, 3 * width :].astype(f32).T[:8]

    frames = jnp.where(step == 0, halo[...].astype(f32), inputs[...].astype(f32))
    normal, _ = centre_rows(frames)
    low = (normal * scales[0:1, :] + scales[1:2, :]).astype(bf16)
    normed[...] = low
    turned = turn(dot(low, weights[:, :width]), cosine[...], sine[...])
    q[...] = (turned.astype(bf16).astype(f32) * 0.125).astype(bf16)
    k[...] = turn(dot(low, weights[:, width : 2 * width]), cosine[...], sine[...]).astype(bf16)
    v[...] = dot(low, weights[:, 2 * width : 3 * width]).astype(bf16)


def qkv_call(starts, rowmap, halo, inputs, pieces, cosine, sine):
    count, width = inputs.shape
    columns = pieces[0].shape[1]
    steps = count // ROWS + 1
    late = lambda i: (jnp.maximum(i - 1, 0), 0)
    here = lambda i: (i, 0)
    return pl.pallas_call(
        qkv_kernel,
        grid=(steps,),
        in_specs=[
            smem(),
            whole(rowmap.shape),
            whole(halo.shape),
            pl.BlockSpec((ROWS, width), late),
            whole(pieces[0].shape),
            whole(pieces[1].shape),
            pl.BlockSpec((ROWS, 128), here),
            pl.BlockSpec((ROWS, 128), here),
        ],
        out_specs=[
            pl.BlockSpec((ROWS, width), late),
            pl.BlockSpec((ROWS, width), late),
            pl.BlockSpec((ROWS, width), here),
            pl.BlockSpec((ROWS, width), here),
            whole((8, width)),
            whole((width, columns)),
        ],
        out_shape=[
            jax.ShapeDtypeStruct((count, width), bf16),
            jax.ShapeDtypeStruct((count, width), bf16),
            jax.ShapeDtypeStruct((count + MARGIN, width), bf16),
            jax.ShapeDtypeStruct((count + MARGIN, width), bf16),
            jax.ShapeDtypeStruct((8, width), f32),
            jax.ShapeDtypeStruct((width, columns), bf16),
        ],
        compiler_params=params(48),
        cost_estimate=cost(4, 8),
        name="project_rows",
    )(starts, rowmap, halo, inputs, *pieces, cosine, sine)


def attend_kernel(q, k, v, bias, mixed, logsum, v_flipped):
    step = pl.program_id(0)
    pairs = q.shape[1] // 128

    @pl.when(step == 0)
    def _():
        for pair in range(pairs):
            lanes = slice(pair * 128, (pair + 1) * 128)
            v_flipped[lanes, :] = flip(v[:, lanes])

    start = pl.multiple_of(step * QROWS, QROWS)
    allowed = jnp.concatenate([bias[0], bias[0]], axis=1)
    rows = []
    for pair in range(pairs):
        lanes = slice(pair * 128, (pair + 1) * 128)
        columns = head_columns(flip(q[:, lanes]))
        scores = dot(k[pl.ds(start, SPAN), lanes], columns) + allowed
        highest = jnp.max(scores, axis=0, keepdims=True)
        raised = jnp.exp(scores - highest)
        total = column_sum(raised)
        joined = dot(v_flipped[lanes, pl.ds(start, SPAN)], raised.astype(bf16))
        joined = joined * (1.0 / total)
        output = jnp.concatenate([joined[:64, :QROWS], joined[64:, QROWS:]], axis=0)
        mixed[:, lanes] = output.T.astype(bf16)
        record = highest + jnp.log(total)
        rows += [record[:, :QROWS], record[:, QROWS:]]
    logsum[...] = jnp.concatenate(rows, axis=0)


def attend_call(q, k, v, bias):
    count, width = q.shape
    return pl.pallas_call(
        attend_kernel,
        grid=(count // QROWS,),
        in_specs=[
            pl.BlockSpec((QROWS, width), lambda i: (i, 0)),
            whole(k.shape),
            whole(v.shape),
            pl.BlockSpec((1, SPAN, QROWS), lambda i: (i, 0, 0)),
        ],
        out_specs=[
            pl.BlockSpec((QROWS, width), lambda i: (i, 0)),
            pl.BlockSpec((HEADS, QROWS), lambda i: (0, i)),
        ],
        out_shape=[
            jax.ShapeDtypeStruct((count, width), bf16),
            jax.ShapeDtypeStruct((HEADS, count), f32),
        ],
        scratch_shapes=[pltpu.VMEM((width, k.shape[0]), bf16)],
        compiler_params=params(40),
        cost_estimate=cost(4, 14),
        name="attend_rows",
    )(q, k, v, bias)


def forward_kernel(
    starts_a, rowmap_a, starts_b, rowmap_b, inputs, mixed, scales, own_a, other_a, own_b, other_b,
    branch_first, after_first, normed, hidden, slope, branch_second, low_out, latent, weights,
):
    step = pl.program_id(0)
    width = inputs.shape[1]
    units = hidden.shape[1]

    @pl.when(step == 0)
    def _():
        unpack_rows(starts_a, rowmap_a, (own_a, other_a), weights.at[:, :units])
        unpack_rows(starts_b, rowmap_b, (own_b, other_b), weights.at[:, units:])

    up, down = 0, units
    proj = 2 * units
    last = proj + latent.shape[1]
    first = dot(mixed[...], weights[:, last : last + width])
    branch_first[...] = first
    after = inputs[...].astype(f32) + scales[4:5, :] * first
    after_first[...] = after
    normal, _ = centre_rows(after)
    low = (normal * scales[2:3, :] + scales[3:4, :]).astype(bf16)
    normed[...] = low
    second = jnp.zeros(after.shape, f32)
    chunk = 512
    for left in range(0, units, chunk):
        pre = dot(low, weights[:, up + left : up + left + chunk])
        share = 0.5 + 0.5 * lax.erf(pre * (1.0 / math.sqrt(2.0)))
        bell = jnp.exp(-0.5 * pre * pre) * (1.0 / math.sqrt(2.0 * math.pi))
        part = (pre * share).astype(bf16)
        hidden[:, left : left + chunk] = part
        slope[:, left : left + chunk] = (share + pre * bell).astype(bf16)
        second = second + dot_nt(part, weights[:, down + left : down + left + chunk])
    branch_second[...] = second
    rounded = (after + scales[5:6, :] * second).astype(bf16)
    low_out[...] = rounded
    latent[...] = dot(rounded, weights[:, proj:last])


def forward_call(orders, inputs, mixed, scales, pieces, units, depth):
    count, width = inputs.shape
    columns = pieces[0].shape[1] + pieces[2].shape[1]
    row = lambda size: pl.BlockSpec((ROWS, size), lambda i: (i, 0))
    kept = ((width, f32), (width, f32), (width, bf16), (units, bf16), (units, bf16),
            (width, f32), (width, bf16), (depth, f32))
    (starts_a, rowmap_a), (starts_b, rowmap_b) = orders
    return pl.pallas_call(
        forward_kernel,
        grid=(count // ROWS,),
        in_specs=[smem(), whole(rowmap_a.shape)] * 2
        + [row(width), row(width), whole(scales.shape)]
        + [whole(piece.shape) for piece in pieces],
        out_specs=[row(size) for size, _ in kept] + [whole((width, columns))],
        out_shape=[jax.ShapeDtypeStruct((count, size), kind) for size, kind in kept]
        + [jax.ShapeDtypeStruct((width, columns), bf16)],
        compiler_params=params(56),
        cost_estimate=cost(4, 17),
        name="feed_rows",
    )(starts_a, rowmap_a, starts_b, rowmap_b, inputs, mixed, scales, *pieces)


def fetch_kernel(active, codes, latent, book, carried, residue, steps):
    level = pl.program_id(0)
    count, depth = latent.shape
    tiles = book.shape[1] // 256

    @pl.when(level == 0)
    def _():
        residue[...] = latent[...]

    factor = jnp.where(level < active[0], 1.0, 0.0).astype(f32)
    lane = lax.broadcasted_iota(jnp.int32, (ROWS, LEVELS), 1)
    place = lax.broadcasted_iota(jnp.int32, (ROWS, 256), 1).astype(f32)
    for top in range(0, count, ROWS):
        rows = slice(top, top + ROWS)
        code = jnp.where(lane == level, codes[rows, :].astype(f32), 0.0)
        code = jnp.sum(code, axis=1, keepdims=True)
        high = jnp.floor(code * (1.0 / 256.0))
        hit = jnp.where(place == code - 256.0 * high, 1.0, 0.0).astype(bf16)
        picks = [hit * jnp.where(high == j, 1.0, 0.0).astype(bf16) for j in range(tiles)]
        found = dot(jnp.concatenate(picks, axis=1), book[0])
        left = residue[rows, :] - factor * found
        residue[rows, :] = left
        steps[level, rows, :] = factor * left

    @pl.when(level == LEVELS - 1)
    def _():
        for top in range(0, count, ROWS):
            rows = slice(top, top + ROWS)
            total = jnp.zeros((ROWS, depth), f32)
            for index in reversed(range(LEVELS)):
                total = total + steps[index, rows, :]
                live = jnp.where(index < active[0], 1.0, 0.0).astype(f32)
                carried[index, rows, :] = (live * total).astype(bf16)


def fetch_call(active, codes, latent, book):
    count, depth = latent.shape
    entries = book.shape[1]
    return pl.pallas_call(
        fetch_kernel,
        grid=(LEVELS,),
        in_specs=[
            smem(),
            whole(codes.shape),
            whole(latent.shape),
            pl.BlockSpec((1, entries, depth), lambda i: (i, 0, 0)),
        ],
        out_specs=whole((LEVELS, count, depth)),
        out_shape=jax.ShapeDtypeStruct((LEVELS, count, depth), bf16),
        scratch_shapes=[
            pltpu.VMEM((count, depth), f32),
            pltpu.VMEM((LEVELS, count, depth), f32),
        ],
        compiler_params=params(48),
        cost_estimate=cost(4, 13),
        name="fetch_codes",
    )(active, codes, latent, book)


def spread_kernel(first, codes, carried, keep, send):
    level = pl.program_id(0) + first
    count = carried.shape[1]
    half = keep.shape[1]
    code = codes[pl.ds(level, 1), :]
    high = code >> 8
    place = lax.broadcasted_iota(jnp.int32, (256, count), 0)
    hit = jnp.where(place == (code & 255), -1.0, 0.0).astype(bf16)
    for j in range(2 * half // 256):
        pick = hit * jnp.where(high == j, 1.0, 0.0).astype(bf16)
        out, inner = (keep, send)[j * 256 // half], j * 256 % half
        out[0, inner : inner + 256, :] = dot(pick, carried[0]).astype(bf16)


def spread_call(first, levels, codes, carried, entries):
    _, count, depth = carried.shape
    half = entries // 2
    return pl.pallas_call(
        lambda *refs: spread_kernel(first, *refs),
        grid=(levels,),
        in_specs=[
            whole(codes.shape),
            pl.BlockSpec((1, count, depth), lambda i: (i + first, 0, 0)),
        ],
        out_specs=[pl.BlockSpec((1, half, depth), lambda i: (i, 0, 0))] * 2,
        out_shape=[jax.ShapeDtypeStruct((levels, half, depth), bf16)] * 2,
        compiler_params=params(32),
        cost_estimate=cost(1, 5),
        name="spread_codes",
    )(codes, carried)


def backward_kernel(
    carried, branch_second, slope, after_first, branch_first, scales, weights,
    out_second, out_pre, out_after, out_first, out_mixed, sums,
):
    step = pl.program_id(0)
    width = after_first.shape[1]
    units = slope.shape[1]
    proj = 2 * units
    last = proj + carried.shape[2]

    @pl.when(step == 0)
    def _():
        sums[...] = jnp.zeros(sums.shape, f32)

    grad_after = dot_nt(carried[0], weights[:, proj:last])
    sums[5:6, :] += column_sum(grad_after * branch_second[...])
    low = (grad_after * scales[5:6, :]).astype(bf16)
    out_second[...] = low
    grad_normed = jnp.zeros(grad_after.shape, f32)
    chunk = 512
    for left in range(0, units, chunk):
        grad_hidden = dot(low, weights[:, units + left : units + left + chunk])
        part = (grad_hidden * slope[:, left : left + chunk].astype(f32)).astype(bf16)
        out_pre[:, left : left + chunk] = part
        grad_normed = grad_normed + dot_nt(part, weights[:, left : left + chunk])
    normal, rstd = centre_rows(after_first[...])
    sums[2:3, :] += column_sum(grad_normed * normal)
    sums[3:4, :] += column_sum(grad_normed)
    grad_first = grad_after + norm_back(normal, rstd, scales[2:3, :], grad_normed)
    out_after[...] = grad_first
    sums[4:5, :] += column_sum(grad_first * branch_first[...])
    low_first = (grad_first * scales[4:5, :]).astype(bf16)
    out_first[...] = low_first
    out_mixed[...] = dot_nt(low_first, weights[:, last : last + width]).astype(bf16)


def backward_call(carried, branch_second, slope, after_first, branch_first, scales, weights):
    count, width = after_first.shape
    units, depth = slope.shape[1], carried.shape[2]
    row = lambda size: pl.BlockSpec((ROWS, size), lambda i: (i, 0))
    kept = ((width, bf16), (units, bf16), (width, f32), (width, bf16), (width, bf16))
    return pl.pallas_call(
        backward_kernel,
        grid=(count // ROWS,),
        in_specs=[
            pl.BlockSpec((1, ROWS, depth), lambda i: (0, i, 0)),
            row(width),
            row(units),
            row(width),
            row(width),
            whole(scales.shape),
            whole(weights.shape),
        ],
        out_specs=[row(size) for size, _ in kept] + [whole((8, width))],
        out_shape=[jax.ShapeDtypeStruct((count, size), kind) for size, kind in kept]
        + [jax.ShapeDtypeStruct((8, width), f32)],
        compiler_params=params(48),
        cost_estimate=cost(1, 13),
        name="feed_back",
    )(carried, branch_second, slope, after_first, branch_first, scales, weights)


def weight_kernel(
    starts_a, rowmap_a, starts_b, rowmap_b,
    normed, grad_pre, grad_second, hidden, low_out, carried, mixed, grad_first,
    keep_a, send_a, keep_b, send_b, work,
):
    units = hidden.shape[1]
    proj = 2 * units
    last = proj + carried.shape[2]
    chunk = 512
    for left_ref, right_ref, base in ((normed, grad_pre, 0), (grad_second, hidden, units)):
        flipped = flip(left_ref[...])
        for left in range(0, units, chunk):
            work[:, base + left : base + left + chunk] = dot(
                flipped, right_ref[:, left : left + chunk]
            ).astype(bf16)
    work[:, proj:last] = dot(flip(low_out[...]), carried[0]).astype(bf16)
    work[:, last:] = dot(flip(mixed[...]), grad_first[...]).astype(bf16)
    half = keep_a.shape[2]
    pack_rows(starts_a, rowmap_a, work.at[:, :half], (keep_a, send_a))
    pack_rows(starts_b, rowmap_b, work.at[:, half:], (keep_b, send_b))


def weight_call(
    orders, normed, grad_pre, grad_second, hidden, low_out, carried, mixed, grad_first
):
    count, width = normed.shape
    depth = carried.shape[2]
    columns = 2 * hidden.shape[1] + depth + width
    operands = (normed, grad_pre, grad_second, hidden, low_out)
    (starts_a, rowmap_a), (starts_b, rowmap_b) = orders
    piece = (1, width // 2, columns // 2)
    return pl.pallas_call(
        weight_kernel,
        grid=(1,),
        in_specs=[smem(), whole(rowmap_a.shape)] * 2
        + [whole(operand.shape) for operand in operands]
        + [whole((1, count, depth)), whole(mixed.shape), whole(grad_first.shape)],
        out_specs=[whole(piece)] * 4,
        out_shape=[jax.ShapeDtypeStruct(piece, bf16)] * 4,
        scratch_shapes=[pltpu.VMEM((width, columns), bf16)],
        compiler_params=params(58),
        cost_estimate=cost(1, 13),
        name="weight_sums",
    )(starts_a, rowmap_a, starts_b, rowmap_b, *operands, carried, mixed, grad_first)


def attend_back_kernel(
    offset, q, k, v, grad, logsum, bias, cosine, sine, start_k, start_v,
    grad_q, grad_k, grad_v, halo, k_flipped,
):
    step = pl.program_id(0)
    pairs = q.shape[1] // 128

    @pl.when(step == 0)
    def _():
        for pair in range(pairs):
            lanes = slice(pair * 128, (pair + 1) * 128)
            k_flipped[lanes, :] = flip(k[:, lanes])
        grad_k[:MARGIN, :] = start_k[...]
        grad_v[:MARGIN, :] = start_v[...]
        grad_k[MARGIN:, :] = jnp.zeros_like(grad_k[MARGIN:, :])
        grad_v[MARGIN:, :] = jnp.zeros_like(grad_v[MARGIN:, :])

    start = pl.multiple_of((step + offset) * QROWS, QROWS)
    own = pl.multiple_of(step * QROWS, QROWS)
    allowed = jnp.concatenate([bias[0], bias[0]], axis=1)
    back = -sine[...]
    for pair in range(pairs):
        lanes = slice(pair * 128, (pair + 1) * 128)
        heads = (2 * pair, 2 * pair + 1)
        record = jnp.concatenate([logsum[h : h + 1, :] for h in heads], axis=1)
        scores = dot(k[pl.ds(start, SPAN), lanes], head_columns(flip(q[:, lanes]))) + allowed
        weights = jnp.exp(scores - record)
        grad_weights = dot(v[pl.ds(start, SPAN), lanes], head_columns(flip(grad[:, lanes])))
        product = weights * grad_weights
        inner = column_sum(product)
        grad_scores = (product - weights * inner).astype(bf16)
        grad_v[pl.ds(own, SPAN), lanes] += dot(weights.astype(bf16), head_rows(grad[:, lanes]))
        grad_k[pl.ds(own, SPAN), lanes] += dot(grad_scores, head_rows(q[:, lanes]))
        joined = dot(k_flipped[lanes, pl.ds(start, SPAN)], grad_scores)
        flat = jnp.concatenate([joined[:64, :QROWS], joined[64:, QROWS:]], axis=0).T * 0.125
        grad_q[:, lanes] = turn(flat, cosine[...], back).astype(bf16)

    @pl.when(step == pl.num_programs(0) - 1)
    def _():
        halo[:MARGIN, :] = grad_k[:MARGIN, :].astype(bf16)
        halo[MARGIN:, :] = grad_v[:MARGIN, :].astype(bf16)


def attend_back_call(offset, blocks, q, k, v, grad, logsum, bias, cosine, sine, start_k, start_v):
    width = q.shape[1]
    keys = blocks * QROWS + MARGIN
    lead = MARGIN // QROWS
    there = lambda i: (i + offset, 0)
    table = lambda i: (i + offset + lead, 0)
    return pl.pallas_call(
        lambda *refs: attend_back_kernel(offset, *refs),
        grid=(blocks,),
        in_specs=[
            pl.BlockSpec((QROWS, width), there),
            whole(k.shape),
            whole(v.shape),
            pl.BlockSpec((QROWS, width), there),
            pl.BlockSpec((HEADS, QROWS), lambda i: (0, i + offset)),
            pl.BlockSpec((1, SPAN, QROWS), lambda i: (i + offset, 0, 0)),
            pl.BlockSpec((QROWS, 128), table),
            pl.BlockSpec((QROWS, 128), table),
            pl.BlockSpec((MARGIN, width), lambda i: (start_k.shape[0] // MARGIN - 1, 0)),
            pl.BlockSpec((MARGIN, width), lambda i: (start_v.shape[0] // MARGIN - 1, 0)),
        ],
        out_specs=[
            pl.BlockSpec((QROWS, width), lambda i: (i, 0)),
            whole((keys, width)),
            whole((keys, width)),
            whole((2 * MARGIN, width)),
        ],
        out_shape=[
            jax.ShapeDtypeStruct((blocks * QROWS, width), bf16),
            jax.ShapeDtypeStruct((keys, width), f32),
            jax.ShapeDtypeStruct((keys, width), f32),
            jax.ShapeDtypeStruct((2 * MARGIN, width), bf16),
        ],
        scratch_shapes=[pltpu.VMEM((width, k.shape[0]), bf16)],
        compiler_params=params(48),
        cost_estimate=cost(1 if offset == MARGIN // QROWS else 8, 2 * blocks),
        name="attend_back",
    )(q, k, v, grad, logsum, bias, cosine, sine, start_k, start_v)


def finish_kernel(
    starts, rowmap, inputs, normed, q_a, q_b, q_c, k_a, k_b, v_a, v_b, halo, cosine, sine,
    grad_after, scales, sums_second, weights,
    out, keep, send, work, turned_q, turned_k, turned_v, sums,
):
    step = pl.program_id(0)
    last = pl.num_programs(0) - 1
    count, width = normed.shape

    @pl.when(step == 0)
    def _():
        sums[...] = jnp.zeros(sums.shape, f32)
        sums[:8, :] = sums_second[...]
        left = 0
        for piece in (q_a, q_b, q_c):
            turned_q[left : left + piece.shape[0], :] = piece[...]
            left += piece.shape[0]

    rows = pl.ds(pl.multiple_of(step * ROWS, ROWS), ROWS)
    near = jnp.where(step == last, 1.0, 0.0).astype(f32)
    part_k = jnp.where(step == 0, k_a[...], k_b[...]) + near * halo[:MARGIN, :].astype(f32)
    part_v = jnp.where(step == 0, v_a[...], v_b[...]) + near * halo[MARGIN:, :].astype(f32)
    turned = turn(part_k, cosine[...], -sine[...]).astype(bf16)
    turned_k[rows, :] = turned
    value = part_v.astype(bf16)
    turned_v[rows, :] = value
    grad = dot_nt(turned_q[rows, :], weights[:, :width])
    grad = grad + dot_nt(turned, weights[:, width : 2 * width])
    grad = grad + dot_nt(value, weights[:, 2 * width : 3 * width])
    normal, rstd = centre_rows(inputs[...].astype(f32))
    sums[0:1, :] += column_sum(grad * normal)
    sums[1:2, :] += column_sum(grad)
    out[...] = grad_after[...] + norm_back(normal, rstd, scales[0:1, :], grad)

    @pl.when(step == last)
    def _():
        flipped = flip(normed[...])
        for index, turned_ref in enumerate((turned_q, turned_k, turned_v)):
            lanes = slice(index * width, (index + 1) * width)
            work[:, lanes] = dot(flipped, turned_ref[...]).astype(bf16)
        work[:, 3 * width :] = sums[...].T.astype(bf16)
        pack_rows(starts, rowmap, work, (keep, send))


def finish_call(
    starts, rowmap, inputs, normed, grad_q, grad_k, grad_v, halo, cosine, sine,
    grad_after, scales, sums_second, weights,
):
    count, width = normed.shape
    columns = 3 * width + 128
    row = pl.BlockSpec((ROWS, width), lambda i: (i, 0))
    first = pl.BlockSpec((ROWS, width), lambda i: (0, 0))
    rest = pl.BlockSpec((ROWS, width), lambda i: (jnp.maximum(i - 1, 0), 0))
    table = pl.BlockSpec((ROWS, 128), lambda i: (i + MARGIN // ROWS, 0))
    shapes = [jax.ShapeDtypeStruct((count, width), f32)] + [
        jax.ShapeDtypeStruct((1, width // 2, columns), bf16)
    ] * 2
    return pl.pallas_call(
        finish_kernel,
        grid=(count // ROWS,),
        in_specs=[smem(), whole(rowmap.shape), row, whole(normed.shape)]
        + [whole(piece.shape) for piece in grad_q]
        + [first, rest, first, rest]
        + [whole(halo.shape), table, table, row]
        + [whole(scales.shape), whole(sums_second.shape), whole(weights.shape)],
        out_specs=[row, whole(shapes[1].shape), whole(shapes[2].shape)],
        out_shape=shapes,
        scratch_shapes=[
            pltpu.VMEM((width, columns), bf16),
            pltpu.VMEM((count, width), bf16),
            pltpu.VMEM((count, width), bf16),
            pltpu.VMEM((count, width), bf16),
            pltpu.VMEM((128, width), f32),
        ],
        compiler_params=params(48),
        cost_estimate=cost(0, 10),
        name="finish_rows",
    )(
        starts, rowmap, inputs, normed, *grad_q, *grad_k, *grad_v, halo, cosine, sine,
        grad_after, scales, sums_second, weights,
    )


def adam_update(master, first, second, gradient, factor, rate):
    clipped = gradient * factor
    momentum = beta_first * first + (1.0 - beta_first) * clipped
    variance = beta_second * second + (1.0 - beta_second) * clipped * clipped
    corrected = momentum / (1.0 - beta_first**STEP)
    divisor = jnp.sqrt(variance / (1.0 - beta_second**STEP)) + adam_floor
    updated = master - rate * (corrected / divisor + weight_decay * master)
    return (momentum, variance, updated, updated.astype(bf16))


def adam_kernel(factor_ref, grad_feed, grad_qkv, grad_book, *refs):
    factor = factor_ref[0]
    masters, firsts, seconds = refs[0:15:3], refs[1:15:3], refs[2:15:3]
    outs = [refs[15 + 4 * group : 19 + 4 * group] for group in range(5)]

    def update(group, index, gradient):
        results = adam_update(
            masters[group][index], firsts[group][index], seconds[group][index],
            gradient, factor, group_rates[group],
        )
        for out, result in zip(outs[group], results):
            out[index] = result

    width = (grad_qkv.shape[1] - 128) // 3
    units = masters[1].shape[2]
    depth = masters[2].shape[1]
    for k in range(3):
        update(0, k, grad_qkv[:, k * width : (k + 1) * width])
    update(0, 3, grad_feed[:, 2 * units + depth :])
    for k in range(2):
        update(1, k, grad_feed[:, k * units : (k + 1) * units])
    update(2, Ellipsis, grad_feed[:, 2 * units : 2 * units + depth])
    for level in range(LEVELS):
        update(3, level, grad_book[level])
    update(4, Ellipsis, grad_qkv[:, 3 * width :].T[:6])


def adam_call(factor, gradients, states):
    operands = list(gradients) + [array for group in states for array in group]
    shapes = [
        jax.ShapeDtypeStruct(group[0].shape, kind)
        for group in states
        for kind in (f32, f32, f32, bf16)
    ]
    return pl.pallas_call(
        adam_kernel,
        grid=(1,),
        in_specs=[smem()] + [whole(operand.shape) for operand in operands],
        out_specs=[whole(shape.shape) for shape in shapes],
        out_shape=shapes,
        compiler_params=params(40),
        cost_estimate=cost(3, 2),
        name="adam_step",
    )(factor, *operands)


def turn_tables(positions, depth):
    half = depth // 2
    freqs = jnp.exp(-math.log(10000.0) * jnp.arange(half, dtype=f32) * 2.0 / depth)
    angles = positions.astype(f32)[:, None] * freqs[None, :]
    cosine, sine = jnp.cos(angles), jnp.sin(angles)
    return (
        jnp.concatenate([cosine] * 4, axis=1),
        jnp.concatenate([-sine, sine, -sine, sine], axis=1),
    )


def score_bias(count, offset):
    block = jnp.arange(count // QROWS, dtype=jnp.int32)[:, None, None]
    key_place = jnp.arange(SPAN, dtype=jnp.int32)[None, :, None]
    query_place = jnp.arange(QROWS, dtype=jnp.int32)[None, None, :]
    distance = MARGIN + query_place - key_place
    reach = offset + block * QROWS + key_place - MARGIN
    allowed = (distance >= 0) & (distance <= WINDOW) & (reach >= 0)
    return jnp.where(allowed, 0.0, masked_score).astype(f32)


def body(
    inputs, codes, levels,
    attention_master, attention_first, attention_second,
    feedforward_master, feedforward_first, feedforward_second,
    projection_master, projection_first, projection_second,
    codebook_master, codebook_first, codebook_second,
    scales_master, scales_first, scales_second,
):
    spans = lax.axis_size("tm")
    devices = lax.axis_size("clip") * spans
    me = lax.axis_index("clip") * spans + lax.axis_index("tm")
    frame_count, width = inputs.shape
    units = feedforward_master.shape[2]
    depth = projection_master.shape[1]
    rows = projection_master.shape[0]
    entries = codebook_master.shape[1] * devices

    early = jnp.concatenate(
        [
            attention_master[0],
            attention_master[1],
            attention_master[2],
            jnp.pad(scales_master.T, ((0, 0), (0, 128 - scales_master.shape[0]))),
        ],
        axis=1,
    ).astype(bf16)
    feed = jnp.concatenate(
        [feedforward_master[0], feedforward_master[1], projection_master, attention_master[3]],
        axis=1,
    ).astype(bf16)
    mid = LEVELS // 2
    book = lax.all_gather(codebook_master.astype(bf16), AXES, axis=1, tiled=True)
    stages = len(digit_plan(devices, 4))
    halo = lax.ppermute(
        inputs[frame_count - MARGIN :], "tm", [(i, i + 1) for i in range(spans - 1)]
    )
    for stage in reversed(range(2, len(digit_plan(devices, 2)))):
        early = join(early, gather_swaps(early, devices, 2, stage))
    for stage in reversed(range(4, stages)):
        feed = join(feed, after(gather_swaps(feed, devices, 4, stage), early))
    early = join(early, gather_swaps(early, devices, 2, 1))
    come = after(gather_swaps(feed, devices, 4, 3), early)
    early_pieces = (early, swap(early, devices, 1))
    feed_a = join(feed[:, :units], [part[:, :units] for part in come])
    feed_b = join(feed[:, units:], [part[:, units:] for part in come])
    come_a = gather_swaps(feed_a, devices, 4, 2)
    come_b = gather_swaps(feed_b, devices, 5, 2)

    def order(kind):
        owners = jnp.asarray(device_of_places(devices, kind)) ^ me
        starts = (owners * rows).astype(jnp.int32)
        rowmap = (starts[:, None] + jnp.arange(rows, dtype=jnp.int32)[None, :]).reshape(1, width)
        return starts, jnp.broadcast_to(rowmap, (8, width))

    orders = [order(kind) for kind in range(6)]
    offset = lax.axis_index("tm") * frame_count
    positions = offset - MARGIN + jnp.arange(frame_count + MARGIN, dtype=jnp.int32)
    cosine, sine = turn_tables(positions, width // HEADS)
    bias = score_bias(frame_count, offset)
    share = entries // devices
    owners = (codes // share) ^ me
    places = jnp.where(
        jnp.arange(LEVELS)[None, :] < mid,
        place_of(owners, devices, 4),
        place_of(owners, devices, 5),
    )
    flat_codes = (places * share + codes % share).astype(jnp.int32).T

    normed_first, q, k, v, scales, qkv_weights = qkv_call(
        *orders[2], halo, inputs, early_pieces, cosine, sine
    )
    come_a, come_b = after((come_a, come_b), q)
    feed_a, feed_b = join(feed_a, come_a), join(feed_b, come_b)
    come_a = gather_swaps(feed_a, devices, 4, 1)
    come_b = gather_swaps(feed_b, devices, 5, 1)
    mixed, logsum = attend_call(q, after(k, feed_a, feed_b), v, bias)
    come_a, come_b = after((come_a, come_b), mixed)
    feed_a, feed_b = join(feed_a, come_a), join(feed_b, come_b)
    feed_pieces = (feed_a, swap(feed_a, devices, 1), feed_b, swap(feed_b, devices, 1))
    (
        branch_first, after_first, normed_second, hidden, slope, branch_second, low_out, latent,
        feed_weights,
    ) = forward_call(orders[4:], inputs, mixed, scales, feed_pieces, units, depth)

    carried = fetch_call(levels, codes, latent, book)
    keep_high, send_high = spread_call(mid, mid, flat_codes, carried, entries)
    come_high = swap_parts([send_high], devices, 5, 0)
    carried = after(carried, keep_high)
    keep_low, send_low = spread_call(0, mid, flat_codes, carried, entries)
    come_low = swap_parts([send_low], devices, 4, 0)
    keep_high, come_high = reduce_split(keep_high, after(come_high, keep_low), devices, 5, 1)
    keep_low, come_low = reduce_split(keep_low, after(come_low, keep_high), devices, 4, 1)

    carried = after(carried, keep_high, keep_low)
    grad_second, grad_pre, grad_after, grad_first, grad_mixed, sums_second = backward_call(
        carried, branch_second, slope, after_first, branch_first, scales, feed_weights
    )
    keep_a, send_a, keep_b, send_b = weight_call(
        orders[4:], normed_second, grad_pre, grad_second, hidden, low_out, carried, mixed,
        grad_first,
    )
    come_a = swap_parts([send_a], devices, 4, 0)
    come_b = swap_parts([send_b], devices, 5, 0)
    come_high, come_low = after((come_high, come_low), keep_a)
    keep_high, come_high = reduce_split(keep_high, come_high, devices, 5, 2)
    keep_low, come_low = reduce_split(keep_low, come_low, devices, 4, 2)

    lead = MARGIN // QROWS
    blocks = frame_count // QROWS
    zeros = jnp.zeros((MARGIN, width), f32)
    grad_mixed = after(grad_mixed, keep_high, keep_low)
    fixed = (logsum, bias, cosine, sine)
    q_a, k_a, v_a, halo = attend_back_call(0, lead, q, k, v, grad_mixed, *fixed, zeros, zeros)
    halo = lax.ppermute(halo, "tm", [(i + 1, i) for i in range(spans - 1)])
    come_a, come_b = after((come_a, come_b), k_a)
    keep_a, come_a = reduce_split(keep_a, come_a, devices, 4, 1)
    keep_b, come_b = reduce_split(keep_b, come_b, devices, 5, 1)
    grad_mixed = after(grad_mixed, keep_a, keep_b)
    q_b, k_b, v_b, _ = attend_back_call(lead, lead, q, k, v, grad_mixed, *fixed, k_a, v_a)
    come_high, come_low = after((come_high, come_low), k_b)
    keep_book, come_book = merge_split(
        ((keep_low, come_low), (keep_high, come_high)), 0, devices, 4, 3
    )
    grad_mixed = after(grad_mixed, keep_book)
    q_c, k_c, v_c, _ = attend_back_call(
        2 * lead, blocks - 2 * lead, q, k, v, grad_mixed, *fixed, k_b, v_b
    )
    come_a, come_b, come_book = after((come_a, come_b, come_book), k_c)
    for stage in range(4, stages):
        keep_book, come_book = reduce_split(keep_book, come_book, devices, 4, stage)
    keep_a, come_a = reduce_split(keep_a, come_a, devices, 4, 2)
    keep_b, come_b = reduce_split(keep_b, come_b, devices, 5, 2)
    input_gradient, keep_qkv, send_qkv = finish_call(
        *orders[2], inputs, normed_first, (q_a, q_b, q_c), (k_b, after(k_c, keep_a, keep_b, keep_book)),
        (v_b, v_c), halo, cosine, sine, grad_after, scales, sums_second, qkv_weights,
    )
    come_qkv = swap_parts([send_qkv], devices, 2, 0)
    grad_book = reduce_add(keep_book, after(come_book, keep_qkv))
    come_a, come_b = after((come_a, come_b), grad_book)
    keep_feed, come_feed = merge_split(
        ((keep_a, come_a), (keep_b, come_b)), 2, devices, 4, 3, 20
    )
    keep_qkv, come_qkv = reduce_split(keep_qkv, after(come_qkv, keep_feed), devices, 2, 1)
    for stage in range(4, stages):
        keep_feed, come_feed = reduce_split(keep_feed, come_feed, devices, 4, stage)
    for stage in range(2, len(digit_plan(devices, 2))):
        keep_qkv, come_qkv = reduce_split(keep_qkv, come_qkv, devices, 2, stage)
    grad_feed = reduce_add(keep_feed, after(come_feed, keep_qkv))[0]
    grad_qkv = reduce_add(keep_qkv, come_qkv)[0]

    gradients = (grad_feed, grad_qkv, grad_book)
    squares = jnp.zeros((), f32)
    for gradient in gradients:
        squares = squares + jnp.sum(gradient * gradient)
    shared = lax.all_to_all(jnp.broadcast_to(squares, (devices, 128)), AXES, 0, 0, tiled=True)
    gradient_norm = jnp.sqrt(jnp.sum(shared[:, 0]))
    factor = clip_level / jnp.maximum(gradient_norm, clip_level)
    updated = adam_call(
        factor.reshape(1),
        gradients,
        (
            (attention_master, attention_first, attention_second),
            (feedforward_master, feedforward_first, feedforward_second),
            (projection_master, projection_first, projection_second),
            (codebook_master, codebook_first, codebook_second),
            (scales_master, scales_first, scales_second),
        ),
    )
    return (latent, input_gradient, gradient_norm, *updated)


def solution(mesh):
    rows = P(AXES, None)
    middle = P(None, AXES, None)
    scale = P(None, AXES)
    in_specs = (rows, rows, P("clip")) + (middle,) * 6 + (rows,) * 3 + (middle,) * 3 + (scale,) * 3
    out_specs = (rows, rows, P()) + (middle,) * 8 + (rows,) * 4 + (middle,) * 4 + (scale,) * 4
    return jax.shard_map(body, mesh=mesh, in_specs=in_specs, out_specs=out_specs, check_vma=False)
```

time: 1360 us -> 282 us (0.21)
  waiting for transfers between devices: 554 us -> 38.2 us
  matrix products: 266 us -> 0 us
  other arithmetic: 216 us -> 12.5 us
  local copies, waits for them, and re-layouts: 163 us -> 13.3 us
  Pallas kernels: 0 us -> 139 us
  blocking collectives: 122 us -> 9.94 us
  starting transfers between devices: 9.99 us -> 44.1 us
    reduce_scatter x3 -> x0, waiting for transfers between devices: 413 us -> none  [the longest x1 178 us: body(): lax.psum_scatter(local_gradients[3], ('clip', 'tm'), scatter_dimension=1,...]
    dot_general x127 -> x0, matrix products: 266 us -> none  [the longest x16 32 us: head_backward(): jnp.einsum('qd,kd->qk', query_head, key_head, preferred_element_type=jnp....]
    unnamed x16 -> x0, other arithmetic: 143 us -> none
    unnamed x10 -> x1, waiting for transfers between devices: 142 us -> 0.02 us
    pallas_call x0 -> x27, Pallas kernels: none -> 139 us  [the longest x3 26.7 us: attend_back_call(): pl.pallas_call(lambda *refs: attend_back_kernel(offset, *refs), grid=(blo...]
    all_gather x2 -> x0, blocking collectives: 81 us -> none  [the longest x1 43.6 us: body(): lax.all_gather(lowered[4], ('clip', 'tm'), axis=1, tiled=True)]
    gather x8 -> x0, local copies, waits for them, and re-layouts: 46.7 us -> none  [body(): jnp.take(codebook[level_index], codes[:, level_index], axis=0)]
    psum x1 -> x0, blocking collectives: 41.1 us -> none  [body(): total_square = lax.psum(squares, ('clip', 'tm'))]
  transfers between devices with their start and end apart: 12 -> 41, of which waited for: 4 -> 15; matrix products, arithmetic and copies ran while one was open for 26% -> 4% of each run, Pallas kernels for 0% -> 42%
where the time goes in v1:
time: 282 us; the launch traced here: 277 us
  Pallas kernels  139 us (49%)
  starting transfers between devices  44.1 us (16%)
  waiting for transfers between devices  38.2 us (14%)
  between operations  20 us (7%)
  local copies, waits for them, and re-layouts  13.3 us (5%)
  other arithmetic  12.5 us (4%)
  blocking collectives  9.94 us (4%)
    ppermute x38, starting transfers between devices, swap(): return lax.ppermute(block, AXES, [(i, i ^ mask) for i in range(count)])  41.5 us
    ppermute x38, waiting for transfers between devices, swap(): return lax.ppermute(block, AXES, [(i, i ^ mask) for i in range(count)])  37.7 us
    pallas_call x3, Pallas kernels, attend_back_call(): pl.pallas_call(lambda *refs: attend_back_kernel(offset, *refs), grid=(blo...  26.7 us
    pallas_call x1, Pallas kernels, forward_call(): pl.pallas_call(forward_kernel, grid=(count // ROWS,), in_specs=[smem(), w...  17 us
    pallas_call x1, Pallas kernels, attend_call(): pl.pallas_call(attend_kernel, grid=(count // QROWS,), in_specs=[pl.BlockS...  14.3 us
    pallas_call x1, Pallas kernels, backward_call(): pl.pallas_call(backward_kernel, grid=(count // ROWS,), in_specs=[pl.Block...  13.1 us
    pallas_call x1, Pallas kernels, fetch_call(): pl.pallas_call(fetch_kernel, grid=(LEVELS,), in_specs=[smem(), whole(code...  13.1 us
    pallas_call x1, Pallas kernels, weight_call(): pl.pallas_call(weight_kernel, grid=(1,), in_specs=[smem(), whole(rowmap_a...  12.8 us
  transfers between devices with their start and end apart: 41, of which 15 were waited for; matrix products, arithmetic and copies ran while one was open for 4% of the time, Pallas kernels for 42%

profile of v1, /device:TPU:0, one launch (start us, length us, event | category | flops | bytes accessed | tf_op | source)
XLA Modules:
  0.0 277.2 jit_solution(8781201379159529973)
XLA Ops:
  10.8 3.1 %collective-permute-start.1 = (bf16[16,1664]{1,0:T(8,128)(2,1)S(1)}, bf16[16,1664]{1,0:T(8,128)(2,1)S(1)}, u32[]{:S(2)}, u32[]{:S(2)}) collective-permute-start(bf16[16,1664]{1,0:T(8,128)(2,1)S(1)} %get-tuple-element.285), channel_id=1, source_target_pairs={{0,8},{1,9},{2,10},{3,11},{4,12},{5,13},{6,14},{7,15},{8,0},{9,1},... | collective-permute-start | bytes 159752 | tf_op jit(solution)/shard_map/ppermute | solution.py:81
  13.9 2.6 collective-permute-start.2
  33.5 3.0 %collective-permute-done.5 = bf16[64,1664]{1,0:T(8,128)(2,1)S(1)} collective-permute-done((bf16[64,1664]{1,0:T(8,128)(2,1)S(1)}, bf16[64,1664]{1,0:T(8,128)(2,1)S(1)}, u32[]{:S(2)}, u32[]{:S(2)}) %collective-permute-start.5) | collective-permute-done | bytes 213024 | tf_op jit(solution)/shard_map/ppermute | solution.py:81
  36.5 3.3 %collective-permute-done.6 = bf16[64,1664]{1,0:T(8,128)(2,1)S(1)} collective-permute-done((bf16[64,1664]{1,0:T(8,128)(2,1)S(1)}, bf16[64,1664]{1,0:T(8,128)(2,1)S(1)}, u32[]{:S(2)}, u32[]{:S(2)}) %collective-permute-start.6) | collective-permute-done | bytes 213024 | tf_op jit(solution)/shard_map/ppermute | solution.py:81
  44.8 7.6 %project_rows.1 = (bf16[1024,512]{1,0:T(8,128)(2,1)S(1)}, bf16[1024,512]{1,0:T(8,128)(2,1)S(1)}, bf16[1280,512]{1,0:T(8,128)(2,1)}, bf16[1280,512]{1,0:T(8,128)(...) custom-call(s32[32]{0:T(128)S(1)} %xor_multiply_fusion.starts, s32[8,512]{1,0:T(8,128)S(1)} %broadcast_in_dim.25.rowmap, ...), custom_call_target="tpu_custom_call" | custom-call | flops 2000000000 | bytes 25165824 | tf_op jit(solution)/shard_map/project_rows/pallas_call | solution.py:312
  52.4 4.6 %collective-permute-done.10 = bf16[64,2048]{1,0:T(8,128)(2,1)S(1)} collective-permute-done((bf16[64,2048]{1,0:T(8,128)(2,1)S(1)}, bf16[64,2048]{1,0:T(8,128)(2,1)S(1)}, u32[]{:S(2)}, u32[]{:S(2)}) %collective-permute-start.10) | collective-permute-done | bytes 262176 | tf_op jit(solution)/shard_map/ppermute | solution.py:81
  59.8 14.3 %attend_rows.1 = (bf16[1024,512]{1,0:T(8,128)(2,1)S(1)}, f32[8,1024]{1,0:T(8,128)S(1)}) custom-call(bf16[1024,512]{1,0:T(8,128)(2,1)S(1)} %get-tuple-element.148.q.refs_0_, bf16[1280,512]{1,0:T(8,128)(2,1)S(1)} %copy-done.8, bf16[1280,512]{1,0:T(8,128)(2,1)S(1)} %copy-done.9, f32[8,384,128]{2,1,0:T(8,128)S(1)} %and_select_fusion.bias.refs_5_), custom_call_target="tpu_custom_call" | custom-call | flops 2000000000 | bytes 44040192 | tf_op jit(solution)/shard_map/attend_rows/pallas_call | solution.py:378
  74.2 5.1 %collective-permute-done.13 = bf16[128,2816]{1,0:T(8,128)(2,1)S(1)} collective-permute-done((bf16[128,2816]{1,0:T(8,128)(2,1)S(1)}, bf16[128,2816]{1,0:T(8,128)(2,1)S(1)}, u32[]{:S(2)}, u32[]{:S(2)}) %collective-permute-start.13) | collective-permute-done | bytes 720928 | tf_op jit(solution)/shard_map/ppermute | solution.py:81
  81.6 2.9 %collective-permute-done.14.other_a = bf16[256,2048]{1,0:T(8,128)(2,1)} collective-permute-done((bf16[256,2048]{1,0:T(8,128)(2,1)S(1)}, bf16[256,2048]{1,0:T(8,128)(2,1)}, u32[]{:S(2)}, u32[]{:S(2)}) %collective-permute-start.14) | collective-permute-done | bytes 1048608 | tf_op jit(solution)/shard_map/ppermute | solution.py:81
  85.6 17.0 %feed_rows.1 = (f32[1024,512]{1,0:T(8,128)}, f32[1024,512]{1,0:T(8,128)}, bf16[1024,512]{1,0:T(8,128)(2,1)}, bf16[1024,2048]{1,0:T(8,128)(2,1)}, bf16[1024,2048]...) custom-call(s32[32]{0:T(128)} %copy-done.57, ...), custom_call_target="tpu_custom_call" | custom-call | flops 2000000000 | bytes 53477376 | tf_op jit(solution)/shard_map/feed_rows/pallas_call | solution.py:448
  104.3 13.1 %fetch_codes.1.refs_1_.carried = bf16[8,1024,256]{2,1,0:T(8,128)(2,1)S(1)} custom-call(s32[1]{0:T(128)S(6)} %copy.64.active, s32[1024,8]{1,0:T(8,128)S(1)} %copy.55.codes, f32[1024,256]{1,0:T(8,128)S(1)} %copy-done.26, bf16[8,2048,256]{2,1,0:T(8,128)(2,1)} %all-gather.2.cloned.1.call-done.book), custom_call_target="tpu_custom_call" | custom-call | flops 2000000000 | bytes 40894464 | tf_op jit(solution)/shard_map/fetch_codes/pallas_call | solution.py:501
  117.4 5.1 %spread_codes.2 = (bf16[4,1024,256]{2,1,0:T(8,128)(2,1)S(1)}, bf16[4,1024,256]{2,1,0:T(8,128)(2,1)S(1)}) custom-call(s32[8,1024]{1,0:T(8,128)S(1)} %fusion.6.refs_0_, bf16[8,1024,256]{2,1,0:T(8,128)(2,1)S(1)} %fetch_codes.1.refs_1_.carried), custom_call_target="tpu_custom_call" | custom-call | flops 500000000 | bytes 15728640 | tf_op jit(solution)/shard_map/spread_codes/pallas_call | solution.py:539
  122.9 5.1 %spread_codes.3 = (bf16[4,1024,256]{2,1,0:T(8,128)(2,1)S(1)}, bf16[4,1024,256]{2,1,0:T(8,128)(2,1)S(1)}) custom-call(s32[8,1024]{1,0:T(8,128)S(1)} %fusion.6.refs_0_, bf16[8,1024,256]{2,1,0:T(8,128)(2,1)S(1)} %fetch_codes.1.refs_1_.carried), custom_call_target="tpu_custom_call" | custom-call | flops 500000000 | bytes 15728640 | tf_op jit(solution)/shard_map/spread_codes/pallas_call | solution.py:539
  135.9 13.1 %feed_back.1 = (bf16[1024,512]{1,0:T(8,128)(2,1)S(1)}, bf16[1024,2048]{1,0:T(8,128)(2,1)}, f32[1024,512]{1,0:T(8,128)S(1)}, bf16[1024,512]{1,0:T(8,128)(2,1)S(1)...) custom-call(bf16[8,1024,256]{2,1,0:T(8,128)(2,1)} %copy-done, f32[1024,512]{1,0:T(8,128)} %get-tuple-element.172.branch_second, ...), custom_call_target="tpu_custom_call" | custom-call | flops 500000000 | bytes 40894464 | tf_op jit(solution)/shard_map/feed_back/pallas_call | solution.py:595
  154.0 12.8 %weight_sums.1 = (bf16[1,256,2432]{2,1,0:T(8,128)(2,1)}, bf16[1,256,2432]{2,1,0:T(8,128)(2,1)}, bf16[1,256,2432]{2,1,0:T(8,128)(2,1)}, bf16[1,256,2432]{2,1,0:T(8,128)(2,1)}) custom-call(s32[32]{0:T(128)} %copy-done.57, s32[8,512]{1,0:T(8,128)} %broadcast_in_dim.21.rowmap_a, s32[32]{0:T(128)} %copy-done.56, s32[8,512]{1,0:T(8,128)} %broadcast_in_dim.22.rowmap_b, ...), custom_call_target="tpu_custom_call" | custom-call | flops 500000000 | bytes 40894464 | tf_op jit(solution)/shard_map/weight_sums/pallas_call | solution.py:647
  170.5 3.5 %split_sums.16 = (f32[4,256,256]{2,1,0:T(8,128)S(1)}, bf16[4,256,256]{2,1,0:T(8,128)(2,1)}) custom-call(f32[4,512,256]{2,1,0:T(8,128)S(1)} %get-tuple-element.167.refs_0_, bf16[4,512,256]{2,1,0:T(8,128)(2,1)} %collective-permute-done.18.refs_1_), custom_call_target="tpu_custom_call" | custom-call | bytes 3145728 | tf_op jit(solution)/shard_map/split_sums/pallas_call | solution.py:141
  176.2 7.1 %attend_back.3 = (bf16[256,512]{1,0:T(8,128)(2,1)S(1)}, f32[512,512]{1,0:T(8,128)S(1)}, f32[512,512]{1,0:T(8,128)S(1)}, bf16[512,512]{1,0:T(8,128)(2,1)}) custom-call(bf16[1024,512]{1,0:T(8,128)(2,1)S(1)} %copy-done.14, bf16[1280,512]{1,0:T(8,128)(2,1)} %get-tuple-element.154.k.refs_1_, bf16[1280,512]{1,0:T(8,128)(2,1)} %get-tuple-element.155.v.refs_2_, ...), custom_call_target="tpu_custom_call" | custom-call | flops 4000000000 | bytes 12582912 | tf_op jit(solution)/shard_map/attend_back/pallas_call | solution.py:711
  188.5 7.6 %attend_back.4 = (bf16[256,512]{1,0:T(8,128)(2,1)S(1)}, f32[512,512]{1,0:T(8,128)S(1)}, f32[512,512]{1,0:T(8,128)S(1)}, bf16[512,512]{1,0:T(8,128)(2,1)}) custom-call(bf16[1024,512]{1,0:T(8,128)(2,1)S(1)} %copy-done.14, bf16[1280,512]{1,0:T(8,128)(2,1)} %get-tuple-element.154.k.refs_1_, bf16[1280,512]{1,0:T(8,128)(2,1)} %get-tuple-element.155.v.refs_2_, ...), custom_call_target="tpu_custom_call" | custom-call | flops 500000000 | bytes 12582912 | tf_op jit(solution)/shard_map/attend_back/pallas_call | solution.py:711
  199.2 12.0 %attend_back.5 = (bf16[512,512]{1,0:T(8,128)(2,1)S(1)}, f32[768,512]{1,0:T(8,128)}, f32[768,512]{1,0:T(8,128)}, bf16[512,512]{1,0:T(8,128)(2,1)}) custom-call(bf16[1024,512]{1,0:T(8,128)(2,1)S(1)} %copy-done.14, bf16[1280,512]{1,0:T(8,128)(2,1)} %get-tuple-element.154.k.refs_1_, bf16[1280,512]{1,0:T(8,128)(2,1)} %get-tuple-element.155.v.refs_2_, ...), custom_call_target="tpu_custom_call" | custom-call | flops 4000000000 | bytes 25165824 | tf_op jit(solution)/shard_map/attend_back/pallas_call | solution.py:711
  215.2 10.0 %finish_rows.1 = (f32[1024,512]{1,0:T(8,128)}, bf16[1,256,1664]{2,1,0:T(8,128)(2,1)S(1)}, bf16[1,256,1664]{2,1,0:T(8,128)(2,1)S(1)}) custom-call(s32[32]{0:T(128)S(1)} %copy-done.42, s32[8,512]{1,0:T(8,128)S(1)} %copy-done.31, bf16[1024,512]{1,0:T(8,128)(2,1)S(1)} %copy-done.7, bf16[1024,512]{1,0:T(8,128)(2,1)} %copy-done.12, ...), custom_call_target="tpu_custom_call" | custom-call | bytes 31457280 | tf_op jit(solution)/shard_map/finish_rows/pallas_call | solution.py:802
  232.2 5.4 %collective-permute-done.31.refs_1_ = bf16[1,32,4864]{2,1,0:T(8,128)(2,1)S(1)} collective-permute-done((bf16[1,32,4864]{2,1,0:T(8,128)(2,1)S(1)}, bf16[1,32,4864]{2,1,0:T(8,128)(2,1)S(1)}, u32[]{:S(2)}, u32[]{:S(2)}) %collective-permute-start.31) | collective-permute-done | bytes 311328 | tf_op jit(solution)/shard_map/ppermute | solution.py:81
  238.8 2.9 %collective-permute-done.36.refs_3_ = bf16[1,64,1664]{2,1,0:T(8,128)(2,1)S(1)} collective-permute-done((bf16[1,64,1664]{2,1,0:T(8,128)(2,1)S(1)}, bf16[1,64,1664]{2,1,0:T(8,128)(2,1)S(1)}, u32[]{:S(2)}, u32[]{:S(2)}) %collective-permute-start.36) | collective-permute-done | bytes 213024 | tf_op jit(solution)/shard_map/ppermute | solution.py:81
  246.3 2.9 %collective-permute-done.32 = bf16[1,16,4864]{2,1,0:T(8,128)(2,1)S(1)} collective-permute-done((bf16[1,16,4864]{2,1,0:T(8,128)(2,1)S(1)}, bf16[1,16,4864]{2,1,0:T(8,128)(2,1)S(1)}, u32[]{:S(2)}, u32[]{:S(2)}) %collective-permute-start.32) | collective-permute-done | bytes 155680 | tf_op jit(solution)/shard_map/ppermute | solution.py:81
  253.5 9.9 %all_to_all.9 = f32[32,1,128]{2,1,0:T(1,128)S(1)} all-to-all(f32[32,1,128]{2,1,0:T(1,128)S(1)} %broadcast_in_dim.56), channel_id=1, replica_groups=mesh['clip'=8,'tm'=4] {'clip','tm'}, dimensions={0} | all-to-all | bytes 32768 | tf_op jit(solution)/shard_map/all_to_all | solution.py:1059
  (268 shorter events, 83.0 us)
Async XLA Ops:
  7.2 95.9 %all-gather.2.cloned.1.call-start = ((), (), s32[]{:S(2)}) async-start(), calls=%async_computation.1 | async-start | bytes 8650752 | tf_op jit(solution)/shard_map/all_gather | solution.py:936
  10.8 15.4 %collective-permute-start.1 = (bf16[16,1664]{1,0:T(8,128)(2,1)S(1)}, bf16[16,1664]{1,0:T(8,128)(2,1)S(1)}, u32[]{:S(2)}, u32[]{:S(2)}) collective-permute-start(bf16[16,1664]{1,0:T(8,128)(2,1)S(1)} %get-tuple-element.285), channel_id=1, source_target_pairs={{0,8},{1,9},{2,10},{3,11},{4,12},{5,13},{6,14},{7,15},{8,0},{9,1},... | collective-permute-start | bytes 159752 | tf_op jit(solution)/shard_map/ppermute | solution.py:81
  13.9 12.3 %collective-permute-start.2 = (bf16[16,1664]{1,0:T(8,128)(2,1)S(1)}, bf16[16,1664]{1,0:T(8,128)(2,1)S(1)}, u32[]{:S(2)}, u32[]{:S(2)}) collective-permute-start(bf16[16,1664]{1,0:T(8,128)(2,1)S(1)} %get-tuple-element.285), channel_id=1, source_target_pairs={{0,16},{1,17},{2,18},{3,19},{4,20},{5,21},{6,22},{7,23},{8,24},{9,... | collective-permute-start | bytes 159752 | tf_op jit(solution)/shard_map/ppermute | solution.py:81
  18.2 12.1 %collective-permute-start.8 = (bf16[16,4864]{1,0:T(8,128)(2,1)S(1)}, bf16[16,4864]{1,0:T(8,128)(2,1)S(1)}, u32[]{:S(2)}, u32[]{:S(2)}) collective-permute-start(bf16[16,4864]{1,0:T(8,128)(2,1)S(1)} %pad_maximum_fusion.10), channel_id=1, source_target_pairs={{0,16},{1,17},{2,18},{3,19},{4,20},{5,21},{6,22},{7,23},{8,24},{9,... | collective-permute-start | bytes 466952 | tf_op jit(solution)/shard_map/ppermute | solution.py:81
  21.1 23.6 %collective-permute-start = (bf16[256,512]{1,0:T(8,128)(2,1)S(1)}, bf16[256,512]{1,0:T(8,128)(2,1)S(1)}, u32[]{:S(2)}, u32[]{:S(2)}) collective-permute-start(bf16[256,512]{1,0:T(8,128)(2,1)S(1)} %slice.42), channel_id=1, source_target_pairs={{0,1},{1,2},{2,3},{4,5},{5,6},{6,7},{8,9},{9,10},{10,11},{12,13},{... | collective-permute-start | bytes 786440 | tf_op jit(solution)/shard_map/ppermute | solution.py:938
  30.3 11.2 %collective-permute-start.9 = (bf16[32,4864]{1,0:T(8,128)(2,1)S(1)}, bf16[32,4864]{1,0:T(8,128)(2,1)S(1)}, u32[]{:S(2)}, u32[]{:S(2)}) collective-permute-start(bf16[32,4864]{1,0:T(8,128)(2,1)S(1)} %pad_maximum_fusion.7), channel_id=1, source_target_pairs={{0,8},{1,9},{2,10},{3,11},{4,12},{5,13},{6,14},{7,15},{8,0},{9,1},... | collective-permute-start | bytes 933896 | tf_op jit(solution)/shard_map/ppermute | solution.py:81
  41.6 15.4 %collective-permute-start.11 = (bf16[64,2816]{1,0:T(8,128)(2,1)S(1)}, bf16[64,2816]{1,0:T(8,128)(2,1)S(1)}, u32[]{:S(2)}, u32[]{:S(2)}) collective-permute-start(bf16[64,2816]{1,0:T(8,128)(2,1)S(1)} %pad_maximum_fusion.6), channel_id=1, source_target_pairs={{0,2},{1,3},{2,0},{3,1},{4,6},{5,7},{6,4},{7,5},{8,10},{9,11},{10,... | collective-permute-start | bytes 1081352 | tf_op jit(solution)/shard_map/ppermute | solution.py:81
  43.1 13.9 %collective-permute-start.10 = (bf16[64,2048]{1,0:T(8,128)(2,1)S(1)}, bf16[64,2048]{1,0:T(8,128)(2,1)S(1)}, u32[]{:S(2)}, u32[]{:S(2)}) collective-permute-start(bf16[64,2048]{1,0:T(8,128)(2,1)S(1)} %pad_maximum_fusion.8), channel_id=1, source_target_pairs={{0,4},{1,5},{2,6},{3,7},{4,0},{5,1},{6,2},{7,3},{8,12},{9,13},{10,... | collective-permute-start | bytes 786440 | tf_op jit(solution)/shard_map/ppermute | solution.py:81
  57.0 22.3 %collective-permute-start.13 = (bf16[128,2816]{1,0:T(8,128)(2,1)S(1)}, bf16[128,2816]{1,0:T(8,128)(2,1)S(1)}, u32[]{:S(2)}, u32[]{:S(2)}) collective-permute-start(bf16[128,2816]{1,0:T(8,128)(2,1)S(1)} %pad_maximum_fusion.2), channel_id=1, source_target_pairs={{0,4},{1,5},{2,6},{3,7},{4,0},{5,1},{6,2},{7,3},{8,12},{9,13},{10,... | collective-permute-start | bytes 2162696 | tf_op jit(solution)/shard_map/ppermute | solution.py:81
  57.5 16.7 %collective-permute-start.12 = (bf16[128,2048]{1,0:T(8,128)(2,1)S(1)}, bf16[128,2048]{1,0:T(8,128)(2,1)S(1)}, u32[]{:S(2)}, u32[]{:S(2)}) collective-permute-start(bf16[128,2048]{1,0:T(8,128)(2,1)S(1)} %pad_maximum_fusion.5), channel_id=1, source_target_pairs={{0,2},{1,3},{2,0},{3,1},{4,6},{5,7},{6,4},{7,5},{8,10},{9,11},{10,... | collective-permute-start | bytes 1572872 | tf_op jit(solution)/shard_map/ppermute | solution.py:81
  133.9 33.4 %collective-permute-start.19 = (bf16[4,512,256]{2,1,0:T(8,128)(2,1)}, bf16[4,512,256]{2,1,0:T(8,128)(2,1)}, u32[]{:S(2)}, u32[]{:S(2)}) collective-permute-start(bf16[4,512,256]{2,1,0:T(8,128)(2,1)} %get-tuple-element.179), channel_id=1, source_target_pairs={{0,2},{1,3},{2,0},{3,1},{4,6},{5,7},{6,4},{7,5},{8,10},{9,11},{10,... | collective-permute-start | bytes 3145736 | tf_op jit(solution)/shard_map/ppermute | solution.py:81
  134.3 33.1 %collective-permute-start.18 = (bf16[4,512,256]{2,1,0:T(8,128)(2,1)}, bf16[4,512,256]{2,1,0:T(8,128)(2,1)}, u32[]{:S(2)}, u32[]{:S(2)}) collective-permute-start(bf16[4,512,256]{2,1,0:T(8,128)(2,1)} %get-tuple-element.178), channel_id=1, source_target_pairs={{0,4},{1,5},{2,6},{3,7},{4,0},{5,1},{6,2},{7,3},{8,12},{9,13},{10,... | collective-permute-start | bytes 3145736 | tf_op jit(solution)/shard_map/ppermute | solution.py:81
  166.9 16.4 %collective-permute-start.20 = (bf16[1,256,2432]{2,1,0:T(8,128)(2,1)}, bf16[1,256,2432]{2,1,0:T(8,128)(2,1)S(1)}, u32[]{:S(2)}, u32[]{:S(2)}) collective-permute-start(bf16[1,256,2432]{2,1,0:T(8,128)(2,1)} %get-tuple-element.194), channel_id=1, source_target_pairs={{0,1},{1,0},{2,3},{3,2},{4,5},{5,4},{6,7},{7,6},{8,9},{9,8},{10,11... | collective-permute-start | bytes 3735560 | tf_op jit(solution)/shard_map/ppermute | solution.py:81
  166.9 16.4 %collective-permute-start.21 = (bf16[1,256,2432]{2,1,0:T(8,128)(2,1)}, bf16[1,256,2432]{2,1,0:T(8,128)(2,1)S(1)}, u32[]{:S(2)}, u32[]{:S(2)}) collective-permute-start(bf16[1,256,2432]{2,1,0:T(8,128)(2,1)} %get-tuple-element.195), channel_id=1, source_target_pairs={{0,1},{1,0},{2,3},{3,2},{4,5},{5,4},{6,7},{7,6},{8,9},{9,8},{10,11... | collective-permute-start | bytes 3735560 | tf_op jit(solution)/shard_map/ppermute | solution.py:81
  174.0 22.1 %collective-permute-start.23 = (bf16[4,256,256]{2,1,0:T(8,128)(2,1)S(1)}, bf16[4,256,256]{2,1,0:T(8,128)(2,1)S(1)}, u32[]{:S(2)}, u32[]{:S(2)}) collective-permute-start(bf16[4,256,256]{2,1,0:T(8,128)(2,1)S(1)} %get-tuple-element.206), channel_id=1, source_target_pairs={{0,4},{1,5},{2,6},{3,7},{4,0},{5,1},{6,2},{7,3},{8,12},{9,13},{10,... | collective-permute-start | bytes 1572872 | tf_op jit(solution)/shard_map/ppermute | solution.py:81
  174.4 21.7 %collective-permute-start.22 = (bf16[4,256,256]{2,1,0:T(8,128)(2,1)}, bf16[4,256,256]{2,1,0:T(8,128)(2,1)S(1)}, u32[]{:S(2)}, u32[]{:S(2)}) collective-permute-start(bf16[4,256,256]{2,1,0:T(8,128)(2,1)} %get-tuple-element.205), channel_id=1, source_target_pairs={{0,2},{1,3},{2,0},{3,1},{4,6},{5,7},{6,4},{7,5},{8,10},{9,11},{10,... | collective-permute-start | bytes 1572872 | tf_op jit(solution)/shard_map/ppermute | solution.py:81
  186.5 24.8 %collective-permute-start.25 = (bf16[1,128,2432]{2,1,0:T(8,128)(2,1)}, bf16[1,128,2432]{2,1,0:T(8,128)(2,1)S(1)}, u32[]{:S(2)}, u32[]{:S(2)}) collective-permute-start(bf16[1,128,2432]{2,1,0:T(8,128)(2,1)} %get-tuple-element.216), channel_id=1, source_target_pairs={{0,4},{1,5},{2,6},{3,7},{4,0},{5,1},{6,2},{7,3},{8,12},{9,13},{10,... | collective-permute-start | bytes 1867784 | tf_op jit(solution)/shard_map/ppermute | solution.py:81
  187.3 24.0 %collective-permute-start.24 = (bf16[1,128,2432]{2,1,0:T(8,128)(2,1)}, bf16[1,128,2432]{2,1,0:T(8,128)(2,1)S(1)}, u32[]{:S(2)}, u32[]{:S(2)}) collective-permute-start(bf16[1,128,2432]{2,1,0:T(8,128)(2,1)} %get-tuple-element.215), channel_id=1, source_target_pairs={{0,2},{1,3},{2,0},{3,1},{4,6},{5,7},{6,4},{7,5},{8,10},{9,11},{10,... | collective-permute-start | bytes 1867784 | tf_op jit(solution)/shard_map/ppermute | solution.py:81
  196.3 15.0 %collective-permute-start.26 = (bf16[8,128,256]{2,1,0:T(8,128)(2,1)S(1)}, bf16[8,128,256]{2,1,0:T(8,128)(2,1)S(1)}, u32[]{:S(2)}, u32[]{:S(2)}) collective-permute-start(bf16[8,128,256]{2,1,0:T(8,128)(2,1)S(1)} %get-tuple-element.217), channel_id=1, source_target_pairs={{0,8},{1,9},{2,10},{3,11},{4,12},{5,13},{6,14},{7,15},{8,0},{9,1},... | collective-permute-start | bytes 1572872 | tf_op jit(solution)/shard_map/ppermute | solution.py:81
  197.9 17.3 %collective-permute-start.27 = (bf16[512,512]{1,0:T(8,128)(2,1)}, bf16[512,512]{1,0:T(8,128)(2,1)S(1)}, u32[]{:S(2)}, u32[]{:S(2)}) collective-permute-start(bf16[512,512]{1,0:T(8,128)(2,1)} %get-tuple-element.226), channel_id=1, source_target_pairs={{1,0},{2,1},{3,2},{5,4},{6,5},{7,6},{9,8},{10,9},{11,10},{13,12},{... | collective-permute-start | bytes 1572872 | tf_op jit(solution)/shard_map/ppermute | solution.py:1018
  211.6 15.7 %collective-permute-start.30 = (bf16[8,64,256]{2,1,0:T(8,128)(2,1)S(1)}, bf16[8,64,256]{2,1,0:T(8,128)(2,1)S(1)}, u32[]{:S(2)}, u32[]{:S(2)}) collective-permute-start(bf16[8,64,256]{2,1,0:T(8,128)(2,1)S(1)} %get-tuple-element.233), channel_id=1, source_target_pairs={{0,16},{1,17},{2,18},{3,19},{4,20},{5,21},{6,22},{7,23},{8,24},{9,... | collective-permute-start | bytes 786440 | tf_op jit(solution)/shard_map/ppermute | solution.py:81
  212.8 15.3 %collective-permute-start.29 = (bf16[1,64,2432]{2,1,0:T(8,128)(2,1)S(1)}, bf16[1,64,2432]{2,1,0:T(8,128)(2,1)S(1)}, u32[]{:S(2)}, u32[]{:S(2)}) collective-permute-start(bf16[1,64,2432]{2,1,0:T(8,128)(2,1)S(1)} %get-tuple-element.232), channel_id=1, source_target_pairs={{0,2},{1,3},{2,0},{3,1},{4,6},{5,7},{6,4},{7,5},{8,10},{9,11},{10,... | collective-permute-start | bytes 933896 | tf_op jit(solution)/shard_map/ppermute | solution.py:81
  214.4 13.7 %collective-permute-start.28 = (bf16[1,64,2432]{2,1,0:T(8,128)(2,1)S(1)}, bf16[1,64,2432]{2,1,0:T(8,128)(2,1)S(1)}, u32[]{:S(2)}, u32[]{:S(2)}) collective-permute-start(bf16[1,64,2432]{2,1,0:T(8,128)(2,1)S(1)} %get-tuple-element.231), channel_id=1, source_target_pairs={{0,4},{1,5},{2,6},{3,7},{4,0},{5,1},{6,2},{7,3},{8,12},{9,13},{10,... | collective-permute-start | bytes 933896 | tf_op jit(solution)/shard_map/ppermute | solution.py:81
  237.8 11.4 %collective-permute-start.32 = (bf16[1,16,4864]{2,1,0:T(8,128)(2,1)S(1)}, bf16[1,16,4864]{2,1,0:T(8,128)(2,1)S(1)}, u32[]{:S(2)}, u32[]{:S(2)}) collective-permute-start(bf16[1,16,4864]{2,1,0:T(8,128)(2,1)S(1)} %get-tuple-element.241), channel_id=1, source_target_pairs={{0,16},{1,17},{2,18},{3,19},{4,20},{5,21},{6,22},{7,23},{8,24},{9,... | collective-permute-start | bytes 466952 | tf_op jit(solution)/shard_map/ppermute | solution.py:81
  (78 other events, 916.4 us)
Sparse Core Ops, SparseCore 0:
  11.5 91.5 all-gather.1

commit v2 on v1

--- a/solution.py
+++ b/solution.py
@@ -29,6 +29,7 @@
 SPAN = QROWS + MARGIN
 ROWS = 256
 MIB = 1 << 20
+FEED_SHARE, BOOK_SHARE = 4, 2
 
 
 def dot(left, right, contract=((1,), (0,))):
@@ -56,7 +57,7 @@
 
 
 def cost(share, length=1):
-    return pl.CostEstimate(flops=share * 500000000, bytes_accessed=length * 3 * MIB, transcendentals=0)
+    return pl.CostEstimate(flops=int(share * 500000000), bytes_accessed=length * 3 * MIB, transcendentals=0)
 
 
 def after(value, *earlier):
@@ -65,13 +66,10 @@
 
 def digit_plan(count, kind):
     bits = count.bit_length() - 1
-    if kind == 2:
-        plan, shift = [(0, 2)], 1
-    else:
-        middle = [(shift, 2) for shift in range(1, min(3, bits))]
-        plan, shift = [(0, 2)] + (middle[::-1] if kind % 2 else middle), 3
+    middle = [(1, 4)] if kind < 4 else [(1, 2), (2, 2)] if kind == 4 else [(2, 2), (1, 2)]
+    plan, shift = [(0, 2)] + middle, 3
     while shift < bits:
-        width = 1 if kind > 2 else min(2, bits - shift)
+        width = min(2, bits - shift) if kind == 2 else 1
         plan.append((shift, 1 << width))
         shift += width
     return plan
@@ -86,8 +84,39 @@
     return [swap(block, count, k << shift) for k in range(1, radix)]
 
 
-def join(block, others, axis=0):
-    return jnp.concatenate([block] + list(others), axis=axis)
+def join_kernel(count, widths, *refs):
+    outs = refs[count:]
+    top = 0
+    for part in refs[:count]:
+        rows, left = part.shape[0], 0
+        for out, width in zip(outs, widths):
+            out[top : top + rows, :] = part[:, left : left + width]
+            left += width
+        top += rows
+
+
+def join(block, others, widths=None, share=0):
+    parts = [block, *others]
+    rows, columns = block.shape
+    widths = widths or (columns,)
+    if rows % 16:
+        whole_block = jnp.concatenate(parts, axis=0)
+        edges = [sum(widths[:index]) for index in range(len(widths) + 1)]
+        outs = [whole_block[:, left:right] for left, right in zip(edges, edges[1:])]
+    else:
+        outs = pl.pallas_call(
+            lambda *refs: join_kernel(len(parts), widths, *refs),
+            grid=(1,),
+            in_specs=[whole(part.shape) for part in parts],
+            out_specs=[whole((len(parts) * rows, width)) for width in widths],
+            out_shape=[
+                jax.ShapeDtypeStruct((len(parts) * rows, width), block.dtype) for width in widths
+            ],
+            compiler_params=params(16),
+            cost_estimate=cost(share, 1),
+            name="join_rows",
+        )(*parts)
+    return outs[0] if len(widths) == 1 else outs
 
 
 def place_of(device, count, kind):
@@ -127,7 +156,7 @@
         out[...] = total[:, k * size : (k + 1) * size, :].astype(out.dtype)
 
 
-def reduce_split(keep, parts, count, kind, stage):
+def reduce_split(keep, parts, count, kind, stage, share=0, held=f32):
     _, radix = digit_plan(count, kind)[stage]
     lead, rows, columns = keep.shape
     size = rows // radix
@@ -137,21 +166,54 @@
         steps = 2 if columns % 256 == 0 else 1
         block, index = (1, rows, columns // steps), lambda i: (0, 0, i)
     shares = (block[0], size, block[2])
-    kinds = [f32] + [bf16] * (radix - 1)
+    kinds = [held] + [bf16] * (radix - 1)
     outs = pl.pallas_call(
         lambda *refs: split_kernel(radix, *refs),
         grid=(steps,),
         in_specs=[pl.BlockSpec(block, index)] * (1 + len(parts)),
         out_specs=[pl.BlockSpec(shares, index)] * radix,
         out_shape=[jax.ShapeDtypeStruct((lead, size, columns), kind) for kind in kinds],
-        compiler_params=params(32),
-        cost_estimate=cost(0, 1),
+        compiler_params=params(20),
+        cost_estimate=cost(share, 1),
         name="split_sums",
     )(keep, *parts)
     return outs[0], swap_parts(outs[1:], count, kind, stage)
 
 
-def merge_kernel(axis, radix, groups, *refs):
+def pair_kernel(radix, *refs):
+    outs, operands = refs[-2 * radix :], refs[: -2 * radix]
+    half = len(operands) // 2
+    for index in range(2):
+        split_kernel(
+            radix,
+            *operands[index * half : (index + 1) * half],
+            *outs[index * radix : (index + 1) * radix],
+        )
+
+
+def pair_split(low, high, count, kinds, stage):
+    _, radix = digit_plan(count, kinds[0])[stage]
+    lead, rows, columns = low[0].shape
+    spec = lambda size: pl.BlockSpec((1, size, columns), lambda i: (i, 0, 0))
+    operands = [low[0], *low[1], high[0], *high[1]]
+    types = ([f32] + [bf16] * (radix - 1)) * 2
+    outs = pl.pallas_call(
+        lambda *refs: pair_kernel(radix, *refs),
+        grid=(lead,),
+        in_specs=[spec(rows)] * len(operands),
+        out_specs=[spec(rows // radix)] * len(types),
+        out_shape=[jax.ShapeDtypeStruct((lead, rows // radix, columns), kind) for kind in types],
+        compiler_params=params(20),
+        cost_estimate=cost(0, 2),
+        name="split_sums",
+    )(*operands)
+    return (
+        (outs[0], swap_parts(outs[1:radix], count, kinds[0], stage)),
+        (outs[radix], swap_parts(outs[radix + 1 :], count, kinds[1], stage)),
+    )
+
+
+def merge_kernel(radix, groups, *refs):
     outs = refs[-radix:]
     base = left = 0
     for size in groups:
@@ -162,29 +224,66 @@
         rows = total.shape[1] // radix
         for k, out in enumerate(outs):
             share = total[:, k * rows : (k + 1) * rows, :].astype(out.dtype)
-            if axis == 0:
-                out[left : left + total.shape[0]] = share
-            else:
-                out[:, :, left : left + total.shape[2]] = share
-        left += total.shape[axis]
-
-
-def merge_split(groups, axis, count, kind, stage, share=0):
+            out[:, :, left : left + total.shape[2]] = share
+        left += total.shape[2]
+
+
+def merge_split(groups, count, kind, stage, share=0):
     _, radix = digit_plan(count, kind)[stage]
     operands = [array for keep, parts in groups for array in (keep, *parts)]
-    shape = list(groups[0][0].shape)
-    shape[axis] = sum(keep.shape[axis] for keep, _ in groups)
-    shape[1] //= radix
+    _, rows, _ = groups[0][0].shape
+    shape = (1, rows // radix, sum(keep.shape[2] for keep, _ in groups))
     sizes = [1 + len(parts) for _, parts in groups]
     kinds = [f32] + [bf16] * (radix - 1)
     outs = pl.pallas_call(
-        lambda *refs: merge_kernel(axis, radix, sizes, *refs),
+        lambda *refs: merge_kernel(radix, sizes, *refs),
         grid=(1,),
         in_specs=[whole(operand.shape) for operand in operands],
         out_specs=[whole(shape)] * radix,
         out_shape=[jax.ShapeDtypeStruct(shape, kind) for kind in kinds],
-        compiler_params=params(32),
+        compiler_params=params(20),
         cost_estimate=cost(share, 1),
+        name="split_sums",
+    )(*operands)
+    return outs[0], swap_parts(outs[1:], count, kind, stage)
+
+
+def stack_kernel(radix, half, *refs):
+    outs, operands = refs[-radix:], refs[:-radix]
+    size = operands[0].shape[1] // radix
+
+    def add(parts):
+        total = sum(part[...].astype(f32) for part in parts)
+        for k, out in enumerate(outs):
+            out[...] = total[:, k * size : (k + 1) * size, :].astype(out.dtype)
+
+    @pl.when(pl.program_id(0) < half)
+    def _():
+        add(operands[: len(operands) // 2])
+
+    @pl.when(pl.program_id(0) >= half)
+    def _():
+        add(operands[len(operands) // 2 :])
+
+
+def stack_split(low, high, count, kind, stage, share=0):
+    _, radix = digit_plan(count, kind)[stage]
+    operands = [low[0], *low[1], high[0], *high[1]]
+    half, rows, columns = low[0].shape
+    kinds = [f32] + [bf16] * (radix - 1)
+    block = (1, rows, columns)
+    below = pl.BlockSpec(block, lambda i: (jnp.minimum(i, half - 1), 0, 0))
+    above = pl.BlockSpec(block, lambda i: (jnp.maximum(i - half, 0), 0, 0))
+    outs = pl.pallas_call(
+        lambda *refs: stack_kernel(radix, half, *refs),
+        grid=(2 * half,),
+        in_specs=[below] * (1 + len(low[1])) + [above] * (1 + len(high[1])),
+        out_specs=[pl.BlockSpec((1, rows // radix, columns), lambda i: (i, 0, 0))] * radix,
+        out_shape=[
+            jax.ShapeDtypeStruct((2 * half, rows // radix, columns), kind) for kind in kinds
+        ],
+        compiler_params=params(20),
+        cost_estimate=cost(share, 2),
         name="split_sums",
     )(*operands)
     return outs[0], swap_parts(outs[1:], count, kind, stage)
@@ -280,6 +379,41 @@
     return jnp.concatenate(
         [jnp.where(lane < 64, block, zero), jnp.where(lane < 64, zero, block)], axis=0
     )
+
+
+def lower_kernel(attention, feed, projection, book, scales, early, later, low_book, work):
+    width = attention.shape[2]
+    units = feed.shape[2]
+    rows = attention.shape[1]
+    for k in range(3):
+        early[:, k * width : (k + 1) * width] = attention[k].astype(bf16)
+    work[...] = jnp.zeros(work.shape, f32)
+    work[: scales.shape[0], :rows] = scales[...]
+    early[:, 3 * width :] = work[...].T[:rows].astype(bf16)
+    for k in range(2):
+        later[:, k * units : (k + 1) * units] = feed[k].astype(bf16)
+    last = 2 * units + projection.shape[1]
+    later[:, 2 * units : last] = projection[...].astype(bf16)
+    later[:, last:] = attention[3].astype(bf16)
+    low_book[...] = book[...].astype(bf16)
+
+
+def lower_call(attention, feed, projection, book, scales):
+    _, rows, width = attention.shape
+    columns = 2 * feed.shape[2] + projection.shape[1] + width
+    shapes = ((rows, 3 * width + 128), (rows, columns), book.shape)
+    operands = (attention, feed, projection, book, scales)
+    return pl.pallas_call(
+        lower_kernel,
+        grid=(1,),
+        in_specs=[whole(operand.shape) for operand in operands],
+        out_specs=[whole(shape) for shape in shapes],
+        out_shape=[jax.ShapeDtypeStruct(shape, bf16) for shape in shapes],
+        scratch_shapes=[pltpu.VMEM((128, 128), f32)],
+        compiler_params=params(62),
+        cost_estimate=cost(0, 1),
+        name="lower_weights",
+    )(*operands)
 
 
 def qkv_kernel(
@@ -460,7 +594,7 @@
     )(starts_a, rowmap_a, starts_b, rowmap_b, inputs, mixed, scales, *pieces)
 
 
-def fetch_kernel(active, codes, latent, book, carried, residue, steps):
+def fetch_kernel(active, codes, latent, book, carried, residue, steps, columns):
     level = pl.program_id(0)
     count, depth = latent.shape
     tiles = book.shape[1] // 256
@@ -468,13 +602,14 @@
     @pl.when(level == 0)
     def _():
         residue[...] = latent[...]
+        columns[...] = codes[...].astype(f32).T
 
     factor = jnp.where(level < active[0], 1.0, 0.0).astype(f32)
     lane = lax.broadcasted_iota(jnp.int32, (ROWS, LEVELS), 1)
     place = lax.broadcasted_iota(jnp.int32, (ROWS, 256), 1).astype(f32)
     for top in range(0, count, ROWS):
         rows = slice(top, top + ROWS)
-        code = jnp.where(lane == level, codes[rows, :].astype(f32), 0.0)
+        code = jnp.where(lane == level, columns[rows, :], 0.0)
         code = jnp.sum(code, axis=1, keepdims=True)
         high = jnp.floor(code * (1.0 / 256.0))
         hit = jnp.where(place == code - 256.0 * high, 1.0, 0.0).astype(bf16)
@@ -512,6 +647,7 @@
         scratch_shapes=[
             pltpu.VMEM((count, depth), f32),
             pltpu.VMEM((LEVELS, count, depth), f32),
+            pltpu.VMEM((count, LEVELS), f32),
         ],
         compiler_params=params(48),
         cost_estimate=cost(4, 13),
@@ -545,21 +681,26 @@
         ],
         out_specs=[pl.BlockSpec((1, half, depth), lambda i: (i, 0, 0))] * 2,
         out_shape=[jax.ShapeDtypeStruct((levels, half, depth), bf16)] * 2,
-        compiler_params=params(32),
+        compiler_params=params(16),
         cost_estimate=cost(1, 5),
         name="spread_codes",
     )(codes, carried)
 
 
 def backward_kernel(
-    carried, branch_second, slope, after_first, branch_first, scales, weights,
-    out_second, out_pre, out_after, out_first, out_mixed, sums,
+    starts_a, rowmap_a, starts_b, rowmap_b, carried, branch_second, slope, after_first, branch_first, normed, hidden, low_out, mixed,
+    scales, weights,
+    out_after, out_mixed, sums, keep_a, send_a, keep_b, send_b,
+    work, grad_pre, kept_hidden, kept_carried, grad_branch, flipped,
 ):
     step = pl.program_id(0)
+    last_step = pl.num_programs(0) - 1
     width = after_first.shape[1]
     units = slope.shape[1]
     proj = 2 * units
     last = proj + carried.shape[2]
+    chunk = 512
+    rows = pl.ds(pl.multiple_of(step * ROWS, ROWS), ROWS)
 
     @pl.when(step == 0)
     def _():
@@ -568,13 +709,11 @@
     grad_after = dot_nt(carried[0], weights[:, proj:last])
     sums[5:6, :] += column_sum(grad_after * branch_second[...])
     low = (grad_after * scales[5:6, :]).astype(bf16)
-    out_second[...] = low
     grad_normed = jnp.zeros(grad_after.shape, f32)
-    chunk = 512
     for left in range(0, units, chunk):
         grad_hidden = dot(low, weights[:, units + left : units + left + chunk])
         part = (grad_hidden * slope[:, left : left + chunk].astype(f32)).astype(bf16)
-        out_pre[:, left : left + chunk] = part
+        grad_pre[rows, left : left + chunk] = part
         grad_normed = grad_normed + dot_nt(part, weights[:, left : left + chunk])
     normal, rstd = centre_rows(after_first[...])
     sums[2:3, :] += column_sum(grad_normed * normal)
@@ -583,116 +722,108 @@
     out_after[...] = grad_first
     sums[4:5, :] += column_sum(grad_first * branch_first[...])
     low_first = (grad_first * scales[4:5, :]).astype(bf16)
-    out_first[...] = low_first
+    grad_branch[rows, :] = low_first
     out_mixed[...] = dot_nt(low_first, weights[:, last : last + width]).astype(bf16)
-
-
-def backward_call(carried, branch_second, slope, after_first, branch_first, scales, weights):
+    kept_hidden[rows, :] = hidden[...]
+    kept_carried[rows, :] = carried[0]
+    for index, block in enumerate((normed[...], low, low_out[...], mixed[...])):
+        flipped[index, :, rows] = flip(block)
+
+    @pl.when(step == last_step)
+    def _():
+        for left in range(0, units, chunk):
+            lanes = slice(left, left + chunk)
+            work[:, lanes] = dot(flipped[0], grad_pre[:, lanes]).astype(bf16)
+            lanes = slice(left, left + chunk)
+            work[:, units + left : units + left + chunk] = dot(
+                flipped[1], kept_hidden[:, lanes]
+            ).astype(bf16)
+        work[:, proj:last] = dot(flipped[2], kept_carried[...]).astype(bf16)
+        work[:, last:] = dot(flipped[3], grad_branch[...]).astype(bf16)
+        half = keep_a.shape[2]
+        pack_rows(starts_a, rowmap_a, work.at[:, :half], (keep_a, send_a))
+        pack_rows(starts_b, rowmap_b, work.at[:, half:], (keep_b, send_b))
+
+
+def backward_call(
+    orders, carried, branch_second, slope, after_first, branch_first, normed, hidden, low_out,
+    mixed, scales, weights,
+):
     count, width = after_first.shape
     units, depth = slope.shape[1], carried.shape[2]
+    columns = weights.shape[1]
     row = lambda size: pl.BlockSpec((ROWS, size), lambda i: (i, 0))
-    kept = ((width, bf16), (units, bf16), (width, f32), (width, bf16), (width, bf16))
+    piece = (1, width // 2, columns // 2)
+    (starts_a, rowmap_a), (starts_b, rowmap_b) = orders
     return pl.pallas_call(
         backward_kernel,
         grid=(count // ROWS,),
-        in_specs=[
-            pl.BlockSpec((1, ROWS, depth), lambda i: (0, i, 0)),
-            row(width),
-            row(units),
-            row(width),
-            row(width),
-            whole(scales.shape),
-            whole(weights.shape),
-        ],
-        out_specs=[row(size) for size, _ in kept] + [whole((8, width))],
-        out_shape=[jax.ShapeDtypeStruct((count, size), kind) for size, kind in kept]
-        + [jax.ShapeDtypeStruct((8, width), f32)],
-        compiler_params=params(48),
-        cost_estimate=cost(1, 13),
+        in_specs=[smem(), whole(rowmap_a.shape)] * 2
+        + [pl.BlockSpec((1, ROWS, depth), lambda i: (0, i, 0))]
+        + [row(width), row(units), row(width), row(width), row(width), row(units), row(width)]
+        + [row(width), whole(scales.shape), whole(weights.shape)],
+        out_specs=[row(width), row(width), whole((8, width))] + [whole(piece)] * 4,
+        out_shape=[
+            jax.ShapeDtypeStruct((count, width), f32),
+            jax.ShapeDtypeStruct((count, width), bf16),
+            jax.ShapeDtypeStruct((8, width), f32),
+        ]
+        + [jax.ShapeDtypeStruct(piece, bf16)] * 4,
+        scratch_shapes=[
+            pltpu.VMEM((width, columns), bf16),
+            pltpu.VMEM((count, units), bf16),
+            pltpu.VMEM((count, units), bf16),
+            pltpu.VMEM((count, depth), bf16),
+            pltpu.VMEM((count, width), bf16),
+            pltpu.VMEM((4, width, count), bf16),
+        ],
+        compiler_params=params(56),
+        cost_estimate=cost(2, 25),
         name="feed_back",
-    )(carried, branch_second, slope, after_first, branch_first, scales, weights)
-
-
-def weight_kernel(
-    starts_a, rowmap_a, starts_b, rowmap_b,
-    normed, grad_pre, grad_second, hidden, low_out, carried, mixed, grad_first,
-    keep_a, send_a, keep_b, send_b, work,
-):
-    units = hidden.shape[1]
-    proj = 2 * units
-    last = proj + carried.shape[2]
-    chunk = 512
-    for left_ref, right_ref, base in ((normed, grad_pre, 0), (grad_second, hidden, units)):
-        flipped = flip(left_ref[...])
-        for left in range(0, units, chunk):
-            work[:, base + left : base + left + chunk] = dot(
-                flipped, right_ref[:, left : left + chunk]
-            ).astype(bf16)
-    work[:, proj:last] = dot(flip(low_out[...]), carried[0]).astype(bf16)
-    work[:, last:] = dot(flip(mixed[...]), grad_first[...]).astype(bf16)
-    half = keep_a.shape[2]
-    pack_rows(starts_a, rowmap_a, work.at[:, :half], (keep_a, send_a))
-    pack_rows(starts_b, rowmap_b, work.at[:, half:], (keep_b, send_b))
-
-
-def weight_call(
-    orders, normed, grad_pre, grad_second, hidden, low_out, carried, mixed, grad_first
-):
-    count, width = normed.shape
-    depth = carried.shape[2]
-    columns = 2 * hidden.shape[1] + depth + width
-    operands = (normed, grad_pre, grad_second, hidden, low_out)
-    (starts_a, rowmap_a), (starts_b, rowmap_b) = orders
-    piece = (1, width // 2, columns // 2)
-    return pl.pallas_call(
-        weight_kernel,
-        grid=(1,),
-        in_specs=[smem(), whole(rowmap_a.shape)] * 2
-        + [whole(operand.shape) for operand in operands]
-        + [whole((1, count, depth)), whole(mixed.shape), whole(grad_first.shape)],
-        out_specs=[whole(piece)] * 4,
-        out_shape=[jax.ShapeDtypeStruct(piece, bf16)] * 4,
-        scratch_shapes=[pltpu.VMEM((width, columns), bf16)],
-        compiler_params=params(58),
-        cost_estimate=cost(1, 13),
-        name="weight_sums",
-    )(starts_a, rowmap_a, starts_b, rowmap_b, *operands, carried, mixed, grad_first)
-
-
-def attend_back_kernel(
-    offset, q, k, v, grad, logsum, bias, cosine, sine, start_k, start_v,
-    grad_q, grad_k, grad_v, halo, k_flipped,
-):
+    )(
+        starts_a, rowmap_a, starts_b, rowmap_b, carried, branch_second, slope, after_first, branch_first, normed, hidden,
+        low_out, mixed, scales, weights,
+    )
+
+
+def attend_back_kernel(pieces, *refs):
+    k_refs, v_refs = refs[:pieces], refs[pieces : 2 * pieces]
+    (q, grad, logsum, bias, cosine, sine, start_k, start_v,
+     grad_q, grad_k, grad_v, halo, k, v, k_flipped) = refs[2 * pieces :]
     step = pl.program_id(0)
     pairs = q.shape[1] // 128
 
     @pl.when(step == 0)
     def _():
-        for pair in range(pairs):
-            lanes = slice(pair * 128, (pair + 1) * 128)
-            k_flipped[lanes, :] = flip(k[:, lanes])
+        for index in range(pieces):
+            rows = slice(index * MARGIN, (index + 1) * MARGIN)
+            k[rows, :] = k_refs[index][...]
+            v[rows, :] = v_refs[index][...]
+            for pair in range(pairs):
+                lanes = slice(pair * 128, (pair + 1) * 128)
+                k_flipped[lanes, rows] = flip(k_refs[index][:, lanes])
         grad_k[:MARGIN, :] = start_k[...]
         grad_v[:MARGIN, :] = start_v[...]
         grad_k[MARGIN:, :] = jnp.zeros_like(grad_k[MARGIN:, :])
         grad_v[MARGIN:, :] = jnp.zeros_like(grad_v[MARGIN:, :])
 
-    start = pl.multiple_of((step + offset) * QROWS, QROWS)
-    own = pl.multiple_of(step * QROWS, QROWS)
+    start = pl.multiple_of(step * QROWS, QROWS)
+    keys = pl.ds(start, SPAN)
     allowed = jnp.concatenate([bias[0], bias[0]], axis=1)
     back = -sine[...]
     for pair in range(pairs):
         lanes = slice(pair * 128, (pair + 1) * 128)
         heads = (2 * pair, 2 * pair + 1)
         record = jnp.concatenate([logsum[h : h + 1, :] for h in heads], axis=1)
-        scores = dot(k[pl.ds(start, SPAN), lanes], head_columns(flip(q[:, lanes]))) + allowed
+        scores = dot(k[keys, lanes], head_columns(flip(q[:, lanes]))) + allowed
         weights = jnp.exp(scores - record)
-        grad_weights = dot(v[pl.ds(start, SPAN), lanes], head_columns(flip(grad[:, lanes])))
+        grad_weights = dot(v[keys, lanes], head_columns(flip(grad[:, lanes])))
         product = weights * grad_weights
         inner = column_sum(product)
         grad_scores = (product - weights * inner).astype(bf16)
-        grad_v[pl.ds(own, SPAN), lanes] += dot(weights.astype(bf16), head_rows(grad[:, lanes]))
-        grad_k[pl.ds(own, SPAN), lanes] += dot(grad_scores, head_rows(q[:, lanes]))
-        joined = dot(k_flipped[lanes, pl.ds(start, SPAN)], grad_scores)
+        grad_v[keys, lanes] += dot(weights.astype(bf16), head_rows(grad[:, lanes]))
+        grad_k[keys, lanes] += dot(grad_scores, head_rows(q[:, lanes]))
+        joined = dot(k_flipped[lanes, keys], grad_scores)
         flat = jnp.concatenate([joined[:64, :QROWS], joined[64:, QROWS:]], axis=0).T * 0.125
         grad_q[:, lanes] = turn(flat, cosine[...], back).astype(bf16)
 
@@ -706,22 +837,23 @@
     width = q.shape[1]
     keys = blocks * QROWS + MARGIN
     lead = MARGIN // QROWS
+    pieces = keys // MARGIN
     there = lambda i: (i + offset, 0)
     table = lambda i: (i + offset + lead, 0)
+    fixed = lambda index: pl.BlockSpec((MARGIN, width), lambda i: (index, 0))
     return pl.pallas_call(
-        lambda *refs: attend_back_kernel(offset, *refs),
+        lambda *refs: attend_back_kernel(pieces, *refs),
         grid=(blocks,),
-        in_specs=[
+        in_specs=[fixed(offset // lead + index) for index in range(pieces)] * 2
+        + [
             pl.BlockSpec((QROWS, width), there),
-            whole(k.shape),
-            whole(v.shape),
             pl.BlockSpec((QROWS, width), there),
             pl.BlockSpec((HEADS, QROWS), lambda i: (0, i + offset)),
             pl.BlockSpec((1, SPAN, QROWS), lambda i: (i + offset, 0, 0)),
             pl.BlockSpec((QROWS, 128), table),
             pl.BlockSpec((QROWS, 128), table),
-            pl.BlockSpec((MARGIN, width), lambda i: (start_k.shape[0] // MARGIN - 1, 0)),
-            pl.BlockSpec((MARGIN, width), lambda i: (start_v.shape[0] // MARGIN - 1, 0)),
+            fixed(start_k.shape[0] // MARGIN - 1),
+            fixed(start_v.shape[0] // MARGIN - 1),
         ],
         out_specs=[
             pl.BlockSpec((QROWS, width), lambda i: (i, 0)),
@@ -735,17 +867,21 @@
             jax.ShapeDtypeStruct((keys, width), f32),
             jax.ShapeDtypeStruct((2 * MARGIN, width), bf16),
         ],
-        scratch_shapes=[pltpu.VMEM((width, k.shape[0]), bf16)],
-        compiler_params=params(48),
-        cost_estimate=cost(1 if offset == MARGIN // QROWS else 8, 2 * blocks),
+        scratch_shapes=[
+            pltpu.VMEM((keys, width), bf16),
+            pltpu.VMEM((keys, width), bf16),
+            pltpu.VMEM((width, keys), bf16),
+        ],
+        compiler_params=params(20),
+        cost_estimate=cost(0 if offset > 0 else 8, 2 * blocks),
         name="attend_back",
-    )(q, k, v, grad, logsum, bias, cosine, sine, start_k, start_v)
+    )(*[k] * pieces, *[v] * pieces, q, grad, logsum, bias, cosine, sine, start_k, start_v)
 
 
 def finish_kernel(
     starts, rowmap, inputs, normed, q_a, q_b, q_c, k_a, k_b, v_a, v_b, halo, cosine, sine,
     grad_after, scales, sums_second, weights,
-    out, keep, send, work, turned_q, turned_k, turned_v, sums,
+    out, keep_a, send_a, keep_b, send_b, work, turned_q, turned_k, turned_v, sums,
 ):
     step = pl.program_id(0)
     last = pl.num_programs(0) - 1
@@ -783,7 +919,9 @@
             lanes = slice(index * width, (index + 1) * width)
             work[:, lanes] = dot(flipped, turned_ref[...]).astype(bf16)
         work[:, 3 * width :] = sums[...].T.astype(bf16)
-        pack_rows(starts, rowmap, work, (keep, send))
+        half = keep_a.shape[2]
+        pack_rows(starts, rowmap, work.at[:, :half], (keep_a, send_a))
+        pack_rows(starts, rowmap, work.at[:, half:], (keep_b, send_b))
 
 
 def finish_call(
@@ -791,14 +929,16 @@
     grad_after, scales, sums_second, weights,
 ):
     count, width = normed.shape
-    columns = 3 * width + 128
+    columns = 3 * width + 256
     row = pl.BlockSpec((ROWS, width), lambda i: (i, 0))
     first = pl.BlockSpec((ROWS, width), lambda i: (0, 0))
     rest = pl.BlockSpec((ROWS, width), lambda i: (jnp.maximum(i - 1, 0), 0))
     table = pl.BlockSpec((ROWS, 128), lambda i: (i + MARGIN // ROWS, 0))
+    half = columns // 256 * 128
     shapes = [jax.ShapeDtypeStruct((count, width), f32)] + [
-        jax.ShapeDtypeStruct((1, width // 2, columns), bf16)
-    ] * 2
+        jax.ShapeDtypeStruct((1, width // 2, size), bf16)
+        for size in (half, half, columns - half, columns - half)
+    ]
     return pl.pallas_call(
         finish_kernel,
         grid=(count // ROWS,),
@@ -807,16 +947,16 @@
         + [first, rest, first, rest]
         + [whole(halo.shape), table, table, row]
         + [whole(scales.shape), whole(sums_second.shape), whole(weights.shape)],
-        out_specs=[row, whole(shapes[1].shape), whole(shapes[2].shape)],
+        out_specs=[row] + [whole(shape.shape) for shape in shapes[1:]],
         out_shape=shapes,
         scratch_shapes=[
             pltpu.VMEM((width, columns), bf16),
             pltpu.VMEM((count, width), bf16),
             pltpu.VMEM((count, width), bf16),
             pltpu.VMEM((count, width), bf16),
-            pltpu.VMEM((128, width), f32),
-        ],
-        compiler_params=params(48),
+            pltpu.VMEM((256, width), f32),
+        ],
+        compiler_params=params(32),
         cost_estimate=cost(0, 10),
         name="finish_rows",
     )(
@@ -835,10 +975,72 @@
     return (momentum, variance, updated, updated.astype(bf16))
 
 
-def adam_kernel(factor_ref, grad_feed, grad_qkv, grad_book, *refs):
-    factor = factor_ref[0]
+def full_sum(values):
+    return jnp.sum(jnp.sum(values, axis=0, keepdims=True), axis=1, keepdims=True)
+
+
+def book_kernel(keep, *refs):
+    parts, (out, length) = refs[:-2], refs[-2:]
+    total = keep[...]
+    for part in parts:
+        total = total + part[...].astype(f32)
+    out[...] = total
+    length[...] = full_sum(jnp.sum(total * total, axis=0))
+
+
+def book_call(keep, parts):
+    return pl.pallas_call(
+        book_kernel,
+        grid=(1,),
+        in_specs=[whole(keep.shape)] * (1 + len(parts)),
+        out_specs=[whole(keep.shape), whole((1, 1))],
+        out_shape=[
+            jax.ShapeDtypeStruct(keep.shape, f32),
+            jax.ShapeDtypeStruct((1, 1), f32),
+        ],
+        compiler_params=params(16),
+        cost_estimate=cost(BOOK_SHARE, 1),
+        name="book_sums",
+    )(keep, *parts)
+
+
+def total_kernel(groups, squares, *refs):
+    outs, shared = refs[-1 - len(groups) : -1], refs[-1]
+    length = squares[...]
+    base = 0
+    for size, out in zip(groups, outs):
+        total = refs[base][0]
+        for part in refs[base + 1 : base + size]:
+            total = total + part[0].astype(f32)
+        base += size
+        out[...] = total
+        length = length + full_sum(total * total)
+    shared[...] = jnp.broadcast_to(length, shared.shape)
+
+
+def total_call(squares, groups, count):
+    operands = [array for keep, parts in groups for array in (keep, *parts)]
+    sizes = [1 + len(parts) for _, parts in groups]
+    shapes = [keep.shape[1:] for keep, _ in groups] + [(count, 128)]
+    return pl.pallas_call(
+        lambda *refs: total_kernel(sizes, *refs),
+        grid=(1,),
+        in_specs=[whole((1, 1))] + [whole(operand.shape) for operand in operands],
+        out_specs=[whole(shape) for shape in shapes],
+        out_shape=[jax.ShapeDtypeStruct(shape, f32) for shape in shapes],
+        compiler_params=params(16),
+        cost_estimate=cost(0, 1),
+        name="last_sums",
+    )(squares, *operands)
+
+
+def adam_kernel(shared, grad_feed, grad_qkv, grad_book, *refs):
     masters, firsts, seconds = refs[0:15:3], refs[1:15:3], refs[2:15:3]
-    outs = [refs[15 + 4 * group : 19 + 4 * group] for group in range(5)]
+    norm_ref = refs[15]
+    outs = [refs[16 + 4 * group : 20 + 4 * group] for group in range(5)]
+    norm = jnp.sqrt(jnp.sum(shared[:, 0:1], axis=0, keepdims=True))
+    norm_ref[...] = norm
+    factor = clip_level / jnp.maximum(norm, clip_level)
 
     def update(group, index, gradient):
         results = adam_update(
@@ -848,7 +1050,7 @@
         for out, result in zip(outs[group], results):
             out[index] = result
 
-    width = (grad_qkv.shape[1] - 128) // 3
+    width = (grad_qkv.shape[1] - 256) // 3
     units = masters[1].shape[2]
     depth = masters[2].shape[1]
     for k in range(3):
@@ -862,9 +1064,9 @@
     update(4, Ellipsis, grad_qkv[:, 3 * width :].T[:6])
 
 
-def adam_call(factor, gradients, states):
-    operands = list(gradients) + [array for group in states for array in group]
-    shapes = [
+def adam_call(shared, gradients, states):
+    operands = [shared, *gradients] + [array for group in states for array in group]
+    shapes = [jax.ShapeDtypeStruct((1, 1), f32)] + [
         jax.ShapeDtypeStruct(group[0].shape, kind)
         for group in states
         for kind in (f32, f32, f32, bf16)
@@ -872,13 +1074,13 @@
     return pl.pallas_call(
         adam_kernel,
         grid=(1,),
-        in_specs=[smem()] + [whole(operand.shape) for operand in operands],
+        in_specs=[whole(operand.shape) for operand in operands],
         out_specs=[whole(shape.shape) for shape in shapes],
         out_shape=shapes,
         compiler_params=params(40),
         cost_estimate=cost(3, 2),
         name="adam_step",
-    )(factor, *operands)
+    )(*operands)
 
 
 def turn_tables(positions, depth):
@@ -919,48 +1121,34 @@
     rows = projection_master.shape[0]
     entries = codebook_master.shape[1] * devices
 
-    early = jnp.concatenate(
-        [
-            attention_master[0],
-            attention_master[1],
-            attention_master[2],
-            jnp.pad(scales_master.T, ((0, 0), (0, 128 - scales_master.shape[0]))),
-        ],
-        axis=1,
-    ).astype(bf16)
-    feed = jnp.concatenate(
-        [feedforward_master[0], feedforward_master[1], projection_master, attention_master[3]],
-        axis=1,
-    ).astype(bf16)
+    early, feed, book = lower_call(
+        attention_master, feedforward_master, projection_master, codebook_master, scales_master
+    )
     mid = LEVELS // 2
-    book = lax.all_gather(codebook_master.astype(bf16), AXES, axis=1, tiled=True)
-    stages = len(digit_plan(devices, 4))
+    book = lax.all_gather(book, AXES, axis=1, tiled=True)
+    stages = len(digit_plan(devices, 3))
+    split_stages = len(digit_plan(devices, 4))
     halo = lax.ppermute(
         inputs[frame_count - MARGIN :], "tm", [(i, i + 1) for i in range(spans - 1)]
     )
     for stage in reversed(range(2, len(digit_plan(devices, 2)))):
         early = join(early, gather_swaps(early, devices, 2, stage))
-    for stage in reversed(range(4, stages)):
+    mark = early
+    for stage in reversed(range(4, split_stages)):
         feed = join(feed, after(gather_swaps(feed, devices, 4, stage), early))
-    early = join(early, gather_swaps(early, devices, 2, 1))
-    come = after(gather_swaps(feed, devices, 4, 3), early)
-    early_pieces = (early, swap(early, devices, 1))
-    feed_a = join(feed[:, :units], [part[:, :units] for part in come])
-    feed_b = join(feed[:, units:], [part[:, units:] for part in come])
-    come_a = gather_swaps(feed_a, devices, 4, 2)
-    come_b = gather_swaps(feed_b, devices, 5, 2)
-
+    offset = lax.axis_index("tm") * frame_count
+    positions = after(offset, mark) - MARGIN + jnp.arange(frame_count + MARGIN, dtype=jnp.int32)
+    cosine, sine = turn_tables(positions, width // HEADS)
+    bias = score_bias(frame_count, offset)
     def order(kind):
         owners = jnp.asarray(device_of_places(devices, kind)) ^ me
         starts = (owners * rows).astype(jnp.int32)
+        if rows % 16 == 0:
+            return starts, jnp.zeros((1, 128), jnp.int32)
         rowmap = (starts[:, None] + jnp.arange(rows, dtype=jnp.int32)[None, :]).reshape(1, width)
-        return starts, jnp.broadcast_to(rowmap, (8, width))
-
-    orders = [order(kind) for kind in range(6)]
-    offset = lax.axis_index("tm") * frame_count
-    positions = offset - MARGIN + jnp.arange(frame_count + MARGIN, dtype=jnp.int32)
-    cosine, sine = turn_tables(positions, width // HEADS)
-    bias = score_bias(frame_count, offset)
+        return starts, rowmap
+
+    orders = {kind: order(kind) for kind in range(2, 6)}
     share = entries // devices
     owners = (codes // share) ^ me
     places = jnp.where(
@@ -969,6 +1157,14 @@
         place_of(owners, devices, 5),
     )
     flat_codes = (places * share + codes % share).astype(jnp.int32).T
+    flat_codes, orders = after((flat_codes, orders), mark)
+    ready = (cosine, sine, bias, flat_codes, orders)
+    early = join(early, after(gather_swaps(early, devices, 2, 1), ready))
+    come = after(gather_swaps(feed, devices, 4, 3), early)
+    early_pieces = (early, swap(early, devices, 1))
+    feed_a, feed_b = join(feed, come, (units, feed.shape[1] - units), 10)
+    come_a = gather_swaps(feed_a, devices, 4, 2)
+    come_b = gather_swaps(feed_b, devices, 5, 2)
 
     normed_first, q, k, v, scales, qkv_weights = qkv_call(
         *orders[2], halo, inputs, early_pieces, cosine, sine
@@ -984,36 +1180,31 @@
     (
         branch_first, after_first, normed_second, hidden, slope, branch_second, low_out, latent,
         feed_weights,
-    ) = forward_call(orders[4:], inputs, mixed, scales, feed_pieces, units, depth)
-
-    carried = fetch_call(levels, codes, latent, book)
+    ) = forward_call((orders[4], orders[5]), inputs, mixed, scales, feed_pieces, units, depth)
+
+    carried = fetch_call(levels, codes.T, latent, book)
     keep_high, send_high = spread_call(mid, mid, flat_codes, carried, entries)
     come_high = swap_parts([send_high], devices, 5, 0)
     carried = after(carried, keep_high)
     keep_low, send_low = spread_call(0, mid, flat_codes, carried, entries)
     come_low = swap_parts([send_low], devices, 4, 0)
-    keep_high, come_high = reduce_split(keep_high, after(come_high, keep_low), devices, 5, 1)
-    keep_low, come_low = reduce_split(keep_low, after(come_low, keep_high), devices, 4, 1)
-
-    carried = after(carried, keep_high, keep_low)
-    grad_second, grad_pre, grad_after, grad_first, grad_mixed, sums_second = backward_call(
-        carried, branch_second, slope, after_first, branch_first, scales, feed_weights
-    )
-    keep_a, send_a, keep_b, send_b = weight_call(
-        orders[4:], normed_second, grad_pre, grad_second, hidden, low_out, carried, mixed,
-        grad_first,
+    high = reduce_split(keep_high, after(come_high, keep_low), devices, 5, 1, 0, bf16)
+    low = reduce_split(keep_low, after(come_low, high[0]), devices, 4, 1, 0, bf16)
+
+    grad_after, grad_mixed, sums_second, keep_a, send_a, keep_b, send_b = backward_call(
+        (orders[4], orders[5]), after(carried, high[0], low[0]), branch_second, slope, after_first, branch_first,
+        normed_second, hidden, low_out, mixed, scales, feed_weights,
     )
     come_a = swap_parts([send_a], devices, 4, 0)
     come_b = swap_parts([send_b], devices, 5, 0)
-    come_high, come_low = after((come_high, come_low), keep_a)
-    keep_high, come_high = reduce_split(keep_high, come_high, devices, 5, 2)
-    keep_low, come_low = reduce_split(keep_low, come_low, devices, 4, 2)
+    come_low, come_high = after((low[1], high[1]), keep_a)
+    low, high = pair_split((low[0], come_low), (high[0], come_high), devices, (4, 5), 2)
 
     lead = MARGIN // QROWS
     blocks = frame_count // QROWS
     zeros = jnp.zeros((MARGIN, width), f32)
-    grad_mixed = after(grad_mixed, keep_high, keep_low)
     fixed = (logsum, bias, cosine, sine)
+    grad_mixed = after(grad_mixed, low[0])
     q_a, k_a, v_a, halo = attend_back_call(0, lead, q, k, v, grad_mixed, *fixed, zeros, zeros)
     halo = lax.ppermute(halo, "tm", [(i + 1, i) for i in range(spans - 1)])
     come_a, come_b = after((come_a, come_b), k_a)
@@ -1021,47 +1212,43 @@
     keep_b, come_b = reduce_split(keep_b, come_b, devices, 5, 1)
     grad_mixed = after(grad_mixed, keep_a, keep_b)
     q_b, k_b, v_b, _ = attend_back_call(lead, lead, q, k, v, grad_mixed, *fixed, k_a, v_a)
-    come_high, come_low = after((come_high, come_low), k_b)
-    keep_book, come_book = merge_split(
-        ((keep_low, come_low), (keep_high, come_high)), 0, devices, 4, 3
-    )
+    come_low, come_high = after((low[1], high[1]), k_b)
+    keep_book, come_book = stack_split((low[0], come_low), (high[0], come_high), devices, 4, 3)
     grad_mixed = after(grad_mixed, keep_book)
     q_c, k_c, v_c, _ = attend_back_call(
         2 * lead, blocks - 2 * lead, q, k, v, grad_mixed, *fixed, k_b, v_b
     )
-    come_a, come_b, come_book = after((come_a, come_b, come_book), k_c)
-    for stage in range(4, stages):
-        keep_book, come_book = reduce_split(keep_book, come_book, devices, 4, stage)
+    come_book, come_a, come_b = after((come_book, come_a, come_b), k_c)
     keep_a, come_a = reduce_split(keep_a, come_a, devices, 4, 2)
     keep_b, come_b = reduce_split(keep_b, come_b, devices, 5, 2)
-    input_gradient, keep_qkv, send_qkv = finish_call(
-        *orders[2], inputs, normed_first, (q_a, q_b, q_c), (k_b, after(k_c, keep_a, keep_b, keep_book)),
-        (v_b, v_c), halo, cosine, sine, grad_after, scales, sums_second, qkv_weights,
-    )
-    come_qkv = swap_parts([send_qkv], devices, 2, 0)
-    grad_book = reduce_add(keep_book, after(come_book, keep_qkv))
+    for stage in range(4, split_stages):
+        keep_book, come_book = reduce_split(keep_book, come_book, devices, 4, stage)
+    input_gradient, qkv_a, send_a, qkv_b, send_b = finish_call(
+        *orders[2], inputs, normed_first, (q_a, q_b, q_c),
+        (k_b, after(k_c, keep_book, keep_a, keep_b)), (v_b, v_c), halo, cosine, sine, grad_after,
+        scales, sums_second, qkv_weights,
+    )
+    send_a = swap_parts([send_a], devices, 2, 0)
+    send_b = swap_parts([send_b], devices, 2, 0)
+    grad_book, squares = book_call(keep_book, after(come_book, qkv_a))
     come_a, come_b = after((come_a, come_b), grad_book)
     keep_feed, come_feed = merge_split(
-        ((keep_a, come_a), (keep_b, come_b)), 2, devices, 4, 3, 20
-    )
-    keep_qkv, come_qkv = reduce_split(keep_qkv, after(come_qkv, keep_feed), devices, 2, 1)
-    for stage in range(4, stages):
+        ((keep_a, come_a), (keep_b, come_b)), devices, 4, 3, FEED_SHARE
+    )
+    send_a, send_b = after((send_a, send_b), keep_feed)
+    keep_qkv, come_qkv = merge_split(((qkv_a, send_a), (qkv_b, send_b)), devices, 2, 1)
+    for stage in range(4, split_stages):
         keep_feed, come_feed = reduce_split(keep_feed, come_feed, devices, 4, stage)
     for stage in range(2, len(digit_plan(devices, 2))):
         keep_qkv, come_qkv = reduce_split(keep_qkv, come_qkv, devices, 2, stage)
-    grad_feed = reduce_add(keep_feed, after(come_feed, keep_qkv))[0]
-    grad_qkv = reduce_add(keep_qkv, come_qkv)[0]
-
-    gradients = (grad_feed, grad_qkv, grad_book)
-    squares = jnp.zeros((), f32)
-    for gradient in gradients:
-        squares = squares + jnp.sum(gradient * gradient)
-    shared = lax.all_to_all(jnp.broadcast_to(squares, (devices, 128)), AXES, 0, 0, tiled=True)
-    gradient_norm = jnp.sqrt(jnp.sum(shared[:, 0]))
-    factor = clip_level / jnp.maximum(gradient_norm, clip_level)
-    updated = adam_call(
-        factor.reshape(1),
-        gradients,
+    grad_feed, grad_qkv, shared = total_call(
+        squares, ((keep_feed, come_feed), (keep_qkv, come_qkv)), devices
+    )
+
+    shared = lax.all_to_all(shared, AXES, 0, 0, tiled=True)
+    gradient_norm, *updated = adam_call(
+        shared,
+        (grad_feed, grad_qkv, grad_book),
         (
             (attention_master, attention_first, attention_second),
             (feedforward_master, feedforward_first, feedforward_second),
@@ -1070,7 +1257,7 @@
             (scales_master, scales_first, scales_second),
         ),
     )
-    return (latent, input_gradient, gradient_norm, *updated)
+    return (latent, input_gradient, gradient_norm[0, 0], *updated)
 
 
 def solution(mesh):

time: 282 us -> 255 us (0.904)
  Pallas kernels: 139 us -> 122 us
  starting transfers between devices: 44.1 us -> 49.5 us
  local copies, waits for them, and re-layouts: 13.3 us -> 7.99 us
  other arithmetic: 12.5 us -> 7.37 us
  between operations: 20 us -> 16.1 us
    pallas_call x12 -> x9, Pallas kernels: 11.9 us -> 4.82 us  [reduce_split(): pl.pallas_call(lambda *refs: split_kernel(radix, *refs), grid=(steps,), i...]
    pallas_call x8 -> x20, Pallas kernels: 55 us -> 48.1 us  [the longest x1 22.1 us: backward_call(): pl.pallas_call(backward_kernel, grid=(count // ROWS,), in_specs=[smem(),...]
    ppermute x38 -> x39, starting transfers between devices: 41.5 us -> 45.6 us  [swap(): return lax.ppermute(block, AXES, [(i, i ^ mask) for i in range(count)])]
    unnamed x128 -> x96, local copies, waits for them, and re-layouts: 10.6 us -> 6.96 us
    another operation x4 -> x0, other arithmetic: 3.3 us -> none
    ppermute x38 -> x39, waiting for transfers between devices: 37.7 us -> 36.4 us  [swap(): return lax.ppermute(block, AXES, [(i, i ^ mask) for i in range(count)])]
  transfers between devices with their start and end apart: 41 -> 42, of which waited for: 15 -> 17; matrix products, arithmetic and copies ran while one was open for 4% -> 3% of each run, Pallas kernels for 42% -> 39%
where the time goes in v2:
time: 255 us; the launch traced here: 250 us
  Pallas kernels  122 us (48%)
  starting transfers between devices  49.5 us (19%)
  waiting for transfers between devices  37.9 us (15%)
  between operations  16.1 us (6%)
  blocking collectives  9.14 us (4%)
  local copies, waits for them, and re-layouts  7.99 us (3%)
  other arithmetic  7.37 us (3%)
    ppermute x39, starting transfers between devices, swap(): return lax.ppermute(block, AXES, [(i, i ^ mask) for i in range(count)])  45.6 us
    ppermute x39, waiting for transfers between devices, swap(): return lax.ppermute(block, AXES, [(i, i ^ mask) for i in range(count)])  36.4 us
    pallas_call x1, Pallas kernels, backward_call(): pl.pallas_call(backward_kernel, grid=(count // ROWS,), in_specs=[smem(),...  22.1 us
    pallas_call x3, Pallas kernels, attend_back_call(): pl.pallas_call(lambda *refs: attend_back_kernel(pieces, *refs), grid=(blo...  18.5 us
    pallas_call x1, Pallas kernels, forward_call(): pl.pallas_call(forward_kernel, grid=(count // ROWS,), in_specs=[smem(), w...  16.9 us
    pallas_call x1, Pallas kernels, attend_call(): pl.pallas_call(attend_kernel, grid=(count // QROWS,), in_specs=[pl.BlockS...  14.3 us
    pallas_call x1, Pallas kernels, fetch_call(): pl.pallas_call(fetch_kernel, grid=(LEVELS,), in_specs=[smem(), whole(code...  13.1 us
    pallas_call x2, Pallas kernels, spread_call(): pl.pallas_call(lambda *refs: spread_kernel(first, *refs), grid=(levels,),...  10.2 us
  transfers between devices with their start and end apart: 42, of which 17 were waited for; matrix products, arithmetic and copies ran while one was open for 3% of the time, Pallas kernels for 39%

profile of v2, /device:TPU:0, one launch (start us, length us, event | category | flops | bytes accessed | tf_op | source)
XLA Modules:
  0.0 250.3 jit_solution(3883409108661002107)
XLA Ops:
  9.2 3.1 %collective-permute-start = (bf16[16,1664]{1,0:T(8,128)(2,1)}, bf16[16,1664]{1,0:T(8,128)(2,1)S(1)}, u32[]{:S(2)}, u32[]{:S(2)}) collective-permute-start(bf16[16,1664]{1,0:T(8,128)(2,1)} %get-tuple-element.169.refs_0_), channel_id=1, source_target_pairs={{0,8},{1,9},{2,10},{3,11},{4,12},{5,13},{6,14},{7,15},{8,0},{9,1},... | collective-permute-start | bytes 159752 | tf_op jit(solution)/shard_map/ppermute | solution.py:79
  12.3 2.6 %collective-permute-start.1 = (bf16[16,1664]{1,0:T(8,128)(2,1)}, bf16[16,1664]{1,0:T(8,128)(2,1)S(1)}, u32[]{:S(2)}, u32[]{:S(2)}) collective-permute-start(bf16[16,1664]{1,0:T(8,128)(2,1)} %get-tuple-element.169.refs_0_), channel_id=1, source_target_pairs={{0,16},{1,17},{2,18},{3,19},{4,20},{5,21},{6,22},{7,23},{8,24},{9,... | collective-permute-start | bytes 159752 | tf_op jit(solution)/shard_map/ppermute | solution.py:79
  27.7 3.3 %collective-permute-start.9 = (bf16[32,4864]{1,0:T(8,128)(2,1)S(1)}, bf16[32,4864]{1,0:T(8,128)(2,1)S(1)}, u32[]{:S(2)}, u32[]{:S(2)}) collective-permute-start(bf16[32,4864]{1,0:T(8,128)(2,1)S(1)} %join_rows.10.refs_0_), channel_id=1, source_target_pairs={{0,8},{1,9},{2,10},{3,11},{4,12},{5,13},{6,14},{7,15},{8,0},{9,1},... | collective-permute-start | bytes 933896 | tf_op jit(solution)/shard_map/ppermute | solution.py:79
  35.5 2.6 %collective-permute-start.3 = (bf16[256,512]{1,0:T(8,128)(2,1)S(1)}, bf16[256,512]{1,0:T(8,128)(2,1)S(1)}, u32[]{:S(2)}, u32[]{:S(2)}) collective-permute-start(bf16[256,512]{1,0:T(8,128)(2,1)S(1)} %slice.3), channel_id=1, source_target_pairs={{0,1},{1,2},{2,3},{4,5},{5,6},{6,7},{8,9},{9,10},{10,11},{12,13},{... | collective-permute-start | bytes 786440 | tf_op jit(solution)/shard_map/ppermute | solution.py:1131
  42.4 7.4 %project_rows.1 = (bf16[1024,512]{1,0:T(8,128)(2,1)S(1)}, bf16[1024,512]{1,0:T(8,128)(2,1)S(1)}, bf16[1280,512]{1,0:T(8,128)(2,1)}, bf16[1280,512]{1,0:T(8,128)(...) custom-call(s32[32]{0:T(128)S(1)} %xor_multiply_fusion.2.starts, ...), custom_call_target="tpu_custom_call" | custom-call | flops 2000000000 | bytes 25165824 | tf_op jit(solution)/shard_map/project_rows/pallas_call | solution.py:446
  49.8 3.2 %collective-permute-done.10.refs_1_ = bf16[64,2048]{1,0:T(8,128)(2,1)S(1)} collective-permute-done((bf16[64,2048]{1,0:T(8,128)(2,1)S(1)}, bf16[64,2048]{1,0:T(8,128)(2,1)S(1)}, u32[]{:S(2)}, u32[]{:S(2)}) %collective-permute-start.10) | collective-permute-done | bytes 262176 | tf_op jit(solution)/shard_map/ppermute | solution.py:79
  59.1 14.3 %attend_rows.1 = (bf16[1024,512]{1,0:T(8,128)(2,1)S(1)}, f32[8,1024]{1,0:T(8,128)S(1)}) custom-call(bf16[1024,512]{1,0:T(8,128)(2,1)S(1)} %get-tuple-element.181.q.refs_4_.refs_6_, bf16[1280,512]{1,0:T(8,128)(2,1)S(1)} %copy-done.1, bf16[1280,512]{1,0:T(8,128)(2,1)S(1)} %copy-done.2, f32[8,384,128]{2,1,0:T(8,128)S(1)} %and_select_fusion.bias.refs_7_.refs_9_), custom_call_target="tpu_custom_call" | custom-call | flops 2000000000 | bytes 44040192 | tf_op jit(solution)/shard_map/attend_rows/pallas_call | solution.py:512
  76.6 3.5 %collective-permute-done.14.other_a = bf16[256,2048]{1,0:T(8,128)(2,1)S(1)} collective-permute-done((bf16[256,2048]{1,0:T(8,128)(2,1)S(1)}, bf16[256,2048]{1,0:T(8,128)(2,1)S(1)}, u32[]{:S(2)}, u32[]{:S(2)}) %collective-permute-start.14) | collective-permute-done | bytes 1048608 | tf_op jit(solution)/shard_map/ppermute | solution.py:79
  82.2 16.9 %feed_rows.1 = (f32[1024,512]{1,0:T(8,128)}, f32[1024,512]{1,0:T(8,128)}, bf16[1024,512]{1,0:T(8,128)(2,1)}, bf16[1024,2048]{1,0:T(8,128)(2,1)}, bf16[1024,2048]...) custom-call(s32[32]{0:T(128)} %get-tuple-element.170.starts_a, ...), custom_call_target="tpu_custom_call" | custom-call | flops 2000000000 | bytes 53477376 | tf_op jit(solution)/shard_map/feed_rows/pallas_call | solution.py:582
  102.5 13.1 %fetch_codes.1.refs_1_.carried = bf16[8,1024,256]{2,1,0:T(8,128)(2,1)S(1)} custom-call(s32[1]{0:T(128)S(6)} %copy.47.active, s32[8,1024]{1,0:T(8,128)S(1)} %bitcast.8, f32[1024,256]{1,0:T(8,128)S(1)} %copy-done.17, bf16[8,2048,256]{2,1,0:T(8,128)(2,1)} %all-gather.2.cloned.1.call-done.book), custom_call_target="tpu_custom_call" | custom-call | flops 2000000000 | bytes 40894464 | tf_op jit(solution)/shard_map/fetch_codes/pallas_call | solution.py:636
  115.6 5.1 %spread_codes.2 = (bf16[4,1024,256]{2,1,0:T(8,128)(2,1)S(1)}, bf16[4,1024,256]{2,1,0:T(8,128)(2,1)S(1)}) custom-call(s32[8,1024]{1,0:T(8,128)S(1)} %copy-done.21, bf16[8,1024,256]{2,1,0:T(8,128)(2,1)S(1)} %fetch_codes.1.refs_1_.carried), custom_call_target="tpu_custom_call" | custom-call | flops 500000000 | bytes 15728640 | tf_op jit(solution)/shard_map/spread_codes/pallas_call | solution.py:675
  121.1 5.1 %spread_codes.3 = (bf16[4,1024,256]{2,1,0:T(8,128)(2,1)S(1)}, bf16[4,1024,256]{2,1,0:T(8,128)(2,1)S(1)}) custom-call(s32[8,1024]{1,0:T(8,128)S(1)} %copy-done.21, bf16[8,1024,256]{2,1,0:T(8,128)(2,1)S(1)} %fetch_codes.1.refs_1_.carried), custom_call_target="tpu_custom_call" | custom-call | flops 500000000 | bytes 15728640 | tf_op jit(solution)/shard_map/spread_codes/pallas_call | solution.py:675
  136.3 22.1 %feed_back.1 = (f32[1024,512]{1,0:T(8,128)}, bf16[1024,512]{1,0:T(8,128)(2,1)}, f32[8,512]{1,0:T(8,128)}, bf16[1,256,2432]{2,1,0:T(8,128)(2,1)}, bf16[1,256,2432...) custom-call(s32[32]{0:T(128)} %get-tuple-element.170.starts_a, s32[1,128]{1,0:T(1,128)} %copy-done.33, ...), custom_call_target="tpu_custom_call" | custom-call | flops 1000000000 | bytes 78643200 | tf_op jit(solution)/shard_map/feed_back/pallas_call | solution.py:758
  162.7 4.2 %attend_back.3 = (bf16[256,512]{1,0:T(8,128)(2,1)S(1)}, f32[512,512]{1,0:T(8,128)S(1)}, f32[512,512]{1,0:T(8,128)S(1)}, bf16[512,512]{1,0:T(8,128)(2,1)S(1)}) custom-call(bf16[1280,512]{1,0:T(8,128)(2,1)S(1)} %copy-done.1, bf16[1280,512]{1,0:T(8,128)(2,1)S(1)} %copy-done.1, bf16[1280,512]{1,0:T(8,128)(2,1)S(1)} %copy-done.3, ...), custom_call_target="tpu_custom_call" | custom-call | flops 4000000000 | bytes 12582912 | tf_op jit(solution)/shard_map/attend_back/pallas_call | solution.py:844
  170.6 5.3 %attend_back.4 = (bf16[256,512]{1,0:T(8,128)(2,1)S(1)}, f32[512,512]{1,0:T(8,128)S(1)}, f32[512,512]{1,0:T(8,128)S(1)}, bf16[512,512]{1,0:T(8,128)(2,1)}) custom-call(bf16[1280,512]{1,0:T(8,128)(2,1)S(1)} %copy-done.1, bf16[1280,512]{1,0:T(8,128)(2,1)S(1)} %copy-done.1, bf16[1280,512]{1,0:T(8,128)(2,1)S(1)} %copy-done.3, bf16[1280,512]{1,0:T(8,128)(2,1)S(1)} %copy-done.3, ...), custom_call_target="tpu_custom_call" | custom-call | bytes 12582912 | tf_op jit(solution)/shard_map/attend_back/pallas_call | solution.py:844
  177.5 3.0 %collective-permute-start.24 = (bf16[8,128,256]{2,1,0:T(8,128)(2,1)S(1)}, bf16[8,128,256]{2,1,0:T(8,128)(2,1)S(1)}, u32[]{:S(2)}, u32[]{:S(2)}) collective-permute-start(bf16[8,128,256]{2,1,0:T(8,128)(2,1)S(1)} %get-tuple-element.249), channel_id=1, source_target_pairs={{0,8},{1,9},{2,10},{3,11},{4,12},{5,13},{6,14},{7,15},{8,0},{9,1},... | collective-permute-start | bytes 1572872 | tf_op jit(solution)/shard_map/ppermute | solution.py:79
  181.8 9.1 %attend_back.5 = (bf16[512,512]{1,0:T(8,128)(2,1)S(1)}, f32[768,512]{1,0:T(8,128)S(1)}, f32[768,512]{1,0:T(8,128)S(1)}, bf16[512,512]{1,0:T(8,128)(2,1)}) custom-call(bf16[1280,512]{1,0:T(8,128)(2,1)S(1)} %copy-done.1, bf16[1280,512]{1,0:T(8,128)(2,1)S(1)} %copy-done.1, bf16[1280,512]{1,0:T(8,128)(2,1)S(1)} %copy-done.1, bf16[1280,512]{1,0:T(8,128)(2,1)S(1)} %copy-done.3, ...), custom_call_target="tpu_custom_call" | custom-call | bytes 25165824 | tf_op jit(solution)/shard_map/attend_back/pallas_call | solution.py:844
  193.3 7.5 %finish_rows.1 = (f32[1024,512]{1,0:T(8,128)}, bf16[1,256,896]{2,1,0:T(8,128)(2,1)S(1)}, bf16[1,256,896]{2,1,0:T(8,128)(2,1)S(1)}, bf16[1,256,896]{2,1,0:T(8,128)(2,1)S(1)}, bf16[1,256,896]{2,1,0:T(8,128)(2,1)S(1)}) custom-call(s32[32]{0:T(128)S(1)} %xor_multiply_fusion.2.starts, s32[1,128]{1,0:T(1,128)S(1)} %copy-done.34, bf16[1024,512]{1,0:T(8,128)(2,1)S(1)} %copy-done.11, ...), custom_call_target="tpu_custom_call" | custom-call | bytes 31457280 | tf_op jit(solution)/shard_map/finish_rows/pallas_call | solution.py:942
  201.9 4.6 %collective-permute-done.28.refs_0_ = bf16[8,64,256]{2,1,0:T(8,128)(2,1)S(1)} collective-permute-done((bf16[8,64,256]{2,1,0:T(8,128)(2,1)S(1)}, bf16[8,64,256]{2,1,0:T(8,128)(2,1)S(1)}, u32[]{:S(2)}, u32[]{:S(2)}) %collective-permute-start.28) | collective-permute-done | bytes 262176 | tf_op jit(solution)/shard_map/ppermute | solution.py:79
  208.6 2.7 %collective-permute-start.37 = (bf16[1,64,1792]{2,1,0:T(8,128)(2,1)S(1)}, bf16[1,64,1792]{2,1,0:T(8,128)(2,1)S(1)}, u32[]{:S(2)}, u32[]{:S(2)}) collective-permute-start(bf16[1,64,1792]{2,1,0:T(8,128)(2,1)S(1)} %get-tuple-element.286), channel_id=1, source_target_pairs={{0,6},{1,7},{2,4},{3,5},{4,2},{5,3},{6,0},{7,1},{8,14},{9,15},{10,... | collective-permute-start | bytes 688136 | tf_op jit(solution)/shard_map/ppermute | solution.py:79
  211.4 5.4 %collective-permute-done.31.refs_1_ = bf16[1,32,4864]{2,1,0:T(8,128)(2,1)S(1)} collective-permute-done((bf16[1,32,4864]{2,1,0:T(8,128)(2,1)S(1)}, bf16[1,32,4864]{2,1,0:T(8,128)(2,1)S(1)}, u32[]{:S(2)}, u32[]{:S(2)}) %collective-permute-start.31) | collective-permute-done | bytes 311328 | tf_op jit(solution)/shard_map/ppermute | solution.py:79
  217.1 4.5 %collective-permute-done.37.refs_3_ = bf16[1,64,1792]{2,1,0:T(8,128)(2,1)S(1)} collective-permute-done((bf16[1,64,1792]{2,1,0:T(8,128)(2,1)S(1)}, bf16[1,64,1792]{2,1,0:T(8,128)(2,1)S(1)}, u32[]{:S(2)}, u32[]{:S(2)}) %collective-permute-start.37) | collective-permute-done | bytes 229408 | tf_op jit(solution)/shard_map/ppermute | solution.py:79
  223.7 2.7 %collective-permute-start.40 = (bf16[1,16,1792]{2,1,0:T(8,128)(2,1)S(1)}, bf16[1,16,1792]{2,1,0:T(8,128)(2,1)S(1)}, u32[]{:S(2)}, u32[]{:S(2)}) collective-permute-start(bf16[1,16,1792]{2,1,0:T(8,128)(2,1)S(1)} %get-tuple-element.290), channel_id=1, source_target_pairs={{0,24},{1,25},{2,26},{3,27},{4,28},{5,29},{6,30},{7,31},{8,16},{9,... | collective-permute-start | bytes 172040 | tf_op jit(solution)/shard_map/ppermute | solution.py:79
  231.5 9.1 %all_to_all.11 = f32[32,1,128]{2,1,0:T(1,128)S(1)} all-to-all(f32[32,1,128]{2,1,0:T(1,128)S(1)} %bitcast.10), channel_id=1, replica_groups=mesh['clip'=8,'tm'=4] {'clip','tm'}, dimensions={0} | all-to-all | bytes 32768 | tf_op jit(solution)/shard_map/all_to_all | solution.py:1248
  (210 shorter events, 73.8 us)
Async XLA Ops:
  7.2 93.3 %all-gather.2.cloned.1.call-start = ((), (), s32[]{:S(2)}) async-start(), calls=%async_computation.1 | async-start | bytes 8650752 | tf_op jit(solution)/shard_map/all_gather | solution.py:1128
  9.2 11.5 %collective-permute-start = (bf16[16,1664]{1,0:T(8,128)(2,1)}, bf16[16,1664]{1,0:T(8,128)(2,1)S(1)}, u32[]{:S(2)}, u32[]{:S(2)}) collective-permute-start(bf16[16,1664]{1,0:T(8,128)(2,1)} %get-tuple-element.169.refs_0_), channel_id=1, source_target_pairs={{0,8},{1,9},{2,10},{3,11},{4,12},{5,13},{6,14},{7,15},{8,0},{9,1},... | collective-permute-start | bytes 159752 | tf_op jit(solution)/shard_map/ppermute | solution.py:79
  14.9 12.7 %collective-permute-start.8 = (bf16[16,4864]{1,0:T(8,128)(2,1)}, bf16[16,4864]{1,0:T(8,128)(2,1)S(1)}, u32[]{:S(2)}, u32[]{:S(2)}) collective-permute-start(bf16[16,4864]{1,0:T(8,128)(2,1)} %get-tuple-element.183.refs_0_), channel_id=1, source_target_pairs={{0,16},{1,17},{2,18},{3,19},{4,20},{5,21},{6,22},{7,23},{8,24},{9,... | collective-permute-start | bytes 466952 | tf_op jit(solution)/shard_map/ppermute | solution.py:79
  21.7 10.3 %collective-permute-start.4 = (bf16[64,1664]{1,0:T(8,128)(2,1)S(1)}, bf16[64,1664]{1,0:T(8,128)(2,1)S(1)}, u32[]{:S(2)}, u32[]{:S(2)}) collective-permute-start(bf16[64,1664]{1,0:T(8,128)(2,1)S(1)} %join_rows.8.refs_0_), channel_id=1, source_target_pairs={{0,2},{1,3},{2,0},{3,1},{4,6},{5,7},{6,4},{7,5},{8,10},{9,11},{10,... | collective-permute-start | bytes 638984 | tf_op jit(solution)/shard_map/ppermute | solution.py:79
  24.8 9.7 %collective-permute-start.6 = (bf16[64,1664]{1,0:T(8,128)(2,1)S(1)}, bf16[64,1664]{1,0:T(8,128)(2,1)S(1)}, u32[]{:S(2)}, u32[]{:S(2)}) collective-permute-start(bf16[64,1664]{1,0:T(8,128)(2,1)S(1)} %join_rows.8.refs_0_), channel_id=1, source_target_pairs={{0,6},{1,7},{2,4},{3,5},{4,2},{5,3},{6,0},{7,1},{8,14},{9,15},{10,... | collective-permute-start | bytes 638984 | tf_op jit(solution)/shard_map/ppermute | solution.py:79
  27.7 11.6 %collective-permute-start.9 = (bf16[32,4864]{1,0:T(8,128)(2,1)S(1)}, bf16[32,4864]{1,0:T(8,128)(2,1)S(1)}, u32[]{:S(2)}, u32[]{:S(2)}) collective-permute-start(bf16[32,4864]{1,0:T(8,128)(2,1)S(1)} %join_rows.10.refs_0_), channel_id=1, source_target_pairs={{0,8},{1,9},{2,10},{3,11},{4,12},{5,13},{6,14},{7,15},{8,0},{9,1},... | collective-permute-start | bytes 933896 | tf_op jit(solution)/shard_map/ppermute | solution.py:79
  39.3 14.3 %collective-permute-start.11 = (bf16[64,2816]{1,0:T(8,128)(2,1)S(1)}, bf16[64,2816]{1,0:T(8,128)(2,1)S(1)}, u32[]{:S(2)}, u32[]{:S(2)}) collective-permute-start(bf16[64,2816]{1,0:T(8,128)(2,1)S(1)} %get-tuple-element.187.refs_0_), channel_id=1, source_target_pairs={{0,2},{1,3},{2,0},{3,1},{4,6},{5,7},{6,4},{7,5},{8,10},{9,11},{10,... | collective-permute-start | bytes 1081352 | tf_op jit(solution)/shard_map/ppermute | solution.py:79
  40.9 12.2 %collective-permute-start.10 = (bf16[64,2048]{1,0:T(8,128)(2,1)S(1)}, bf16[64,2048]{1,0:T(8,128)(2,1)S(1)}, u32[]{:S(2)}, u32[]{:S(2)}) collective-permute-start(bf16[64,2048]{1,0:T(8,128)(2,1)S(1)} %get-tuple-element.186.refs_0_), channel_id=1, source_target_pairs={{0,4},{1,5},{2,6},{3,7},{4,0},{5,1},{6,2},{7,3},{8,12},{9,13},{10,... | collective-permute-start | bytes 786440 | tf_op jit(solution)/shard_map/ppermute | solution.py:79
  53.6 21.4 %collective-permute-start.13 = (bf16[128,2816]{1,0:T(8,128)(2,1)S(1)}, bf16[128,2816]{1,0:T(8,128)(2,1)S(1)}, u32[]{:S(2)}, u32[]{:S(2)}) collective-permute-start(bf16[128,2816]{1,0:T(8,128)(2,1)S(1)} %join_rows.13.refs_0_), channel_id=1, source_target_pairs={{0,4},{1,5},{2,6},{3,7},{4,0},{5,1},{6,2},{7,3},{8,12},{9,13},{10,... | collective-permute-start | bytes 2162696 | tf_op jit(solution)/shard_map/ppermute | solution.py:79
  55.3 18.2 %collective-permute-start.12 = (bf16[128,2048]{1,0:T(8,128)(2,1)S(1)}, bf16[128,2048]{1,0:T(8,128)(2,1)S(1)}, u32[]{:S(2)}, u32[]{:S(2)}) collective-permute-start(bf16[128,2048]{1,0:T(8,128)(2,1)S(1)} %join_rows.12.refs_0_), channel_id=1, source_target_pairs={{0,2},{1,3},{2,0},{3,1},{4,6},{5,7},{6,4},{7,5},{8,10},{9,11},{10,... | collective-permute-start | bytes 1572872 | tf_op jit(solution)/shard_map/ppermute | solution.py:79
  132.1 27.0 %collective-permute-start.18 = (bf16[4,512,256]{2,1,0:T(8,128)(2,1)}, bf16[4,512,256]{2,1,0:T(8,128)(2,1)S(1)}, u32[]{:S(2)}, u32[]{:S(2)}) collective-permute-start(bf16[4,512,256]{2,1,0:T(8,128)(2,1)} %get-tuple-element.218), channel_id=1, source_target_pairs={{0,2},{1,3},{2,0},{3,1},{4,6},{5,7},{6,4},{7,5},{8,10},{9,11},{10,... | collective-permute-start | bytes 3145736 | tf_op jit(solution)/shard_map/ppermute | solution.py:79
  134.6 25.3 %collective-permute-start.19 = (bf16[4,512,256]{2,1,0:T(8,128)(2,1)}, bf16[4,512,256]{2,1,0:T(8,128)(2,1)S(1)}, u32[]{:S(2)}, u32[]{:S(2)}) collective-permute-start(bf16[4,512,256]{2,1,0:T(8,128)(2,1)} %get-tuple-element.219), channel_id=1, source_target_pairs={{0,4},{1,5},{2,6},{3,7},{4,0},{5,1},{6,2},{7,3},{8,12},{9,13},{10,... | collective-permute-start | bytes 3145736 | tf_op jit(solution)/shard_map/ppermute | solution.py:79
  160.5 15.3 %collective-permute-start.22 = (bf16[4,256,256]{2,1,0:T(8,128)(2,1)S(1)}, bf16[4,256,256]{2,1,0:T(8,128)(2,1)S(1)}, u32[]{:S(2)}, u32[]{:S(2)}) collective-permute-start(bf16[4,256,256]{2,1,0:T(8,128)(2,1)S(1)} %get-tuple-element.238), channel_id=1, source_target_pairs={{0,4},{1,5},{2,6},{3,7},{4,0},{5,1},{6,2},{7,3},{8,12},{9,13},{10,... | collective-permute-start | bytes 1572872 | tf_op jit(solution)/shard_map/ppermute | solution.py:79
  162.3 14.9 %collective-permute-start.23 = (bf16[4,256,256]{2,1,0:T(8,128)(2,1)S(1)}, bf16[4,256,256]{2,1,0:T(8,128)(2,1)S(1)}, u32[]{:S(2)}, u32[]{:S(2)}) collective-permute-start(bf16[4,256,256]{2,1,0:T(8,128)(2,1)S(1)} %get-tuple-element.239), channel_id=1, source_target_pairs={{0,2},{1,3},{2,0},{3,1},{4,6},{5,7},{6,4},{7,5},{8,10},{9,11},{10,... | collective-permute-start | bytes 1572872 | tf_op jit(solution)/shard_map/ppermute | solution.py:79
  168.5 22.3 %collective-permute-start.26 = (bf16[1,128,2432]{2,1,0:T(8,128)(2,1)S(1)}, bf16[1,128,2432]{2,1,0:T(8,128)(2,1)S(1)}, u32[]{:S(2)}, u32[]{:S(2)}) collective-permute-start(bf16[1,128,2432]{2,1,0:T(8,128)(2,1)S(1)} %get-tuple-element.251), channel_id=1, source_target_pairs={{0,4},{1,5},{2,6},{3,7},{4,0},{5,1},{6,2},{7,3},{8,12},{9,13},{10,... | collective-permute-start | bytes 1867784 | tf_op jit(solution)/shard_map/ppermute | solution.py:79
  169.6 21.2 %collective-permute-start.25 = (bf16[1,128,2432]{2,1,0:T(8,128)(2,1)S(1)}, bf16[1,128,2432]{2,1,0:T(8,128)(2,1)S(1)}, u32[]{:S(2)}, u32[]{:S(2)}) collective-permute-start(bf16[1,128,2432]{2,1,0:T(8,128)(2,1)S(1)} %get-tuple-element.250), channel_id=1, source_target_pairs={{0,2},{1,3},{2,0},{3,1},{4,6},{5,7},{6,4},{7,5},{8,10},{9,11},{10,... | collective-permute-start | bytes 1867784 | tf_op jit(solution)/shard_map/ppermute | solution.py:79
  177.5 13.3 %collective-permute-start.24 = (bf16[8,128,256]{2,1,0:T(8,128)(2,1)S(1)}, bf16[8,128,256]{2,1,0:T(8,128)(2,1)S(1)}, u32[]{:S(2)}, u32[]{:S(2)}) collective-permute-start(bf16[8,128,256]{2,1,0:T(8,128)(2,1)S(1)} %get-tuple-element.249), channel_id=1, source_target_pairs={{0,8},{1,9},{2,10},{3,11},{4,12},{5,13},{6,14},{7,15},{8,0},{9,1},... | collective-permute-start | bytes 1572872 | tf_op jit(solution)/shard_map/ppermute | solution.py:79
  180.5 12.4 %collective-permute-start.27 = (bf16[512,512]{1,0:T(8,128)(2,1)S(1)}, bf16[512,512]{1,0:T(8,128)(2,1)S(1)}, u32[]{:S(2)}, u32[]{:S(2)}) collective-permute-start(bf16[512,512]{1,0:T(8,128)(2,1)S(1)} %get-tuple-element.260), channel_id=1, source_target_pairs={{1,0},{2,1},{3,2},{5,4},{6,5},{7,6},{9,8},{10,9},{11,10},{13,12},{... | collective-permute-start | bytes 1572872 | tf_op jit(solution)/shard_map/ppermute | solution.py:1209
  191.1 15.4 %collective-permute-start.28 = (bf16[8,64,256]{2,1,0:T(8,128)(2,1)S(1)}, bf16[8,64,256]{2,1,0:T(8,128)(2,1)S(1)}, u32[]{:S(2)}, u32[]{:S(2)}) collective-permute-start(bf16[8,64,256]{2,1,0:T(8,128)(2,1)S(1)} %get-tuple-element.265), channel_id=1, source_target_pairs={{0,16},{1,17},{2,18},{3,19},{4,20},{5,21},{6,22},{7,23},{8,24},{9,... | collective-permute-start | bytes 786440 | tf_op jit(solution)/shard_map/ppermute | solution.py:79
  191.4 15.8 %collective-permute-start.30 = (bf16[1,64,2432]{2,1,0:T(8,128)(2,1)S(1)}, bf16[1,64,2432]{2,1,0:T(8,128)(2,1)S(1)}, u32[]{:S(2)}, u32[]{:S(2)}) collective-permute-start(bf16[1,64,2432]{2,1,0:T(8,128)(2,1)S(1)} %get-tuple-element.270), channel_id=1, source_target_pairs={{0,2},{1,3},{2,0},{3,1},{4,6},{5,7},{6,4},{7,5},{8,10},{9,11},{10,... | collective-permute-start | bytes 933896 | tf_op jit(solution)/shard_map/ppermute | solution.py:79
  192.4 14.8 %collective-permute-start.29 = (bf16[1,64,2432]{2,1,0:T(8,128)(2,1)S(1)}, bf16[1,64,2432]{2,1,0:T(8,128)(2,1)S(1)}, u32[]{:S(2)}, u32[]{:S(2)}) collective-permute-start(bf16[1,64,2432]{2,1,0:T(8,128)(2,1)S(1)} %get-tuple-element.269), channel_id=1, source_target_pairs={{0,4},{1,5},{2,6},{3,7},{4,0},{5,1},{6,2},{7,3},{8,12},{9,13},{10,... | collective-permute-start | bytes 933896 | tf_op jit(solution)/shard_map/ppermute | solution.py:79
  207.3 9.4 %collective-permute-start.31 = (bf16[1,32,4864]{2,1,0:T(8,128)(2,1)S(1)}, bf16[1,32,4864]{2,1,0:T(8,128)(2,1)S(1)}, u32[]{:S(2)}, u32[]{:S(2)}) collective-permute-start(bf16[1,32,4864]{2,1,0:T(8,128)(2,1)S(1)} %get-tuple-element.275), channel_id=1, source_target_pairs={{0,8},{1,9},{2,10},{3,11},{4,12},{5,13},{6,14},{7,15},{8,0},{9,1},... | collective-permute-start | bytes 933896 | tf_op jit(solution)/shard_map/ppermute | solution.py:79
  208.6 13.0 %collective-permute-start.37 = (bf16[1,64,1792]{2,1,0:T(8,128)(2,1)S(1)}, bf16[1,64,1792]{2,1,0:T(8,128)(2,1)S(1)}, u32[]{:S(2)}, u32[]{:S(2)}) collective-permute-start(bf16[1,64,1792]{2,1,0:T(8,128)(2,1)S(1)} %get-tuple-element.286), channel_id=1, source_target_pairs={{0,6},{1,7},{2,4},{3,5},{4,2},{5,3},{6,0},{7,1},{8,14},{9,15},{10,... | collective-permute-start | bytes 688136 | tf_op jit(solution)/shard_map/ppermute | solution.py:79
  217.0 13.5 %collective-permute-start.32 = (bf16[1,16,4864]{2,1,0:T(8,128)(2,1)S(1)}, bf16[1,16,4864]{2,1,0:T(8,128)(2,1)S(1)}, u32[]{:S(2)}, u32[]{:S(2)}) collective-permute-start(bf16[1,16,4864]{2,1,0:T(8,128)(2,1)S(1)} %get-tuple-element.277), channel_id=1, source_target_pairs={{0,16},{1,17},{2,18},{3,19},{4,20},{5,21},{6,22},{7,23},{8,24},{9,... | collective-permute-start | bytes 466952 | tf_op jit(solution)/shard_map/ppermute | solution.py:79
  (66 other events, 818.3 us)
Sparse Core Ops, SparseCore 0:
  11.5 88.9 all-gather.1

commit v3 on v2

--- a/solution.py
+++ b/solution.py
@@ -312,23 +312,24 @@
             out_ref[:, left : left + 128] = dot(spread, joined).astype(bf16)
 
 
-def pack_rows(starts_ref, rowmap_ref, work_ref, outs):
-    size, columns = work_ref.shape
-    half = size // 2
-    count = starts_ref.shape[0]
+def store_flipped(dests_ref, rowmap_ref, block, out_ref, lanes):
+    flipped = flip(block)
+    size = flipped.shape[0]
+    count = dests_ref.shape[0]
     rows = size // count
     if rows % 16 == 0:
-        for place in range(count):
-            start = pl.multiple_of(starts_ref[place], rows)
-            out, inner = outs[place * rows // half], place * rows % half
-            out[0, inner : inner + rows, :] = work_ref[pl.ds(start, rows), :]
+        for index in range(count):
+            start = pl.multiple_of(dests_ref[index], rows)
+            out_ref[pl.ds(start, rows), lanes] = flipped[index * rows : (index + 1) * rows]
     else:
         spread = one_hot_rows(rowmap_ref[0:1, :], size)
-        for left in range(0, columns, 128):
-            lanes = slice(left, left + 128)
-            joined = dot(spread, work_ref[:, lanes], ((0,), (0,))).astype(bf16)
-            for index, out in enumerate(outs):
-                out[0, :, lanes] = joined[index * half : (index + 1) * half]
+        out_ref[:, lanes] = dot(spread, flipped, ((0,), (0,))).astype(bf16)
+
+
+def store_halves(values, keep, send, lanes):
+    half = keep.shape[1]
+    keep[0, :, lanes] = values[:half].astype(bf16)
+    send[0, :, lanes] = values[half:].astype(bf16)
 
 
 def centre_rows(values):
@@ -472,37 +473,32 @@
             jax.ShapeDtypeStruct((8, width), f32),
             jax.ShapeDtypeStruct((width, columns), bf16),
         ],
-        compiler_params=params(48),
+        compiler_params=params(32),
         cost_estimate=cost(4, 8),
         name="project_rows",
     )(starts, rowmap, halo, inputs, *pieces, cosine, sine)
 
 
-def attend_kernel(q, k, v, bias, mixed, logsum, v_flipped):
+def attend_kernel(q, k, v, bias, mixed, logsum):
     step = pl.program_id(0)
-    pairs = q.shape[1] // 128
-
-    @pl.when(step == 0)
-    def _():
-        for pair in range(pairs):
-            lanes = slice(pair * 128, (pair + 1) * 128)
-            v_flipped[lanes, :] = flip(v[:, lanes])
-
     start = pl.multiple_of(step * QROWS, QROWS)
+    keys = pl.ds(start, SPAN)
     allowed = jnp.concatenate([bias[0], bias[0]], axis=1)
+    lane = lax.broadcasted_iota(jnp.int32, (QROWS, 128), 1)
+    pairs = [slice(left, left + 128) for left in range(0, q.shape[1], 128)]
+    columns = [head_columns(flip(q[:, lanes])) for lanes in pairs]
+    scores = [dot(k[keys, lanes], column) + allowed for lanes, column in zip(pairs, columns)]
+    highest = [jnp.max(score, axis=0, keepdims=True) for score in scores]
+    raised = [jnp.exp(score - high) for score, high in zip(scores, highest)]
+    totals = [column_sum(part) for part in raised]
+    weights = [(part * (1.0 / total)).astype(bf16) for part, total in zip(raised, totals)]
+    outputs = [
+        dot(weight, v[keys, lanes], ((0,), (0,))) for weight, lanes in zip(weights, pairs)
+    ]
     rows = []
-    for pair in range(pairs):
-        lanes = slice(pair * 128, (pair + 1) * 128)
-        columns = head_columns(flip(q[:, lanes]))
-        scores = dot(k[pl.ds(start, SPAN), lanes], columns) + allowed
-        highest = jnp.max(scores, axis=0, keepdims=True)
-        raised = jnp.exp(scores - highest)
-        total = column_sum(raised)
-        joined = dot(v_flipped[lanes, pl.ds(start, SPAN)], raised.astype(bf16))
-        joined = joined * (1.0 / total)
-        output = jnp.concatenate([joined[:64, :QROWS], joined[64:, QROWS:]], axis=0)
-        mixed[:, lanes] = output.T.astype(bf16)
-        record = highest + jnp.log(total)
+    for lanes, output, high, total in zip(pairs, outputs, highest, totals):
+        mixed[:, lanes] = jnp.where(lane < 64, output[:QROWS], output[QROWS:]).astype(bf16)
+        record = high + jnp.log(total)
         rows += [record[:, :QROWS], record[:, QROWS:]]
     logsum[...] = jnp.concatenate(rows, axis=0)
 
@@ -526,8 +522,7 @@
             jax.ShapeDtypeStruct((count, width), bf16),
             jax.ShapeDtypeStruct((HEADS, count), f32),
         ],
-        scratch_shapes=[pltpu.VMEM((width, k.shape[0]), bf16)],
-        compiler_params=params(40),
+        compiler_params=params(24),
         cost_estimate=cost(4, 14),
         name="attend_rows",
     )(q, k, v, bias)
@@ -550,23 +545,22 @@
     proj = 2 * units
     last = proj + latent.shape[1]
     first = dot(mixed[...], weights[:, last : last + width])
-    branch_first[...] = first
+    branch_first[...] = first.astype(bf16)
     after = inputs[...].astype(f32) + scales[4:5, :] * first
     after_first[...] = after
     normal, _ = centre_rows(after)
     low = (normal * scales[2:3, :] + scales[3:4, :]).astype(bf16)
     normed[...] = low
-    second = jnp.zeros(after.shape, f32)
     chunk = 512
-    for left in range(0, units, chunk):
-        pre = dot(low, weights[:, up + left : up + left + chunk])
+    lefts = range(0, units, chunk)
+    pres = [dot(low, weights[:, up + left : up + left + chunk]) for left in lefts]
+    for left, pre in zip(lefts, pres):
         share = 0.5 + 0.5 * lax.erf(pre * (1.0 / math.sqrt(2.0)))
         bell = jnp.exp(-0.5 * pre * pre) * (1.0 / math.sqrt(2.0 * math.pi))
-        part = (pre * share).astype(bf16)
-        hidden[:, left : left + chunk] = part
+        hidden[:, left : left + chunk] = (pre * share).astype(bf16)
         slope[:, left : left + chunk] = (share + pre * bell).astype(bf16)
-        second = second + dot_nt(part, weights[:, down + left : down + left + chunk])
-    branch_second[...] = second
+    second = dot_nt(hidden[...], weights[:, down : down + units])
+    branch_second[...] = second.astype(bf16)
     rounded = (after + scales[5:6, :] * second).astype(bf16)
     low_out[...] = rounded
     latent[...] = dot(rounded, weights[:, proj:last])
@@ -576,8 +570,8 @@
     count, width = inputs.shape
     columns = pieces[0].shape[1] + pieces[2].shape[1]
     row = lambda size: pl.BlockSpec((ROWS, size), lambda i: (i, 0))
-    kept = ((width, f32), (width, f32), (width, bf16), (units, bf16), (units, bf16),
-            (width, f32), (width, bf16), (depth, f32))
+    kept = ((width, bf16), (width, f32), (width, bf16), (units, bf16), (units, bf16),
+            (width, bf16), (width, bf16), (depth, f32))
     (starts_a, rowmap_a), (starts_b, rowmap_b) = orders
     return pl.pallas_call(
         forward_kernel,
@@ -602,20 +596,23 @@
     @pl.when(level == 0)
     def _():
         residue[...] = latent[...]
-        columns[...] = codes[...].astype(f32).T
+        columns[...] = codes[:LEVELS, :].astype(f32).T
 
     factor = jnp.where(level < active[0], 1.0, 0.0).astype(f32)
     lane = lax.broadcasted_iota(jnp.int32, (ROWS, LEVELS), 1)
     place = lax.broadcasted_iota(jnp.int32, (ROWS, 256), 1).astype(f32)
-    for top in range(0, count, ROWS):
-        rows = slice(top, top + ROWS)
+    blocks = [slice(top, top + ROWS) for top in range(0, count, ROWS)]
+    picked = []
+    for rows in blocks:
         code = jnp.where(lane == level, columns[rows, :], 0.0)
         code = jnp.sum(code, axis=1, keepdims=True)
         high = jnp.floor(code * (1.0 / 256.0))
         hit = jnp.where(place == code - 256.0 * high, 1.0, 0.0).astype(bf16)
         picks = [hit * jnp.where(high == j, 1.0, 0.0).astype(bf16) for j in range(tiles)]
-        found = dot(jnp.concatenate(picks, axis=1), book[0])
-        left = residue[rows, :] - factor * found
+        picked.append(jnp.concatenate(picks, axis=1))
+    found = [dot(pick, book[0]) for pick in picked]
+    for rows, row in zip(blocks, found):
+        left = residue[rows, :] - factor * row
         residue[rows, :] = left
         steps[level, rows, :] = factor * left
 
@@ -626,8 +623,7 @@
             total = jnp.zeros((ROWS, depth), f32)
             for index in reversed(range(LEVELS)):
                 total = total + steps[index, rows, :]
-                live = jnp.where(index < active[0], 1.0, 0.0).astype(f32)
-                carried[index, rows, :] = (live * total).astype(bf16)
+                carried[index, rows, :] = total.astype(bf16)
 
 
 def fetch_call(active, codes, latent, book):
@@ -656,10 +652,10 @@
 
 
 def spread_kernel(first, codes, carried, keep, send):
-    level = pl.program_id(0) + first
     count = carried.shape[1]
     half = keep.shape[1]
-    code = codes[pl.ds(level, 1), :]
+    level = pl.program_id(0) + first
+    code = codes[pl.ds(LEVELS + level, 1), :]
     high = code >> 8
     place = lax.broadcasted_iota(jnp.int32, (256, count), 0)
     hit = jnp.where(place == (code & 255), -1.0, 0.0).astype(bf16)
@@ -688,10 +684,10 @@
 
 
 def backward_kernel(
-    starts_a, rowmap_a, starts_b, rowmap_b, carried, branch_second, slope, after_first, branch_first, normed, hidden, low_out, mixed,
+    dests_a, rowmap_a, dests_b, rowmap_b, carried, branch_second, slope, after_first, branch_first, normed, hidden, low_out, mixed,
     scales, weights,
     out_after, out_mixed, sums, keep_a, send_a, keep_b, send_b,
-    work, grad_pre, kept_hidden, kept_carried, grad_branch, flipped,
+    grad_pre, kept_hidden, kept_carried, grad_branch, flipped,
 ):
     step = pl.program_id(0)
     last_step = pl.num_programs(0) - 1
@@ -707,7 +703,7 @@
         sums[...] = jnp.zeros(sums.shape, f32)
 
     grad_after = dot_nt(carried[0], weights[:, proj:last])
-    sums[5:6, :] += column_sum(grad_after * branch_second[...])
+    sums[5:6, :] += column_sum(grad_after * branch_second[...].astype(f32))
     low = (grad_after * scales[5:6, :]).astype(bf16)
     grad_normed = jnp.zeros(grad_after.shape, f32)
     for left in range(0, units, chunk):
@@ -720,29 +716,27 @@
     sums[3:4, :] += column_sum(grad_normed)
     grad_first = grad_after + norm_back(normal, rstd, scales[2:3, :], grad_normed)
     out_after[...] = grad_first
-    sums[4:5, :] += column_sum(grad_first * branch_first[...])
+    sums[4:5, :] += column_sum(grad_first * branch_first[...].astype(f32))
     low_first = (grad_first * scales[4:5, :]).astype(bf16)
     grad_branch[rows, :] = low_first
     out_mixed[...] = dot_nt(low_first, weights[:, last : last + width]).astype(bf16)
     kept_hidden[rows, :] = hidden[...]
     kept_carried[rows, :] = carried[0]
-    for index, block in enumerate((normed[...], low, low_out[...], mixed[...])):
-        flipped[index, :, rows] = flip(block)
+    for index, block in enumerate((normed[...], low_out[...])):
+        store_flipped(dests_a, rowmap_a, block, flipped.at[index], rows)
+    for index, block in enumerate((low, mixed[...])):
+        store_flipped(dests_b, rowmap_b, block, flipped.at[2 + index], rows)
 
     @pl.when(step == last_step)
     def _():
         for left in range(0, units, chunk):
             lanes = slice(left, left + chunk)
-            work[:, lanes] = dot(flipped[0], grad_pre[:, lanes]).astype(bf16)
-            lanes = slice(left, left + chunk)
-            work[:, units + left : units + left + chunk] = dot(
-                flipped[1], kept_hidden[:, lanes]
-            ).astype(bf16)
-        work[:, proj:last] = dot(flipped[2], kept_carried[...]).astype(bf16)
-        work[:, last:] = dot(flipped[3], grad_branch[...]).astype(bf16)
-        half = keep_a.shape[2]
-        pack_rows(starts_a, rowmap_a, work.at[:, :half], (keep_a, send_a))
-        pack_rows(starts_b, rowmap_b, work.at[:, half:], (keep_b, send_b))
+            store_halves(dot(flipped[0], grad_pre[:, lanes]), keep_a, send_a, lanes)
+            store_halves(dot(flipped[2], kept_hidden[:, lanes]), keep_b, send_b, lanes)
+        rest = slice(units, keep_a.shape[2])
+        store_halves(dot(flipped[1], kept_carried[...]), keep_a, send_a, rest)
+        rest = slice(units, keep_b.shape[2])
+        store_halves(dot(flipped[3], grad_branch[...]), keep_b, send_b, rest)
 
 
 def backward_call(
@@ -751,10 +745,9 @@
 ):
     count, width = after_first.shape
     units, depth = slope.shape[1], carried.shape[2]
-    columns = weights.shape[1]
     row = lambda size: pl.BlockSpec((ROWS, size), lambda i: (i, 0))
-    piece = (1, width // 2, columns // 2)
-    (starts_a, rowmap_a), (starts_b, rowmap_b) = orders
+    pieces = [(1, width // 2, units + extra) for extra in (depth, depth, width, width)]
+    (_, rowmap_a, dests_a), (_, rowmap_b, dests_b) = orders
     return pl.pallas_call(
         backward_kernel,
         grid=(count // ROWS,),
@@ -762,15 +755,14 @@
         + [pl.BlockSpec((1, ROWS, depth), lambda i: (0, i, 0))]
         + [row(width), row(units), row(width), row(width), row(width), row(units), row(width)]
         + [row(width), whole(scales.shape), whole(weights.shape)],
-        out_specs=[row(width), row(width), whole((8, width))] + [whole(piece)] * 4,
+        out_specs=[row(width), row(width), whole((8, width))] + [whole(piece) for piece in pieces],
         out_shape=[
             jax.ShapeDtypeStruct((count, width), f32),
             jax.ShapeDtypeStruct((count, width), bf16),
             jax.ShapeDtypeStruct((8, width), f32),
         ]
-        + [jax.ShapeDtypeStruct(piece, bf16)] * 4,
+        + [jax.ShapeDtypeStruct(piece, bf16) for piece in pieces],
         scratch_shapes=[
-            pltpu.VMEM((width, columns), bf16),
             pltpu.VMEM((count, units), bf16),
             pltpu.VMEM((count, units), bf16),
             pltpu.VMEM((count, depth), bf16),
@@ -781,7 +773,7 @@
         cost_estimate=cost(2, 25),
         name="feed_back",
     )(
-        starts_a, rowmap_a, starts_b, rowmap_b, carried, branch_second, slope, after_first, branch_first, normed, hidden,
+        dests_a, rowmap_a, dests_b, rowmap_b, carried, branch_second, slope, after_first, branch_first, normed, hidden,
         low_out, mixed, scales, weights,
     )
 
@@ -789,9 +781,8 @@
 def attend_back_kernel(pieces, *refs):
     k_refs, v_refs = refs[:pieces], refs[pieces : 2 * pieces]
     (q, grad, logsum, bias, cosine, sine, start_k, start_v,
-     grad_q, grad_k, grad_v, halo, k, v, k_flipped) = refs[2 * pieces :]
+     grad_q, grad_k, grad_v, halo, k, v) = refs[2 * pieces :]
     step = pl.program_id(0)
-    pairs = q.shape[1] // 128
 
     @pl.when(step == 0)
     def _():
@@ -799,9 +790,6 @@
             rows = slice(index * MARGIN, (index + 1) * MARGIN)
             k[rows, :] = k_refs[index][...]
             v[rows, :] = v_refs[index][...]
-            for pair in range(pairs):
-                lanes = slice(pair * 128, (pair + 1) * 128)
-                k_flipped[lanes, rows] = flip(k_refs[index][:, lanes])
         grad_k[:MARGIN, :] = start_k[...]
         grad_v[:MARGIN, :] = start_v[...]
         grad_k[MARGIN:, :] = jnp.zeros_like(grad_k[MARGIN:, :])
@@ -810,21 +798,30 @@
     start = pl.multiple_of(step * QROWS, QROWS)
     keys = pl.ds(start, SPAN)
     allowed = jnp.concatenate([bias[0], bias[0]], axis=1)
+    lane = lax.broadcasted_iota(jnp.int32, (QROWS, 128), 1)
+    pairs = [slice(left, left + 128) for left in range(0, q.shape[1], 128)]
+    records = [
+        jnp.concatenate([logsum[h : h + 1, :], logsum[h + 1 : h + 2, :]], axis=1)
+        for h in range(0, HEADS, 2)
+    ]
+    scores = [dot(k[keys, lanes], head_columns(flip(q[:, lanes]))) + allowed for lanes in pairs]
+    grads = [dot(v[keys, lanes], head_columns(flip(grad[:, lanes]))) for lanes in pairs]
+    weights = [jnp.exp(score - record) for score, record in zip(scores, records)]
+    products = [weight * part for weight, part in zip(weights, grads)]
+    inners = [column_sum(product) for product in products]
+    grad_scores = [
+        (product - weight * inner).astype(bf16)
+        for product, weight, inner in zip(products, weights, inners)
+    ]
+    low = [weight.astype(bf16) for weight in weights]
+    for lanes, weight in zip(pairs, low):
+        grad_v[keys, lanes] += dot(weight, head_rows(grad[:, lanes]))
+    for lanes, part in zip(pairs, grad_scores):
+        grad_k[keys, lanes] += dot(part, head_rows(q[:, lanes]))
+    joined = [dot(part, k[keys, lanes], ((0,), (0,))) for lanes, part in zip(pairs, grad_scores)]
     back = -sine[...]
-    for pair in range(pairs):
-        lanes = slice(pair * 128, (pair + 1) * 128)
-        heads = (2 * pair, 2 * pair + 1)
-        record = jnp.concatenate([logsum[h : h + 1, :] for h in heads], axis=1)
-        scores = dot(k[keys, lanes], head_columns(flip(q[:, lanes]))) + allowed
-        weights = jnp.exp(scores - record)
-        grad_weights = dot(v[keys, lanes], head_columns(flip(grad[:, lanes])))
-        product = weights * grad_weights
-        inner = column_sum(product)
-        grad_scores = (product - weights * inner).astype(bf16)
-        grad_v[keys, lanes] += dot(weights.astype(bf16), head_rows(grad[:, lanes]))
-        grad_k[keys, lanes] += dot(grad_scores, head_rows(q[:, lanes]))
-        joined = dot(k_flipped[lanes, keys], grad_scores)
-        flat = jnp.concatenate([joined[:64, :QROWS], joined[64:, QROWS:]], axis=0).T * 0.125
+    for lanes, part in zip(pairs, joined):
+        flat = jnp.where(lane < 64, part[:QROWS], part[QROWS:]) * 0.125
         grad_q[:, lanes] = turn(flat, cosine[...], back).astype(bf16)
 
     @pl.when(step == pl.num_programs(0) - 1)
@@ -870,7 +867,6 @@
         scratch_shapes=[
             pltpu.VMEM((keys, width), bf16),
             pltpu.VMEM((keys, width), bf16),
-            pltpu.VMEM((width, keys), bf16),
         ],
         compiler_params=params(20),
         cost_estimate=cost(0 if offset > 0 else 8, 2 * blocks),
@@ -879,13 +875,13 @@
 
 
 def finish_kernel(
-    starts, rowmap, inputs, normed, q_a, q_b, q_c, k_a, k_b, v_a, v_b, halo, cosine, sine,
+    dests, rowmap, inputs, normed, q_a, q_b, q_c, k_a, k_b, v_a, v_b, halo, cosine, sine,
     grad_after, scales, sums_second, weights,
-    out, keep_a, send_a, keep_b, send_b, work, turned_q, turned_k, turned_v, sums,
+    out, keep_a, send_a, keep_b, send_b, flipped, turned_q, turned_k, turned_v, sums, tail,
 ):
     step = pl.program_id(0)
     last = pl.num_programs(0) - 1
-    count, width = normed.shape
+    width = normed.shape[1]
 
     @pl.when(step == 0)
     def _():
@@ -912,23 +908,25 @@
     sums[1:2, :] += column_sum(grad)
     out[...] = grad_after[...] + norm_back(normal, rstd, scales[0:1, :], grad)
 
+    store_flipped(dests, rowmap, normed[...], flipped, rows)
+
     @pl.when(step == last)
     def _():
-        flipped = flip(normed[...])
-        for index, turned_ref in enumerate((turned_q, turned_k, turned_v)):
-            lanes = slice(index * width, (index + 1) * width)
-            work[:, lanes] = dot(flipped, turned_ref[...]).astype(bf16)
-        work[:, 3 * width :] = sums[...].T.astype(bf16)
-        half = keep_a.shape[2]
-        pack_rows(starts, rowmap, work.at[:, :half], (keep_a, send_a))
-        pack_rows(starts, rowmap, work.at[:, half:], (keep_b, send_b))
+        store_flipped(dests, rowmap, sums[...], tail, slice(None))
+        parts = [dot(flipped[...], ref[...]).astype(bf16) for ref in (turned_q, turned_k, turned_v)]
+        joined = jnp.concatenate(parts + [tail[...]], axis=1)
+        split = keep_a.shape[2]
+        half = keep_a.shape[1]
+        keep_a[0], send_a[0] = joined[:half, :split], joined[half:, :split]
+        keep_b[0], send_b[0] = joined[:half, split:], joined[half:, split:]
 
 
 def finish_call(
-    starts, rowmap, inputs, normed, grad_q, grad_k, grad_v, halo, cosine, sine,
+    order, inputs, normed, grad_q, grad_k, grad_v, halo, cosine, sine,
     grad_after, scales, sums_second, weights,
 ):
     count, width = normed.shape
+    _, rowmap, dests = order
     columns = 3 * width + 256
     row = pl.BlockSpec((ROWS, width), lambda i: (i, 0))
     first = pl.BlockSpec((ROWS, width), lambda i: (0, 0))
@@ -942,7 +940,7 @@
     return pl.pallas_call(
         finish_kernel,
         grid=(count // ROWS,),
-        in_specs=[smem(), whole(rowmap.shape), row, whole(normed.shape)]
+        in_specs=[smem(), whole(rowmap.shape), row, row]
         + [whole(piece.shape) for piece in grad_q]
         + [first, rest, first, rest]
         + [whole(halo.shape), table, table, row]
@@ -950,17 +948,18 @@
         out_specs=[row] + [whole(shape.shape) for shape in shapes[1:]],
         out_shape=shapes,
         scratch_shapes=[
-            pltpu.VMEM((width, columns), bf16),
+            pltpu.VMEM((width, count), bf16),
             pltpu.VMEM((count, width), bf16),
             pltpu.VMEM((count, width), bf16),
             pltpu.VMEM((count, width), bf16),
             pltpu.VMEM((256, width), f32),
+            pltpu.VMEM((width, 256), bf16),
         ],
         compiler_params=params(32),
         cost_estimate=cost(0, 10),
         name="finish_rows",
     )(
-        starts, rowmap, inputs, normed, *grad_q, *grad_k, *grad_v, halo, cosine, sine,
+        dests, rowmap, inputs, normed, *grad_q, *grad_k, *grad_v, halo, cosine, sine,
         grad_after, scales, sums_second, weights,
     )
 
@@ -1055,10 +1054,11 @@
     depth = masters[2].shape[1]
     for k in range(3):
         update(0, k, grad_qkv[:, k * width : (k + 1) * width])
-    update(0, 3, grad_feed[:, 2 * units + depth :])
-    for k in range(2):
-        update(1, k, grad_feed[:, k * units : (k + 1) * units])
-    update(2, Ellipsis, grad_feed[:, 2 * units : 2 * units + depth])
+    middle = units + depth
+    update(1, 0, grad_feed[:, :units])
+    update(2, Ellipsis, grad_feed[:, units:middle])
+    update(1, 1, grad_feed[:, middle : middle + units])
+    update(0, 3, grad_feed[:, middle + units :])
     for level in range(LEVELS):
         update(3, level, grad_book[level])
     update(4, Ellipsis, grad_qkv[:, 3 * width :].T[:6])
@@ -1144,9 +1144,10 @@
         owners = jnp.asarray(device_of_places(devices, kind)) ^ me
         starts = (owners * rows).astype(jnp.int32)
         if rows % 16 == 0:
-            return starts, jnp.zeros((1, 128), jnp.int32)
+            places = place_of(jnp.arange(devices, dtype=jnp.int32) ^ me, devices, kind)
+            return starts, jnp.zeros((1, 128), jnp.int32), (places * rows).astype(jnp.int32)
         rowmap = (starts[:, None] + jnp.arange(rows, dtype=jnp.int32)[None, :]).reshape(1, width)
-        return starts, rowmap
+        return starts, rowmap, starts
 
     orders = {kind: order(kind) for kind in range(2, 6)}
     share = entries // devices
@@ -1156,7 +1157,8 @@
         place_of(owners, devices, 4),
         place_of(owners, devices, 5),
     )
-    flat_codes = (places * share + codes % share).astype(jnp.int32).T
+    places = (places * share + codes % share).astype(jnp.int32)
+    flat_codes = jnp.concatenate([codes.T, places.T], axis=0)
     flat_codes, orders = after((flat_codes, orders), mark)
     ready = (cosine, sine, bias, flat_codes, orders)
     early = join(early, after(gather_swaps(early, devices, 2, 1), ready))
@@ -1167,7 +1169,7 @@
     come_b = gather_swaps(feed_b, devices, 5, 2)
 
     normed_first, q, k, v, scales, qkv_weights = qkv_call(
-        *orders[2], halo, inputs, early_pieces, cosine, sine
+        *orders[2][:2], halo, inputs, early_pieces, cosine, sine
     )
     come_a, come_b = after((come_a, come_b), q)
     feed_a, feed_b = join(feed_a, come_a), join(feed_b, come_b)
@@ -1180,9 +1182,9 @@
     (
         branch_first, after_first, normed_second, hidden, slope, branch_second, low_out, latent,
         feed_weights,
-    ) = forward_call((orders[4], orders[5]), inputs, mixed, scales, feed_pieces, units, depth)
-
-    carried = fetch_call(levels, codes.T, latent, book)
+    ) = forward_call((orders[4][:2], orders[5][:2]), inputs, mixed, scales, feed_pieces, units, depth)
+
+    carried = fetch_call(levels, flat_codes, latent, book)
     keep_high, send_high = spread_call(mid, mid, flat_codes, carried, entries)
     come_high = swap_parts([send_high], devices, 5, 0)
     carried = after(carried, keep_high)
@@ -1224,7 +1226,7 @@
     for stage in range(4, split_stages):
         keep_book, come_book = reduce_split(keep_book, come_book, devices, 4, stage)
     input_gradient, qkv_a, send_a, qkv_b, send_b = finish_call(
-        *orders[2], inputs, normed_first, (q_a, q_b, q_c),
+        orders[2], inputs, normed_first, (q_a, q_b, q_c),
         (k_b, after(k_c, keep_book, keep_a, keep_b)), (v_b, v_c), halo, cosine, sine, grad_after,
         scales, sums_second, qkv_weights,
     )

time: 255 us -> 248 us (0.973); the launches traced: 250 us -> 247 us
  waiting for transfers between devices: 37.9 us -> 49 us
  Pallas kernels: 122 us -> 113 us
  local copies, waits for them, and re-layouts: 7.99 us -> 3.7 us
  starting transfers between devices: 49.5 us -> 46.8 us
    ppermute x39, waiting for transfers between devices: 36.4 us -> 48.2 us  [swap(): return lax.ppermute(block, AXES, [(i, i ^ mask) for i in range(count)])]
    pallas_call x1, Pallas kernels: 14.3 us -> 8.42 us  [attend_call(): pl.pallas_call(attend_kernel, grid=(count // QROWS,), in_specs=[pl.BlockS...]
    unnamed x96 -> x90, local copies, waits for them, and re-layouts: 6.96 us -> 3.63 us
    ppermute x39, starting transfers between devices: 45.6 us -> 42.9 us  [swap(): return lax.ppermute(block, AXES, [(i, i ^ mask) for i in range(count)])]
    pallas_call x3, Pallas kernels: 18.5 us -> 16 us  [attend_back_call(): pl.pallas_call(lambda *refs: attend_back_kernel(pieces, *refs), grid=(blo...]
  transfers between devices with their start and end apart: 42 -> 42, of which waited for: 17 -> 18; matrix products, arithmetic and copies ran while one was open for 3% -> 4% of each run, Pallas kernels for 39% -> 36%
where the time goes in v3:
time: 248 us; the launch traced here: 247 us
  Pallas kernels  113 us (46%)
  waiting for transfers between devices  49 us (20%)
  starting transfers between devices  46.8 us (19%)
  between operations  15.7 us (6%)
  other arithmetic  9.69 us (4%)
  blocking collectives  9.24 us (4%)
  local copies, waits for them, and re-layouts  3.7 us (1%)
    ppermute x39, waiting for transfers between devices, swap(): return lax.ppermute(block, AXES, [(i, i ^ mask) for i in range(count)])  48.2 us
    ppermute x39, starting transfers between devices, swap(): return lax.ppermute(block, AXES, [(i, i ^ mask) for i in range(count)])  42.9 us
    pallas_call x1, Pallas kernels, backward_call(): pl.pallas_call(backward_kernel, grid=(count // ROWS,), in_specs=[smem(),...  21.6 us
    pallas_call x1, Pallas kernels, forward_call(): pl.pallas_call(forward_kernel, grid=(count // ROWS,), in_specs=[smem(), w...  16.3 us
    pallas_call x3, Pallas kernels, attend_back_call(): pl.pallas_call(lambda *refs: attend_back_kernel(pieces, *refs), grid=(blo...  16 us
    pallas_call x1, Pallas kernels, fetch_call(): pl.pallas_call(fetch_kernel, grid=(LEVELS,), in_specs=[smem(), whole(code...  12.9 us
    pallas_call x2, Pallas kernels, spread_call(): pl.pallas_call(lambda *refs: spread_kernel(first, *refs), grid=(levels,),...  10.2 us
    all_to_all x1, blocking collectives, body(): shared = lax.all_to_all(shared, AXES, 0, 0, tiled=True)  9.24 us
  transfers between devices with their start and end apart: 42, of which 18 were waited for; matrix products, arithmetic and copies ran while one was open for 4% of the time, Pallas kernels for 36%

profile of v3, /device:TPU:0, one launch (start us, length us, event | category | flops | bytes accessed | tf_op | source)
XLA Modules:
  0.0 247.0 jit_solution(16463858480395463151)
XLA Ops:
  9.2 3.1 %collective-permute-start = (bf16[16,1664]{1,0:T(8,128)(2,1)}, bf16[16,1664]{1,0:T(8,128)(2,1)S(1)}, u32[]{:S(2)}, u32[]{:S(2)}) collective-permute-start(bf16[16,1664]{1,0:T(8,128)(2,1)} %get-tuple-element.172.refs_0_), channel_id=1, source_target_pairs={{0,8},{1,9},{2,10},{3,11},{4,12},{5,13},{6,14},{7,15},{8,0},{9,1},... | collective-permute-start | bytes 159752 | tf_op jit(solution)/shard_map/ppermute | solution.py:79
  12.3 2.6 %collective-permute-start.1 = (bf16[16,1664]{1,0:T(8,128)(2,1)}, bf16[16,1664]{1,0:T(8,128)(2,1)S(1)}, u32[]{:S(2)}, u32[]{:S(2)}) collective-permute-start(bf16[16,1664]{1,0:T(8,128)(2,1)} %get-tuple-element.172.refs_0_), channel_id=1, source_target_pairs={{0,16},{1,17},{2,18},{3,19},{4,20},{5,21},{6,22},{7,23},{8,24},{9,... | collective-permute-start | bytes 159752 | tf_op jit(solution)/shard_map/ppermute | solution.py:79
  32.9 3.8 %collective-permute-done.6.refs_3_ = bf16[64,1664]{1,0:T(8,128)(2,1)S(1)} collective-permute-done((bf16[64,1664]{1,0:T(8,128)(2,1)S(1)}, bf16[64,1664]{1,0:T(8,128)(2,1)S(1)}, u32[]{:S(2)}, u32[]{:S(2)}) %collective-permute-start.6) | collective-permute-done | bytes 213024 | tf_op jit(solution)/shard_map/ppermute | solution.py:79
  43.1 6.1 %project_rows.1 = (bf16[1024,512]{1,0:T(8,128)(2,1)S(1)}, bf16[1024,512]{1,0:T(8,128)(2,1)S(1)}, bf16[1280,512]{1,0:T(8,128)(2,1)S(1)}, bf16[1280,512]{1,0:T(8,1...) custom-call(s32[32]{0:T(128)S(1)} %get-tuple-element.177.starts, ...), custom_call_target="tpu_custom_call" | custom-call | flops 2000000000 | bytes 25165824 | tf_op jit(solution)/shard_map/project_rows/pallas_call | solution.py:447
  49.4 5.4 %collective-permute-done.10.refs_1_ = bf16[64,2048]{1,0:T(8,128)(2,1)S(1)} collective-permute-done((bf16[64,2048]{1,0:T(8,128)(2,1)S(1)}, bf16[64,2048]{1,0:T(8,128)(2,1)S(1)}, u32[]{:S(2)}, u32[]{:S(2)}) %collective-permute-start.10) | collective-permute-done | bytes 262176 | tf_op jit(solution)/shard_map/ppermute | solution.py:79
  58.2 8.4 %attend_rows.1 = (bf16[1024,512]{1,0:T(8,128)(2,1)S(1)}, f32[8,1024]{1,0:T(8,128)S(1)}) custom-call(bf16[1024,512]{1,0:T(8,128)(2,1)S(1)} %get-tuple-element.187.q.refs_4_.refs_6_, bf16[1280,512]{1,0:T(8,128)(2,1)S(1)} %get-tuple-element.196.k.refs_0_.refs_1_.refs_2_, bf16[1280,512]{1,0:T(8,128)(2,1)S(1)} %get-tuple-element.197.v.refs_2_.refs_3_.refs_4_.refs_5_, ...), custom_call_target="tpu_custom_call" | custom-call | flops 2000000000 | bytes 44040192 | tf_op jit(solution)/shard_map/attend_rows/pallas_call | solution.py:508
  66.7 5.5 %collective-permute-done.12.refs_1_ = bf16[128,2048]{1,0:T(8,128)(2,1)S(1)} collective-permute-done((bf16[128,2048]{1,0:T(8,128)(2,1)S(1)}, bf16[128,2048]{1,0:T(8,128)(2,1)S(1)}, u32[]{:S(2)}, u32[]{:S(2)}) %collective-permute-start.12) | collective-permute-done | bytes 524320 | tf_op jit(solution)/shard_map/ppermute | solution.py:79
  72.2 5.0 %collective-permute-done.13.refs_1_ = bf16[128,2816]{1,0:T(8,128)(2,1)S(1)} collective-permute-done((bf16[128,2816]{1,0:T(8,128)(2,1)S(1)}, bf16[128,2816]{1,0:T(8,128)(2,1)S(1)}, u32[]{:S(2)}, u32[]{:S(2)}) %collective-permute-start.13) | collective-permute-done | bytes 720928 | tf_op jit(solution)/shard_map/ppermute | solution.py:79
  78.7 3.5 %collective-permute-done.14.other_a = bf16[256,2048]{1,0:T(8,128)(2,1)S(1)} collective-permute-done((bf16[256,2048]{1,0:T(8,128)(2,1)S(1)}, bf16[256,2048]{1,0:T(8,128)(2,1)S(1)}, u32[]{:S(2)}, u32[]{:S(2)}) %collective-permute-start.14) | collective-permute-done | bytes 1048608 | tf_op jit(solution)/shard_map/ppermute | solution.py:79
  84.3 16.3 %feed_rows.1 = (bf16[1024,512]{1,0:T(8,128)(2,1)}, f32[1024,512]{1,0:T(8,128)}, bf16[1024,512]{1,0:T(8,128)(2,1)}, bf16[1024,2048]{1,0:T(8,128)(2,1)}, bf16[1024...) custom-call(s32[32]{0:T(128)} %get-tuple-element.173.starts_a, ...), custom_call_target="tpu_custom_call" | custom-call | flops 2000000000 | bytes 53477376 | tf_op jit(solution)/shard_map/feed_rows/pallas_call | solution.py:576
  102.6 12.9 %fetch_codes.1.refs_1_.carried = bf16[8,1024,256]{2,1,0:T(8,128)(2,1)S(1)} custom-call(s32[1]{0:T(128)S(6)} %copy.47.active, s32[16,1024]{1,0:T(8,128)S(1)} %pad_add_fusion.codes.refs_0_, f32[1024,256]{1,0:T(8,128)S(1)} %copy-done.18, bf16[8,2048,256]{2,1,0:T(8,128)(2,1)} %all-gather.2.cloned.1.call-done.book), custom_call_target="tpu_custom_call" | custom-call | flops 2000000000 | bytes 40894464 | tf_op jit(solution)/shard_map/fetch_codes/pallas_call | solution.py:632
  115.6 5.1 %spread_codes.2 = (bf16[4,1024,256]{2,1,0:T(8,128)(2,1)S(1)}, bf16[4,1024,256]{2,1,0:T(8,128)(2,1)S(1)}) custom-call(s32[16,1024]{1,0:T(8,128)S(1)} %pad_add_fusion.codes.refs_0_, bf16[8,1024,256]{2,1,0:T(8,128)(2,1)S(1)} %fetch_codes.1.refs_1_.carried), custom_call_target="tpu_custom_call" | custom-call | flops 500000000 | bytes 15728640 | tf_op jit(solution)/shard_map/spread_codes/pallas_call | solution.py:671
  121.0 5.1 %spread_codes.3 = (bf16[4,1024,256]{2,1,0:T(8,128)(2,1)S(1)}, bf16[4,1024,256]{2,1,0:T(8,128)(2,1)S(1)}) custom-call(s32[16,1024]{1,0:T(8,128)S(1)} %pad_add_fusion.codes.refs_0_, bf16[8,1024,256]{2,1,0:T(8,128)(2,1)S(1)} %fetch_codes.1.refs_1_.carried), custom_call_target="tpu_custom_call" | custom-call | flops 500000000 | bytes 15728640 | tf_op jit(solution)/shard_map/spread_codes/pallas_call | solution.py:671
  135.4 21.6 %feed_back.1 = (f32[1024,512]{1,0:T(8,128)}, bf16[1024,512]{1,0:T(8,128)(2,1)}, f32[8,512]{1,0:T(8,128)}, bf16[1,256,2304]{2,1,0:T(8,128)(2,1)}, bf16[1,256,2304...) custom-call(s32[32]{0:T(128)} %get-tuple-element.182.dests_a, s32[1,128]{1,0:T(1,128)} %copy-done.30, ...), custom_call_target="tpu_custom_call" | custom-call | flops 1000000000 | bytes 78643200 | tf_op jit(solution)/shard_map/feed_back/pallas_call | solution.py:751
  161.8 3.5 %attend_back.3 = (bf16[256,512]{1,0:T(8,128)(2,1)S(1)}, f32[512,512]{1,0:T(8,128)S(1)}, f32[512,512]{1,0:T(8,128)S(1)}, bf16[512,512]{1,0:T(8,128)(2,1)S(1)}) custom-call(bf16[1280,512]{1,0:T(8,128)(2,1)S(1)} %get-tuple-element.196.k.refs_0_.refs_1_.refs_2_, bf16[1280,512]{1,0:T(8,128)(2,1)S(1)} %get-tuple-element.196.k.refs_0_.refs_1_.refs_2_, ...), custom_call_target="tpu_custom_call" | custom-call | flops 4000000000 | bytes 12582912 | tf_op jit(solution)/shard_map/attend_back/pallas_call | solution.py:841
  169.3 4.4 %attend_back.4 = (bf16[256,512]{1,0:T(8,128)(2,1)S(1)}, f32[512,512]{1,0:T(8,128)S(1)}, f32[512,512]{1,0:T(8,128)S(1)}, bf16[512,512]{1,0:T(8,128)(2,1)}) custom-call(bf16[1280,512]{1,0:T(8,128)(2,1)S(1)} %get-tuple-element.196.k.refs_0_.refs_1_.refs_2_, bf16[1280,512]{1,0:T(8,128)(2,1)S(1)} %get-tuple-element.196.k.refs_0_.refs_1_.refs_2_, ...), custom_call_target="tpu_custom_call" | custom-call | bytes 12582912 | tf_op jit(solution)/shard_map/attend_back/pallas_call | solution.py:841
  179.6 8.1 %attend_back.5 = (bf16[512,512]{1,0:T(8,128)(2,1)S(1)}, f32[768,512]{1,0:T(8,128)S(1)}, f32[768,512]{1,0:T(8,128)S(1)}, bf16[512,512]{1,0:T(8,128)(2,1)}) custom-call(bf16[1280,512]{1,0:T(8,128)(2,1)S(1)} %get-tuple-element.196.k.refs_0_.refs_1_.refs_2_, bf16[1280,512]{1,0:T(8,128)(2,1)S(1)} %get-tuple-element.196.k.refs_0_.refs_1_.refs_2_, ...), custom_call_target="tpu_custom_call" | custom-call | bytes 25165824 | tf_op jit(solution)/shard_map/attend_back/pallas_call | solution.py:841
  191.8 7.9 %finish_rows.1 = (f32[1024,512]{1,0:T(8,128)}, bf16[1,256,896]{2,1,0:T(8,128)(2,1)S(1)}, bf16[1,256,896]{2,1,0:T(8,128)(2,1)S(1)}, bf16[1,256,896]{2,1,0:T(8,128)(2,1)S(1)}, bf16[1,256,896]{2,1,0:T(8,128)(2,1)S(1)}) custom-call(s32[32]{0:T(128)S(1)} %get-tuple-element.181.dests, s32[1,128]{1,0:T(1,128)S(1)} %copy-done.31, bf16[1024,512]{1,0:T(8,128)(2,1)S(1)} %copy-done.12, ...), custom_call_target="tpu_custom_call" | custom-call | bytes 31457280 | tf_op jit(solution)/shard_map/finish_rows/pallas_call | solution.py:940
  200.2 3.5 %collective-permute-done.28.refs_0_ = bf16[8,64,256]{2,1,0:T(8,128)(2,1)S(1)} collective-permute-done((bf16[8,64,256]{2,1,0:T(8,128)(2,1)S(1)}, bf16[8,64,256]{2,1,0:T(8,128)(2,1)S(1)}, u32[]{:S(2)}, u32[]{:S(2)}) %collective-permute-start.28) | collective-permute-done | bytes 262176 | tf_op jit(solution)/shard_map/ppermute | solution.py:79
  205.9 2.6 %collective-permute-start.37 = (bf16[1,64,1792]{2,1,0:T(8,128)(2,1)S(1)}, bf16[1,64,1792]{2,1,0:T(8,128)(2,1)S(1)}, u32[]{:S(2)}, u32[]{:S(2)}) collective-permute-start(bf16[1,64,1792]{2,1,0:T(8,128)(2,1)S(1)} %get-tuple-element.292), channel_id=1, source_target_pairs={{0,6},{1,7},{2,4},{3,5},{4,2},{5,3},{6,0},{7,1},{8,14},{9,15},{10,... | collective-permute-start | bytes 688136 | tf_op jit(solution)/shard_map/ppermute | solution.py:79
  208.6 5.4 %collective-permute-done.31.refs_1_ = bf16[1,32,4864]{2,1,0:T(8,128)(2,1)S(1)} collective-permute-done((bf16[1,32,4864]{2,1,0:T(8,128)(2,1)S(1)}, bf16[1,32,4864]{2,1,0:T(8,128)(2,1)S(1)}, u32[]{:S(2)}, u32[]{:S(2)}) %collective-permute-start.31) | collective-permute-done | bytes 311328 | tf_op jit(solution)/shard_map/ppermute | solution.py:79
  214.3 4.5 %collective-permute-done.37.refs_3_ = bf16[1,64,1792]{2,1,0:T(8,128)(2,1)S(1)} collective-permute-done((bf16[1,64,1792]{2,1,0:T(8,128)(2,1)S(1)}, bf16[1,64,1792]{2,1,0:T(8,128)(2,1)S(1)}, u32[]{:S(2)}, u32[]{:S(2)}) %collective-permute-start.37) | collective-permute-done | bytes 229408 | tf_op jit(solution)/shard_map/ppermute | solution.py:79
  220.9 2.7 %collective-permute-start.40 = (bf16[1,16,1792]{2,1,0:T(8,128)(2,1)S(1)}, bf16[1,16,1792]{2,1,0:T(8,128)(2,1)S(1)}, u32[]{:S(2)}, u32[]{:S(2)}) collective-permute-start(bf16[1,16,1792]{2,1,0:T(8,128)(2,1)S(1)} %get-tuple-element.296), channel_id=1, source_target_pairs={{0,24},{1,25},{2,26},{3,27},{4,28},{5,29},{6,30},{7,31},{8,16},{9,... | collective-permute-start | bytes 172040 | tf_op jit(solution)/shard_map/ppermute | solution.py:79
  228.5 9.2 %all_to_all.11 = f32[32,1,128]{2,1,0:T(1,128)S(1)} all-to-all(f32[32,1,128]{2,1,0:T(1,128)S(1)} %bitcast.9), channel_id=1, replica_groups=mesh['clip'=8,'tm'=4] {'clip','tm'}, dimensions={0} | all-to-all | bytes 32768 | tf_op jit(solution)/shard_map/all_to_all | solution.py:1250
  (206 shorter events, 75.1 us)
Async XLA Ops:
  7.2 94.2 %all-gather.2.cloned.1.call-start = ((), (), s32[]{:S(2)}) async-start(), calls=%async_computation.1 | async-start | bytes 8650752 | tf_op jit(solution)/shard_map/all_gather | solution.py:1128
  9.2 13.8 %collective-permute-start = (bf16[16,1664]{1,0:T(8,128)(2,1)}, bf16[16,1664]{1,0:T(8,128)(2,1)S(1)}, u32[]{:S(2)}, u32[]{:S(2)}) collective-permute-start(bf16[16,1664]{1,0:T(8,128)(2,1)} %get-tuple-element.172.refs_0_), channel_id=1, source_target_pairs={{0,8},{1,9},{2,10},{3,11},{4,12},{5,13},{6,14},{7,15},{8,0},{9,1},... | collective-permute-start | bytes 159752 | tf_op jit(solution)/shard_map/ppermute | solution.py:79
  12.3 10.8 %collective-permute-start.1 = (bf16[16,1664]{1,0:T(8,128)(2,1)}, bf16[16,1664]{1,0:T(8,128)(2,1)S(1)}, u32[]{:S(2)}, u32[]{:S(2)}) collective-permute-start(bf16[16,1664]{1,0:T(8,128)(2,1)} %get-tuple-element.172.refs_0_), channel_id=1, source_target_pairs={{0,16},{1,17},{2,18},{3,19},{4,20},{5,21},{6,22},{7,23},{8,24},{9,... | collective-permute-start | bytes 159752 | tf_op jit(solution)/shard_map/ppermute | solution.py:79
  14.9 14.2 %collective-permute-start.8 = (bf16[16,4864]{1,0:T(8,128)(2,1)}, bf16[16,4864]{1,0:T(8,128)(2,1)S(1)}, u32[]{:S(2)}, u32[]{:S(2)}) collective-permute-start(bf16[16,4864]{1,0:T(8,128)(2,1)} %get-tuple-element.189.refs_0_), channel_id=1, source_target_pairs={{0,16},{1,17},{2,18},{3,19},{4,20},{5,21},{6,22},{7,23},{8,24},{9,... | collective-permute-start | bytes 466952 | tf_op jit(solution)/shard_map/ppermute | solution.py:79
  23.1 9.6 %collective-permute-start.4 = (bf16[64,1664]{1,0:T(8,128)(2,1)S(1)}, bf16[64,1664]{1,0:T(8,128)(2,1)S(1)}, u32[]{:S(2)}, u32[]{:S(2)}) collective-permute-start(bf16[64,1664]{1,0:T(8,128)(2,1)S(1)} %join_rows.8.refs_0_), channel_id=1, source_target_pairs={{0,2},{1,3},{2,0},{3,1},{4,6},{5,7},{6,4},{7,5},{8,10},{9,11},{10,... | collective-permute-start | bytes 638984 | tf_op jit(solution)/shard_map/ppermute | solution.py:79
  26.2 10.5 %collective-permute-start.6 = (bf16[64,1664]{1,0:T(8,128)(2,1)S(1)}, bf16[64,1664]{1,0:T(8,128)(2,1)S(1)}, u32[]{:S(2)}, u32[]{:S(2)}) collective-permute-start(bf16[64,1664]{1,0:T(8,128)(2,1)S(1)} %join_rows.8.refs_0_), channel_id=1, source_target_pairs={{0,6},{1,7},{2,4},{3,5},{4,2},{5,3},{6,0},{7,1},{8,14},{9,15},{10,... | collective-permute-start | bytes 638984 | tf_op jit(solution)/shard_map/ppermute | solution.py:79
  29.1 11.1 %collective-permute-start.9 = (bf16[32,4864]{1,0:T(8,128)(2,1)S(1)}, bf16[32,4864]{1,0:T(8,128)(2,1)S(1)}, u32[]{:S(2)}, u32[]{:S(2)}) collective-permute-start(bf16[32,4864]{1,0:T(8,128)(2,1)S(1)} %join_rows.10.refs_0_), channel_id=1, source_target_pairs={{0,8},{1,9},{2,10},{3,11},{4,12},{5,13},{6,14},{7,15},{8,0},{9,1},... | collective-permute-start | bytes 933896 | tf_op jit(solution)/shard_map/ppermute | solution.py:79
  40.2 14.5 %collective-permute-start.11 = (bf16[64,2816]{1,0:T(8,128)(2,1)S(1)}, bf16[64,2816]{1,0:T(8,128)(2,1)S(1)}, u32[]{:S(2)}, u32[]{:S(2)}) collective-permute-start(bf16[64,2816]{1,0:T(8,128)(2,1)S(1)} %get-tuple-element.193.refs_0_), channel_id=1, source_target_pairs={{0,2},{1,3},{2,0},{3,1},{4,6},{5,7},{6,4},{7,5},{8,10},{9,11},{10,... | collective-permute-start | bytes 1081352 | tf_op jit(solution)/shard_map/ppermute | solution.py:79
  41.8 13.0 %collective-permute-start.10 = (bf16[64,2048]{1,0:T(8,128)(2,1)S(1)}, bf16[64,2048]{1,0:T(8,128)(2,1)S(1)}, u32[]{:S(2)}, u32[]{:S(2)}) collective-permute-start(bf16[64,2048]{1,0:T(8,128)(2,1)S(1)} %get-tuple-element.192.refs_0_), channel_id=1, source_target_pairs={{0,4},{1,5},{2,6},{3,7},{4,0},{5,1},{6,2},{7,3},{8,12},{9,13},{10,... | collective-permute-start | bytes 786440 | tf_op jit(solution)/shard_map/ppermute | solution.py:79
  54.8 22.3 %collective-permute-start.13 = (bf16[128,2816]{1,0:T(8,128)(2,1)S(1)}, bf16[128,2816]{1,0:T(8,128)(2,1)S(1)}, u32[]{:S(2)}, u32[]{:S(2)}) collective-permute-start(bf16[128,2816]{1,0:T(8,128)(2,1)S(1)} %join_rows.13.refs_0_), channel_id=1, source_target_pairs={{0,4},{1,5},{2,6},{3,7},{4,0},{5,1},{6,2},{7,3},{8,12},{9,13},{10,... | collective-permute-start | bytes 2162696 | tf_op jit(solution)/shard_map/ppermute | solution.py:79
  57.0 15.2 %collective-permute-start.12 = (bf16[128,2048]{1,0:T(8,128)(2,1)S(1)}, bf16[128,2048]{1,0:T(8,128)(2,1)S(1)}, u32[]{:S(2)}, u32[]{:S(2)}) collective-permute-start(bf16[128,2048]{1,0:T(8,128)(2,1)S(1)} %join_rows.12.refs_0_), channel_id=1, source_target_pairs={{0,2},{1,3},{2,0},{3,1},{4,6},{5,7},{6,4},{7,5},{8,10},{9,11},{10,... | collective-permute-start | bytes 1572872 | tf_op jit(solution)/shard_map/ppermute | solution.py:79
  132.0 26.1 %collective-permute-start.18 = (bf16[4,512,256]{2,1,0:T(8,128)(2,1)}, bf16[4,512,256]{2,1,0:T(8,128)(2,1)S(1)}, u32[]{:S(2)}, u32[]{:S(2)}) collective-permute-start(bf16[4,512,256]{2,1,0:T(8,128)(2,1)} %get-tuple-element.224), channel_id=1, source_target_pairs={{0,2},{1,3},{2,0},{3,1},{4,6},{5,7},{6,4},{7,5},{8,10},{9,11},{10,... | collective-permute-start | bytes 3145736 | tf_op jit(solution)/shard_map/ppermute | solution.py:79
  134.3 25.2 %collective-permute-start.19 = (bf16[4,512,256]{2,1,0:T(8,128)(2,1)}, bf16[4,512,256]{2,1,0:T(8,128)(2,1)S(1)}, u32[]{:S(2)}, u32[]{:S(2)}) collective-permute-start(bf16[4,512,256]{2,1,0:T(8,128)(2,1)} %get-tuple-element.225), channel_id=1, source_target_pairs={{0,4},{1,5},{2,6},{3,7},{4,0},{5,1},{6,2},{7,3},{8,12},{9,13},{10,... | collective-permute-start | bytes 3145736 | tf_op jit(solution)/shard_map/ppermute | solution.py:79
  160.1 14.9 %collective-permute-start.22 = (bf16[4,256,256]{2,1,0:T(8,128)(2,1)S(1)}, bf16[4,256,256]{2,1,0:T(8,128)(2,1)S(1)}, u32[]{:S(2)}, u32[]{:S(2)}) collective-permute-start(bf16[4,256,256]{2,1,0:T(8,128)(2,1)S(1)} %get-tuple-element.244), channel_id=1, source_target_pairs={{0,4},{1,5},{2,6},{3,7},{4,0},{5,1},{6,2},{7,3},{8,12},{9,13},{10,... | collective-permute-start | bytes 1572872 | tf_op jit(solution)/shard_map/ppermute | solution.py:79
  161.3 14.9 %collective-permute-start.23 = (bf16[4,256,256]{2,1,0:T(8,128)(2,1)S(1)}, bf16[4,256,256]{2,1,0:T(8,128)(2,1)S(1)}, u32[]{:S(2)}, u32[]{:S(2)}) collective-permute-start(bf16[4,256,256]{2,1,0:T(8,128)(2,1)S(1)} %get-tuple-element.245), channel_id=1, source_target_pairs={{0,2},{1,3},{2,0},{3,1},{4,6},{5,7},{6,4},{7,5},{8,10},{9,11},{10,... | collective-permute-start | bytes 1572872 | tf_op jit(solution)/shard_map/ppermute | solution.py:79
  166.0 21.7 %collective-permute-start.26 = (bf16[1,128,2560]{2,1,0:T(8,128)(2,1)S(1)}, bf16[1,128,2560]{2,1,0:T(8,128)(2,1)S(1)}, u32[]{:S(2)}, u32[]{:S(2)}) collective-permute-start(bf16[1,128,2560]{2,1,0:T(8,128)(2,1)S(1)} %get-tuple-element.257), channel_id=1, source_target_pairs={{0,4},{1,5},{2,6},{3,7},{4,0},{5,1},{6,2},{7,3},{8,12},{9,13},{10,... | collective-permute-start | bytes 1966088 | tf_op jit(solution)/shard_map/ppermute | solution.py:79
  167.8 19.8 %collective-permute-start.25 = (bf16[1,128,2304]{2,1,0:T(8,128)(2,1)S(1)}, bf16[1,128,2304]{2,1,0:T(8,128)(2,1)S(1)}, u32[]{:S(2)}, u32[]{:S(2)}) collective-permute-start(bf16[1,128,2304]{2,1,0:T(8,128)(2,1)S(1)} %get-tuple-element.256), channel_id=1, source_target_pairs={{0,2},{1,3},{2,0},{3,1},{4,6},{5,7},{6,4},{7,5},{8,10},{9,11},{10,... | collective-permute-start | bytes 1769480 | tf_op jit(solution)/shard_map/ppermute | solution.py:79
  176.5 11.1 %collective-permute-start.24 = (bf16[8,128,256]{2,1,0:T(8,128)(2,1)S(1)}, bf16[8,128,256]{2,1,0:T(8,128)(2,1)S(1)}, u32[]{:S(2)}, u32[]{:S(2)}) collective-permute-start(bf16[8,128,256]{2,1,0:T(8,128)(2,1)S(1)} %get-tuple-element.255), channel_id=1, source_target_pairs={{0,8},{1,9},{2,10},{3,11},{4,12},{5,13},{6,14},{7,15},{8,0},{9,1},... | collective-permute-start | bytes 1572872 | tf_op jit(solution)/shard_map/ppermute | solution.py:79
  178.3 13.4 %collective-permute-start.27 = (bf16[512,512]{1,0:T(8,128)(2,1)S(1)}, bf16[512,512]{1,0:T(8,128)(2,1)S(1)}, u32[]{:S(2)}, u32[]{:S(2)}) collective-permute-start(bf16[512,512]{1,0:T(8,128)(2,1)S(1)} %get-tuple-element.266), channel_id=1, source_target_pairs={{1,0},{2,1},{3,2},{5,4},{6,5},{7,6},{9,8},{10,9},{11,10},{13,12},{... | collective-permute-start | bytes 1572872 | tf_op jit(solution)/shard_map/ppermute | solution.py:1211
  188.0 15.7 %collective-permute-start.28 = (bf16[8,64,256]{2,1,0:T(8,128)(2,1)S(1)}, bf16[8,64,256]{2,1,0:T(8,128)(2,1)S(1)}, u32[]{:S(2)}, u32[]{:S(2)}) collective-permute-start(bf16[8,64,256]{2,1,0:T(8,128)(2,1)S(1)} %get-tuple-element.271), channel_id=1, source_target_pairs={{0,16},{1,17},{2,18},{3,19},{4,20},{5,21},{6,22},{7,23},{8,24},{9,... | collective-permute-start | bytes 786440 | tf_op jit(solution)/shard_map/ppermute | solution.py:79
  189.3 15.1 %collective-permute-start.30 = (bf16[1,64,2560]{2,1,0:T(8,128)(2,1)S(1)}, bf16[1,64,2560]{2,1,0:T(8,128)(2,1)S(1)}, u32[]{:S(2)}, u32[]{:S(2)}) collective-permute-start(bf16[1,64,2560]{2,1,0:T(8,128)(2,1)S(1)} %get-tuple-element.276), channel_id=1, source_target_pairs={{0,2},{1,3},{2,0},{3,1},{4,6},{5,7},{6,4},{7,5},{8,10},{9,11},{10,... | collective-permute-start | bytes 983048 | tf_op jit(solution)/shard_map/ppermute | solution.py:79
  190.6 13.8 %collective-permute-start.29 = (bf16[1,64,2304]{2,1,0:T(8,128)(2,1)S(1)}, bf16[1,64,2304]{2,1,0:T(8,128)(2,1)S(1)}, u32[]{:S(2)}, u32[]{:S(2)}) collective-permute-start(bf16[1,64,2304]{2,1,0:T(8,128)(2,1)S(1)} %get-tuple-element.275), channel_id=1, source_target_pairs={{0,4},{1,5},{2,6},{3,7},{4,0},{5,1},{6,2},{7,3},{8,12},{9,13},{10,... | collective-permute-start | bytes 884744 | tf_op jit(solution)/shard_map/ppermute | solution.py:79
  205.9 12.9 %collective-permute-start.37 = (bf16[1,64,1792]{2,1,0:T(8,128)(2,1)S(1)}, bf16[1,64,1792]{2,1,0:T(8,128)(2,1)S(1)}, u32[]{:S(2)}, u32[]{:S(2)}) collective-permute-start(bf16[1,64,1792]{2,1,0:T(8,128)(2,1)S(1)} %get-tuple-element.292), channel_id=1, source_target_pairs={{0,6},{1,7},{2,4},{3,5},{4,2},{5,3},{6,0},{7,1},{8,14},{9,15},{10,... | collective-permute-start | bytes 688136 | tf_op jit(solution)/shard_map/ppermute | solution.py:79
  214.2 13.4 %collective-permute-start.32 = (bf16[1,16,4864]{2,1,0:T(8,128)(2,1)S(1)}, bf16[1,16,4864]{2,1,0:T(8,128)(2,1)S(1)}, u32[]{:S(2)}, u32[]{:S(2)}) collective-permute-start(bf16[1,16,4864]{2,1,0:T(8,128)(2,1)S(1)} %get-tuple-element.283), channel_id=1, source_target_pairs={{0,16},{1,17},{2,18},{3,19},{4,20},{5,21},{6,22},{7,23},{8,24},{9,... | collective-permute-start | bytes 466952 | tf_op jit(solution)/shard_map/ppermute | solution.py:79
  (63 other events, 815.2 us)
Sparse Core Ops, SparseCore 0:
  11.5 89.8 all-gather.1

commit v4 on v3

--- a/solution.py
+++ b/solution.py
@@ -180,39 +180,6 @@
     return outs[0], swap_parts(outs[1:], count, kind, stage)
 
 
-def pair_kernel(radix, *refs):
-    outs, operands = refs[-2 * radix :], refs[: -2 * radix]
-    half = len(operands) // 2
-    for index in range(2):
-        split_kernel(
-            radix,
-            *operands[index * half : (index + 1) * half],
-            *outs[index * radix : (index + 1) * radix],
-        )
-
-
-def pair_split(low, high, count, kinds, stage):
-    _, radix = digit_plan(count, kinds[0])[stage]
-    lead, rows, columns = low[0].shape
-    spec = lambda size: pl.BlockSpec((1, size, columns), lambda i: (i, 0, 0))
-    operands = [low[0], *low[1], high[0], *high[1]]
-    types = ([f32] + [bf16] * (radix - 1)) * 2
-    outs = pl.pallas_call(
-        lambda *refs: pair_kernel(radix, *refs),
-        grid=(lead,),
-        in_specs=[spec(rows)] * len(operands),
-        out_specs=[spec(rows // radix)] * len(types),
-        out_shape=[jax.ShapeDtypeStruct((lead, rows // radix, columns), kind) for kind in types],
-        compiler_params=params(20),
-        cost_estimate=cost(0, 2),
-        name="split_sums",
-    )(*operands)
-    return (
-        (outs[0], swap_parts(outs[1:radix], count, kinds[0], stage)),
-        (outs[radix], swap_parts(outs[radix + 1 :], count, kinds[1], stage)),
-    )
-
-
 def merge_kernel(radix, groups, *refs):
     outs = refs[-radix:]
     base = left = 0
@@ -530,7 +497,7 @@
 
 def forward_kernel(
     starts_a, rowmap_a, starts_b, rowmap_b, inputs, mixed, scales, own_a, other_a, own_b, other_b,
-    branch_first, after_first, normed, hidden, slope, branch_second, low_out, latent, weights,
+    branch_first, after_first, normed, hidden, slope, branch_second, low_out, latent, again, weights,
 ):
     step = pl.program_id(0)
     width = inputs.shape[1]
@@ -563,7 +530,9 @@
     branch_second[...] = second.astype(bf16)
     rounded = (after + scales[5:6, :] * second).astype(bf16)
     low_out[...] = rounded
-    latent[...] = dot(rounded, weights[:, proj:last])
+    result = dot(rounded, weights[:, proj:last])
+    latent[...] = result
+    again[...] = result
 
 
 def forward_call(orders, inputs, mixed, scales, pieces, units, depth):
@@ -571,7 +540,7 @@
     columns = pieces[0].shape[1] + pieces[2].shape[1]
     row = lambda size: pl.BlockSpec((ROWS, size), lambda i: (i, 0))
     kept = ((width, bf16), (width, f32), (width, bf16), (units, bf16), (units, bf16),
-            (width, bf16), (width, bf16), (depth, f32))
+            (width, bf16), (width, bf16), (depth, f32), (depth, f32))
     (starts_a, rowmap_a), (starts_b, rowmap_b) = orders
     return pl.pallas_call(
         forward_kernel,
@@ -927,7 +896,7 @@
 ):
     count, width = normed.shape
     _, rowmap, dests = order
-    columns = 3 * width + 256
+    columns = 3 * width + 128
     row = pl.BlockSpec((ROWS, width), lambda i: (i, 0))
     first = pl.BlockSpec((ROWS, width), lambda i: (0, 0))
     rest = pl.BlockSpec((ROWS, width), lambda i: (jnp.maximum(i - 1, 0), 0))
@@ -952,8 +921,8 @@
             pltpu.VMEM((count, width), bf16),
             pltpu.VMEM((count, width), bf16),
             pltpu.VMEM((count, width), bf16),
-            pltpu.VMEM((256, width), f32),
-            pltpu.VMEM((width, 256), bf16),
+            pltpu.VMEM((128, width), f32),
+            pltpu.VMEM((width, 128), bf16),
         ],
         compiler_params=params(32),
         cost_estimate=cost(0, 10),
@@ -1049,7 +1018,7 @@
         for out, result in zip(outs[group], results):
             out[index] = result
 
-    width = (grad_qkv.shape[1] - 256) // 3
+    width = (grad_qkv.shape[1] - 128) // 3
     units = masters[1].shape[2]
     depth = masters[2].shape[1]
     for k in range(3):
@@ -1139,26 +1108,27 @@
     offset = lax.axis_index("tm") * frame_count
     positions = after(offset, mark) - MARGIN + jnp.arange(frame_count + MARGIN, dtype=jnp.int32)
     cosine, sine = turn_tables(positions, width // HEADS)
-    bias = score_bias(frame_count, offset)
+    bias = score_bias(frame_count, after(offset, mark))
     def order(kind):
-        owners = jnp.asarray(device_of_places(devices, kind)) ^ me
+        owners = jnp.asarray(device_of_places(devices, kind)) ^ after(me, mark)
         starts = (owners * rows).astype(jnp.int32)
         if rows % 16 == 0:
-            places = place_of(jnp.arange(devices, dtype=jnp.int32) ^ me, devices, kind)
+            places = place_of(jnp.arange(devices, dtype=jnp.int32) ^ after(me, mark), devices, kind)
             return starts, jnp.zeros((1, 128), jnp.int32), (places * rows).astype(jnp.int32)
         rowmap = (starts[:, None] + jnp.arange(rows, dtype=jnp.int32)[None, :]).reshape(1, width)
         return starts, rowmap, starts
 
     orders = {kind: order(kind) for kind in range(2, 6)}
     share = entries // devices
-    owners = (codes // share) ^ me
+    late_codes, late_me = after((codes, me), mark)
+    owners = (late_codes // share) ^ late_me
     places = jnp.where(
         jnp.arange(LEVELS)[None, :] < mid,
         place_of(owners, devices, 4),
         place_of(owners, devices, 5),
     )
-    places = (places * share + codes % share).astype(jnp.int32)
-    flat_codes = jnp.concatenate([codes.T, places.T], axis=0)
+    places = (places * share + late_codes % share).astype(jnp.int32)
+    flat_codes = jnp.concatenate([late_codes.T, places.T], axis=0)
     flat_codes, orders = after((flat_codes, orders), mark)
     ready = (cosine, sine, bias, flat_codes, orders)
     early = join(early, after(gather_swaps(early, devices, 2, 1), ready))
@@ -1181,10 +1151,10 @@
     feed_pieces = (feed_a, swap(feed_a, devices, 1), feed_b, swap(feed_b, devices, 1))
     (
         branch_first, after_first, normed_second, hidden, slope, branch_second, low_out, latent,
-        feed_weights,
+        latent_again, feed_weights,
     ) = forward_call((orders[4][:2], orders[5][:2]), inputs, mixed, scales, feed_pieces, units, depth)
 
-    carried = fetch_call(levels, flat_codes, latent, book)
+    carried = fetch_call(levels, flat_codes, latent_again, book)
     keep_high, send_high = spread_call(mid, mid, flat_codes, carried, entries)
     come_high = swap_parts([send_high], devices, 5, 0)
     carried = after(carried, keep_high)
@@ -1199,8 +1169,8 @@
     )
     come_a = swap_parts([send_a], devices, 4, 0)
     come_b = swap_parts([send_b], devices, 5, 0)
-    come_low, come_high = after((low[1], high[1]), keep_a)
-    low, high = pair_split((low[0], come_low), (high[0], come_high), devices, (4, 5), 2)
+    high = reduce_split(high[0], after(high[1], keep_a), devices, 5, 2, 2)
+    low = reduce_split(low[0], after(low[1], high[0]), devices, 4, 2)
 
     lead = MARGIN // QROWS
     blocks = frame_count // QROWS

time: 248 us -> 245 us (0.988)
  other arithmetic: 9.69 us -> 5.22 us
  starting transfers between devices: 46.8 us -> 50.8 us
  waiting for transfers between devices: 49 us -> 45.1 us
    ppermute x39, starting transfers between devices: 42.9 us -> 46.8 us  [swap(): return lax.ppermute(block, AXES, [(i, i ^ mask) for i in range(count)])]
    ppermute x39, waiting for transfers between devices: 48.2 us -> 45.1 us  [swap(): return lax.ppermute(block, AXES, [(i, i ^ mask) for i in range(count)])]
    unnamed x90 -> x98, local copies, waits for them, and re-layouts: 3.63 us -> 5.39 us
    pallas_call x9 -> x11, Pallas kernels: 6.02 us -> 6.38 us  [reduce_split(): pl.pallas_call(lambda *refs: split_kernel(radix, *refs), grid=(steps,), i...]
  transfers between devices with their start and end apart: 42 -> 42, of which waited for: 18 -> 19; matrix products, arithmetic and copies ran while one was open for 4% -> 2% of each run, Pallas kernels for 36% -> 37%
where the time goes in v4:
time: 245 us; the launch traced here: 244 us
  Pallas kernels  113 us (46%)
  starting transfers between devices  50.8 us (21%)
  waiting for transfers between devices  45.1 us (18%)
  between operations  15.7 us (6%)
  blocking collectives  9.18 us (4%)
  local copies, waits for them, and re-layouts  5.46 us (2%)
  other arithmetic  5.22 us (2%)
    ppermute x39, starting transfers between devices, swap(): return lax.ppermute(block, AXES, [(i, i ^ mask) for i in range(count)])  46.8 us
    ppermute x39, waiting for transfers between devices, swap(): return lax.ppermute(block, AXES, [(i, i ^ mask) for i in range(count)])  45.1 us
    pallas_call x1, Pallas kernels, backward_call(): pl.pallas_call(backward_kernel, grid=(count // ROWS,), in_specs=[smem(),...  21.6 us
    pallas_call x1, Pallas kernels, forward_call(): pl.pallas_call(forward_kernel, grid=(count // ROWS,), in_specs=[smem(), w...  16.4 us
    pallas_call x3, Pallas kernels, attend_back_call(): pl.pallas_call(lambda *refs: attend_back_kernel(pieces, *refs), grid=(blo...  16 us
    pallas_call x1, Pallas kernels, fetch_call(): pl.pallas_call(fetch_kernel, grid=(LEVELS,), in_specs=[smem(), whole(code...  12.9 us
    pallas_call x2, Pallas kernels, spread_call(): pl.pallas_call(lambda *refs: spread_kernel(first, *refs), grid=(levels,),...  10.2 us
    all_to_all x1, blocking collectives, body(): shared = lax.all_to_all(shared, AXES, 0, 0, tiled=True)  9.18 us
  transfers between devices with their start and end apart: 42, of which 19 were waited for; matrix products, arithmetic and copies ran while one was open for 2% of the time, Pallas kernels for 37%

profile of v4, /device:TPU:0, one launch (start us, length us, event | category | flops | bytes accessed | tf_op | source)
XLA Modules:
  0.0 244.4 jit_solution(14618910980483730134)
XLA Ops:
  9.2 3.1 %collective-permute-start = (bf16[16,1664]{1,0:T(8,128)(2,1)}, bf16[16,1664]{1,0:T(8,128)(2,1)S(1)}, u32[]{:S(2)}, u32[]{:S(2)}) collective-permute-start(bf16[16,1664]{1,0:T(8,128)(2,1)} %get-tuple-element.176.refs_0_), channel_id=1, source_target_pairs={{0,8},{1,9},{2,10},{3,11},{4,12},{5,13},{6,14},{7,15},{8,0},{9,1},... | collective-permute-start | bytes 159752 | tf_op jit(solution)/shard_map/ppermute | solution.py:79
  18.7 3.0 %collective-permute-done.2.refs_3_ = bf16[16,1664]{1,0:T(8,128)(2,1)S(1)} collective-permute-done((bf16[16,1664]{1,0:T(8,128)(2,1)}, bf16[16,1664]{1,0:T(8,128)(2,1)S(1)}, u32[]{:S(2)}, u32[]{:S(2)}) %collective-permute-start.2) | collective-permute-done | bytes 53280 | tf_op jit(solution)/shard_map/ppermute | solution.py:79
  31.3 3.3 %collective-permute-start.9 = (bf16[32,4864]{1,0:T(8,128)(2,1)S(1)}, bf16[32,4864]{1,0:T(8,128)(2,1)S(1)}, u32[]{:S(2)}, u32[]{:S(2)}) collective-permute-start(bf16[32,4864]{1,0:T(8,128)(2,1)S(1)} %join_rows.10.refs_0_), channel_id=1, source_target_pairs={{0,8},{1,9},{2,10},{3,11},{4,12},{5,13},{6,14},{7,15},{8,0},{9,1},... | collective-permute-start | bytes 933896 | tf_op jit(solution)/shard_map/ppermute | solution.py:79
  43.2 6.2 %project_rows.1 = (bf16[1024,512]{1,0:T(8,128)(2,1)S(1)}, bf16[1024,512]{1,0:T(8,128)(2,1)S(1)}, bf16[1280,512]{1,0:T(8,128)(2,1)S(1)}, bf16[1280,512]{1,0:T(8,1...) custom-call(s32[32]{0:T(128)S(1)} %get-tuple-element.184.starts, ...), custom_call_target="tpu_custom_call" | custom-call | flops 2000000000 | bytes 25165824 | tf_op jit(solution)/shard_map/project_rows/pallas_call | solution.py:414
  50.0 3.8 %collective-permute-done.10.refs_1_ = bf16[64,2048]{1,0:T(8,128)(2,1)S(1)} collective-permute-done((bf16[64,2048]{1,0:T(8,128)(2,1)S(1)}, bf16[64,2048]{1,0:T(8,128)(2,1)S(1)}, u32[]{:S(2)}, u32[]{:S(2)}) %collective-permute-start.10) | collective-permute-done | bytes 262176 | tf_op jit(solution)/shard_map/ppermute | solution.py:79
  57.7 8.5 %attend_rows.1 = (bf16[1024,512]{1,0:T(8,128)(2,1)S(1)}, f32[8,1024]{1,0:T(8,128)S(1)}) custom-call(bf16[1024,512]{1,0:T(8,128)(2,1)S(1)} %get-tuple-element.194.q.refs_4_.refs_6_, bf16[1280,512]{1,0:T(8,128)(2,1)S(1)} %get-tuple-element.203.k.refs_0_.refs_1_.refs_2_, bf16[1280,512]{1,0:T(8,128)(2,1)S(1)} %get-tuple-element.204.v.refs_2_.refs_3_.refs_4_.refs_5_, ...), custom_call_target="tpu_custom_call" | custom-call | flops 2000000000 | bytes 44040192 | tf_op jit(solution)/shard_map/attend_rows/pallas_call | solution.py:475
  66.2 5.9 %collective-permute-done.12.refs_1_ = bf16[128,2048]{1,0:T(8,128)(2,1)S(1)} collective-permute-done((bf16[128,2048]{1,0:T(8,128)(2,1)S(1)}, bf16[128,2048]{1,0:T(8,128)(2,1)S(1)}, u32[]{:S(2)}, u32[]{:S(2)}) %collective-permute-start.12) | collective-permute-done | bytes 524320 | tf_op jit(solution)/shard_map/ppermute | solution.py:79
  72.1 4.3 %collective-permute-done.13.refs_1_ = bf16[128,2816]{1,0:T(8,128)(2,1)S(1)} collective-permute-done((bf16[128,2816]{1,0:T(8,128)(2,1)S(1)}, bf16[128,2816]{1,0:T(8,128)(2,1)S(1)}, u32[]{:S(2)}, u32[]{:S(2)}) %collective-permute-start.13) | collective-permute-done | bytes 720928 | tf_op jit(solution)/shard_map/ppermute | solution.py:79
  78.0 3.4 %collective-permute-done.14.other_a = bf16[256,2048]{1,0:T(8,128)(2,1)S(1)} collective-permute-done((bf16[256,2048]{1,0:T(8,128)(2,1)S(1)}, bf16[256,2048]{1,0:T(8,128)(2,1)S(1)}, u32[]{:S(2)}, u32[]{:S(2)}) %collective-permute-start.14) | collective-permute-done | bytes 1048608 | tf_op jit(solution)/shard_map/ppermute | solution.py:79
  83.5 16.4 %feed_rows.1 = (bf16[1024,512]{1,0:T(8,128)(2,1)}, f32[1024,512]{1,0:T(8,128)}, bf16[1024,512]{1,0:T(8,128)(2,1)}, bf16[1024,2048]{1,0:T(8,128)(2,1)}, bf16[1024...) custom-call(s32[32]{0:T(128)} %get-tuple-element.180.starts_a, ...), custom_call_target="tpu_custom_call" | custom-call | flops 2000000000 | bytes 53477376 | tf_op jit(solution)/shard_map/feed_rows/pallas_call | solution.py:545
  101.2 12.9 %fetch_codes.1.refs_1_.carried = bf16[8,1024,256]{2,1,0:T(8,128)(2,1)S(1)} custom-call(s32[1]{0:T(128)S(6)} %copy.47.active, s32[16,1024]{1,0:T(8,128)S(1)} %pad_add_fusion.codes.refs_0_, f32[1024,256]{1,0:T(8,128)S(1)} %copy-done.20, bf16[8,2048,256]{2,1,0:T(8,128)(2,1)} %all-gather.2.cloned.1.call-done.book), custom_call_target="tpu_custom_call" | custom-call | flops 2000000000 | bytes 40894464 | tf_op jit(solution)/shard_map/fetch_codes/pallas_call | solution.py:601
  114.1 5.1 %spread_codes.2 = (bf16[4,1024,256]{2,1,0:T(8,128)(2,1)S(1)}, bf16[4,1024,256]{2,1,0:T(8,128)(2,1)S(1)}) custom-call(s32[16,1024]{1,0:T(8,128)S(1)} %pad_add_fusion.codes.refs_0_, bf16[8,1024,256]{2,1,0:T(8,128)(2,1)S(1)} %fetch_codes.1.refs_1_.carried), custom_call_target="tpu_custom_call" | custom-call | flops 500000000 | bytes 15728640 | tf_op jit(solution)/shard_map/spread_codes/pallas_call | solution.py:640
  119.5 5.1 %spread_codes.3 = (bf16[4,1024,256]{2,1,0:T(8,128)(2,1)S(1)}, bf16[4,1024,256]{2,1,0:T(8,128)(2,1)S(1)}) custom-call(s32[16,1024]{1,0:T(8,128)S(1)} %pad_add_fusion.codes.refs_0_, bf16[8,1024,256]{2,1,0:T(8,128)(2,1)S(1)} %fetch_codes.1.refs_1_.carried), custom_call_target="tpu_custom_call" | custom-call | flops 500000000 | bytes 15728640 | tf_op jit(solution)/shard_map/spread_codes/pallas_call | solution.py:640
  133.3 21.6 %feed_back.1 = (f32[1024,512]{1,0:T(8,128)}, bf16[1024,512]{1,0:T(8,128)(2,1)}, f32[8,512]{1,0:T(8,128)}, bf16[1,256,2304]{2,1,0:T(8,128)(2,1)}, bf16[1,256,2304...) custom-call(s32[32]{0:T(128)} %get-tuple-element.189.dests_a, s32[1,128]{1,0:T(1,128)} %copy-done.30, ...), custom_call_target="tpu_custom_call" | custom-call | flops 1000000000 | bytes 78643200 | tf_op jit(solution)/shard_map/feed_back/pallas_call | solution.py:720
  161.5 3.5 %attend_back.3 = (bf16[256,512]{1,0:T(8,128)(2,1)S(1)}, f32[512,512]{1,0:T(8,128)S(1)}, f32[512,512]{1,0:T(8,128)S(1)}, bf16[512,512]{1,0:T(8,128)(2,1)S(1)}) custom-call(bf16[1280,512]{1,0:T(8,128)(2,1)S(1)} %get-tuple-element.203.k.refs_0_.refs_1_.refs_2_, bf16[1280,512]{1,0:T(8,128)(2,1)S(1)} %get-tuple-element.203.k.refs_0_.refs_1_.refs_2_, ...), custom_call_target="tpu_custom_call" | custom-call | flops 4000000000 | bytes 12582912 | tf_op jit(solution)/shard_map/attend_back/pallas_call | solution.py:810
  167.3 4.3 %attend_back.4 = (bf16[256,512]{1,0:T(8,128)(2,1)S(1)}, f32[512,512]{1,0:T(8,128)S(1)}, f32[512,512]{1,0:T(8,128)S(1)}, bf16[512,512]{1,0:T(8,128)(2,1)}) custom-call(bf16[1280,512]{1,0:T(8,128)(2,1)S(1)} %get-tuple-element.203.k.refs_0_.refs_1_.refs_2_, bf16[1280,512]{1,0:T(8,128)(2,1)S(1)} %get-tuple-element.203.k.refs_0_.refs_1_.refs_2_, ...), custom_call_target="tpu_custom_call" | custom-call | bytes 12582912 | tf_op jit(solution)/shard_map/attend_back/pallas_call | solution.py:810
  176.3 8.1 %attend_back.5 = (bf16[512,512]{1,0:T(8,128)(2,1)S(1)}, f32[768,512]{1,0:T(8,128)S(1)}, f32[768,512]{1,0:T(8,128)S(1)}, bf16[512,512]{1,0:T(8,128)(2,1)}) custom-call(bf16[1280,512]{1,0:T(8,128)(2,1)S(1)} %get-tuple-element.203.k.refs_0_.refs_1_.refs_2_, bf16[1280,512]{1,0:T(8,128)(2,1)S(1)} %get-tuple-element.203.k.refs_0_.refs_1_.refs_2_, ...), custom_call_target="tpu_custom_call" | custom-call | bytes 25165824 | tf_op jit(solution)/shard_map/attend_back/pallas_call | solution.py:810
  190.1 7.9 %finish_rows.1 = (f32[1024,512]{1,0:T(8,128)}, bf16[1,256,768]{2,1,0:T(8,128)(2,1)S(1)}, bf16[1,256,768]{2,1,0:T(8,128)(2,1)S(1)}, bf16[1,256,896]{2,1,0:T(8,128)(2,1)S(1)}, bf16[1,256,896]{2,1,0:T(8,128)(2,1)S(1)}) custom-call(s32[32]{0:T(128)S(1)} %get-tuple-element.188.dests, s32[1,128]{1,0:T(1,128)S(1)} %copy-done.31, bf16[1024,512]{1,0:T(8,128)(2,1)S(1)} %copy-done.12, ...), custom_call_target="tpu_custom_call" | custom-call | bytes 31457280 | tf_op jit(solution)/shard_map/finish_rows/pallas_call | solution.py:909
  198.0 2.7 %collective-permute-start.33 = (bf16[1,256,768]{2,1,0:T(8,128)(2,1)S(1)}, bf16[1,256,768]{2,1,0:T(8,128)(2,1)S(1)}, u32[]{:S(2)}, u32[]{:S(2)}) collective-permute-start(bf16[1,256,768]{2,1,0:T(8,128)(2,1)S(1)} %get-tuple-element.292), channel_id=1, source_target_pairs={{0,1},{1,0},{2,3},{3,2},{4,5},{5,4},{6,7},{7,6},{8,9},{9,8},{10,11... | collective-permute-start | bytes 1179656 | tf_op jit(solution)/shard_map/ppermute | solution.py:79
  203.9 2.7 %collective-permute-start.37 = (bf16[1,64,1664]{2,1,0:T(8,128)(2,1)S(1)}, bf16[1,64,1664]{2,1,0:T(8,128)(2,1)S(1)}, u32[]{:S(2)}, u32[]{:S(2)}) collective-permute-start(bf16[1,64,1664]{2,1,0:T(8,128)(2,1)S(1)} %get-tuple-element.300), channel_id=1, source_target_pairs={{0,6},{1,7},{2,4},{3,5},{4,2},{5,3},{6,0},{7,1},{8,14},{9,15},{10,... | collective-permute-start | bytes 638984 | tf_op jit(solution)/shard_map/ppermute | solution.py:79
  206.6 4.7 %collective-permute-done.31.refs_1_ = bf16[1,32,4864]{2,1,0:T(8,128)(2,1)S(1)} collective-permute-done((bf16[1,32,4864]{2,1,0:T(8,128)(2,1)S(1)}, bf16[1,32,4864]{2,1,0:T(8,128)(2,1)S(1)}, u32[]{:S(2)}, u32[]{:S(2)}) %collective-permute-start.31) | collective-permute-done | bytes 311328 | tf_op jit(solution)/shard_map/ppermute | solution.py:79
  211.9 4.5 %collective-permute-done.37.refs_3_ = bf16[1,64,1664]{2,1,0:T(8,128)(2,1)S(1)} collective-permute-done((bf16[1,64,1664]{2,1,0:T(8,128)(2,1)S(1)}, bf16[1,64,1664]{2,1,0:T(8,128)(2,1)S(1)}, u32[]{:S(2)}, u32[]{:S(2)}) %collective-permute-start.37) | collective-permute-done | bytes 213024 | tf_op jit(solution)/shard_map/ppermute | solution.py:79
  217.6 3.3 %collective-permute-start.40 = (bf16[1,16,1664]{2,1,0:T(8,128)(2,1)S(1)}, bf16[1,16,1664]{2,1,0:T(8,128)(2,1)S(1)}, u32[]{:S(2)}, u32[]{:S(2)}) collective-permute-start(bf16[1,16,1664]{2,1,0:T(8,128)(2,1)S(1)} %get-tuple-element.304), channel_id=1, source_target_pairs={{0,24},{1,25},{2,26},{3,27},{4,28},{5,29},{6,30},{7,31},{8,16},{9,... | collective-permute-start | bytes 159752 | tf_op jit(solution)/shard_map/ppermute | solution.py:79
  226.0 9.2 %all_to_all.11 = f32[32,1,128]{2,1,0:T(1,128)S(1)} all-to-all(f32[32,1,128]{2,1,0:T(1,128)S(1)} %bitcast.9), channel_id=1, replica_groups=mesh['clip'=8,'tm'=4] {'clip','tm'}, dimensions={0} | all-to-all | bytes 32768 | tf_op jit(solution)/shard_map/all_to_all | solution.py:1220
  (215 shorter events, 75.2 us)
Async XLA Ops:
  7.2 92.7 %all-gather.2.cloned.1.call-start = ((), (), s32[]{:S(2)}) async-start(), calls=%async_computation.1 | async-start | bytes 8650752 | tf_op jit(solution)/shard_map/all_gather | solution.py:1097
  14.9 16.4 %collective-permute-start.8 = (bf16[16,4864]{1,0:T(8,128)(2,1)}, bf16[16,4864]{1,0:T(8,128)(2,1)S(1)}, u32[]{:S(2)}, u32[]{:S(2)}) collective-permute-start(bf16[16,4864]{1,0:T(8,128)(2,1)} %get-tuple-element.196.refs_0_), channel_id=1, source_target_pairs={{0,16},{1,17},{2,18},{3,19},{4,20},{5,21},{6,22},{7,23},{8,24},{9,... | collective-permute-start | bytes 466952 | tf_op jit(solution)/shard_map/ppermute | solution.py:79
  22.5 12.1 %collective-permute-start.4 = (bf16[64,1664]{1,0:T(8,128)(2,1)S(1)}, bf16[64,1664]{1,0:T(8,128)(2,1)S(1)}, u32[]{:S(2)}, u32[]{:S(2)}) collective-permute-start(bf16[64,1664]{1,0:T(8,128)(2,1)S(1)} %join_rows.8.refs_0_), channel_id=1, source_target_pairs={{0,2},{1,3},{2,0},{3,1},{4,6},{5,7},{6,4},{7,5},{8,10},{9,11},{10,... | collective-permute-start | bytes 638984 | tf_op jit(solution)/shard_map/ppermute | solution.py:79
  24.1 10.5 %collective-permute-start.5 = (bf16[64,1664]{1,0:T(8,128)(2,1)S(1)}, bf16[64,1664]{1,0:T(8,128)(2,1)S(1)}, u32[]{:S(2)}, u32[]{:S(2)}) collective-permute-start(bf16[64,1664]{1,0:T(8,128)(2,1)S(1)} %join_rows.8.refs_0_), channel_id=1, source_target_pairs={{0,4},{1,5},{2,6},{3,7},{4,0},{5,1},{6,2},{7,3},{8,12},{9,13},{10,... | collective-permute-start | bytes 638984 | tf_op jit(solution)/shard_map/ppermute | solution.py:79
  40.5 13.3 %collective-permute-start.11 = (bf16[64,2816]{1,0:T(8,128)(2,1)S(1)}, bf16[64,2816]{1,0:T(8,128)(2,1)S(1)}, u32[]{:S(2)}, u32[]{:S(2)}) collective-permute-start(bf16[64,2816]{1,0:T(8,128)(2,1)S(1)} %get-tuple-element.200.refs_0_), channel_id=1, source_target_pairs={{0,2},{1,3},{2,0},{3,1},{4,6},{5,7},{6,4},{7,5},{8,10},{9,11},{10,... | collective-permute-start | bytes 1081352 | tf_op jit(solution)/shard_map/ppermute | solution.py:79
  42.0 11.8 %collective-permute-start.10 = (bf16[64,2048]{1,0:T(8,128)(2,1)S(1)}, bf16[64,2048]{1,0:T(8,128)(2,1)S(1)}, u32[]{:S(2)}, u32[]{:S(2)}) collective-permute-start(bf16[64,2048]{1,0:T(8,128)(2,1)S(1)} %get-tuple-element.199.refs_0_), channel_id=1, source_target_pairs={{0,4},{1,5},{2,6},{3,7},{4,0},{5,1},{6,2},{7,3},{8,12},{9,13},{10,... | collective-permute-start | bytes 786440 | tf_op jit(solution)/shard_map/ppermute | solution.py:79
  53.8 22.7 %collective-permute-start.13 = (bf16[128,2816]{1,0:T(8,128)(2,1)S(1)}, bf16[128,2816]{1,0:T(8,128)(2,1)S(1)}, u32[]{:S(2)}, u32[]{:S(2)}) collective-permute-start(bf16[128,2816]{1,0:T(8,128)(2,1)S(1)} %join_rows.13.refs_0_), channel_id=1, source_target_pairs={{0,4},{1,5},{2,6},{3,7},{4,0},{5,1},{6,2},{7,3},{8,12},{9,13},{10,... | collective-permute-start | bytes 2162696 | tf_op jit(solution)/shard_map/ppermute | solution.py:79
  56.0 16.1 %collective-permute-start.12 = (bf16[128,2048]{1,0:T(8,128)(2,1)S(1)}, bf16[128,2048]{1,0:T(8,128)(2,1)S(1)}, u32[]{:S(2)}, u32[]{:S(2)}) collective-permute-start(bf16[128,2048]{1,0:T(8,128)(2,1)S(1)} %join_rows.12.refs_0_), channel_id=1, source_target_pairs={{0,2},{1,3},{2,0},{3,1},{4,6},{5,7},{6,4},{7,5},{8,10},{9,11},{10,... | collective-permute-start | bytes 1572872 | tf_op jit(solution)/shard_map/ppermute | solution.py:79
  126.7 28.8 %collective-permute-start.19 = (bf16[4,512,256]{2,1,0:T(8,128)(2,1)}, bf16[4,512,256]{2,1,0:T(8,128)(2,1)S(1)}, u32[]{:S(2)}, u32[]{:S(2)}) collective-permute-start(bf16[4,512,256]{2,1,0:T(8,128)(2,1)} %get-tuple-element.233), channel_id=1, source_target_pairs={{0,4},{1,5},{2,6},{3,7},{4,0},{5,1},{6,2},{7,3},{8,12},{9,13},{10,... | collective-permute-start | bytes 3145736 | tf_op jit(solution)/shard_map/ppermute | solution.py:79
  130.9 26.1 %collective-permute-start.18 = (bf16[4,512,256]{2,1,0:T(8,128)(2,1)}, bf16[4,512,256]{2,1,0:T(8,128)(2,1)S(1)}, u32[]{:S(2)}, u32[]{:S(2)}) collective-permute-start(bf16[4,512,256]{2,1,0:T(8,128)(2,1)} %get-tuple-element.232), channel_id=1, source_target_pairs={{0,2},{1,3},{2,0},{3,1},{4,6},{5,7},{6,4},{7,5},{8,10},{9,11},{10,... | collective-permute-start | bytes 3145736 | tf_op jit(solution)/shard_map/ppermute | solution.py:79
  154.9 10.2 %collective-permute-start.21 = (bf16[1,256,2560]{2,1,0:T(8,128)(2,1)}, bf16[1,256,2560]{2,1,0:T(8,128)(2,1)S(1)}, u32[]{:S(2)}, u32[]{:S(2)}) collective-permute-start(bf16[1,256,2560]{2,1,0:T(8,128)(2,1)} %get-tuple-element.243), channel_id=1, source_target_pairs={{0,1},{1,0},{2,3},{3,2},{4,5},{5,4},{6,7},{7,6},{8,9},{9,8},{10,11... | collective-permute-start | bytes 3932168 | tf_op jit(solution)/shard_map/ppermute | solution.py:79
  155.0 10.1 %collective-permute-start.20 = (bf16[1,256,2304]{2,1,0:T(8,128)(2,1)}, bf16[1,256,2304]{2,1,0:T(8,128)(2,1)S(1)}, u32[]{:S(2)}, u32[]{:S(2)}) collective-permute-start(bf16[1,256,2304]{2,1,0:T(8,128)(2,1)} %get-tuple-element.242), channel_id=1, source_target_pairs={{0,1},{1,0},{2,3},{3,2},{4,5},{5,4},{6,7},{7,6},{8,9},{9,8},{10,11... | collective-permute-start | bytes 3538952 | tf_op jit(solution)/shard_map/ppermute | solution.py:79
  157.2 15.2 %collective-permute-start.22 = (bf16[4,256,256]{2,1,0:T(8,128)(2,1)S(1)}, bf16[4,256,256]{2,1,0:T(8,128)(2,1)S(1)}, u32[]{:S(2)}, u32[]{:S(2)}) collective-permute-start(bf16[4,256,256]{2,1,0:T(8,128)(2,1)S(1)} %get-tuple-element.253), channel_id=1, source_target_pairs={{0,4},{1,5},{2,6},{3,7},{4,0},{5,1},{6,2},{7,3},{8,12},{9,13},{10,... | collective-permute-start | bytes 1572872 | tf_op jit(solution)/shard_map/ppermute | solution.py:79
  159.7 14.9 %collective-permute-start.23 = (bf16[4,256,256]{2,1,0:T(8,128)(2,1)S(1)}, bf16[4,256,256]{2,1,0:T(8,128)(2,1)S(1)}, u32[]{:S(2)}, u32[]{:S(2)}) collective-permute-start(bf16[4,256,256]{2,1,0:T(8,128)(2,1)S(1)} %get-tuple-element.254), channel_id=1, source_target_pairs={{0,2},{1,3},{2,0},{3,1},{4,6},{5,7},{6,4},{7,5},{8,10},{9,11},{10,... | collective-permute-start | bytes 1572872 | tf_op jit(solution)/shard_map/ppermute | solution.py:79
  165.8 19.9 %collective-permute-start.26 = (bf16[1,128,2560]{2,1,0:T(8,128)(2,1)S(1)}, bf16[1,128,2560]{2,1,0:T(8,128)(2,1)S(1)}, u32[]{:S(2)}, u32[]{:S(2)}) collective-permute-start(bf16[1,128,2560]{2,1,0:T(8,128)(2,1)S(1)} %get-tuple-element.265), channel_id=1, source_target_pairs={{0,4},{1,5},{2,6},{3,7},{4,0},{5,1},{6,2},{7,3},{8,12},{9,13},{10,... | collective-permute-start | bytes 1966088 | tf_op jit(solution)/shard_map/ppermute | solution.py:79
  167.0 18.7 %collective-permute-start.25 = (bf16[1,128,2304]{2,1,0:T(8,128)(2,1)S(1)}, bf16[1,128,2304]{2,1,0:T(8,128)(2,1)S(1)}, u32[]{:S(2)}, u32[]{:S(2)}) collective-permute-start(bf16[1,128,2304]{2,1,0:T(8,128)(2,1)S(1)} %get-tuple-element.264), channel_id=1, source_target_pairs={{0,2},{1,3},{2,0},{3,1},{4,6},{5,7},{6,4},{7,5},{8,10},{9,11},{10,... | collective-permute-start | bytes 1769480 | tf_op jit(solution)/shard_map/ppermute | solution.py:79
  174.9 11.0 %collective-permute-start.24 = (bf16[8,128,256]{2,1,0:T(8,128)(2,1)S(1)}, bf16[8,128,256]{2,1,0:T(8,128)(2,1)S(1)}, u32[]{:S(2)}, u32[]{:S(2)}) collective-permute-start(bf16[8,128,256]{2,1,0:T(8,128)(2,1)S(1)} %get-tuple-element.263), channel_id=1, source_target_pairs={{0,8},{1,9},{2,10},{3,11},{4,12},{5,13},{6,14},{7,15},{8,0},{9,1},... | collective-permute-start | bytes 1572872 | tf_op jit(solution)/shard_map/ppermute | solution.py:79
  175.0 15.1 %collective-permute-start.27 = (bf16[512,512]{1,0:T(8,128)(2,1)S(1)}, bf16[512,512]{1,0:T(8,128)(2,1)S(1)}, u32[]{:S(2)}, u32[]{:S(2)}) collective-permute-start(bf16[512,512]{1,0:T(8,128)(2,1)S(1)} %get-tuple-element.274), channel_id=1, source_target_pairs={{1,0},{2,1},{3,2},{5,4},{6,5},{7,6},{9,8},{10,9},{11,10},{13,12},{... | collective-permute-start | bytes 1572872 | tf_op jit(solution)/shard_map/ppermute | solution.py:1181
  186.1 14.6 %collective-permute-start.28 = (bf16[8,64,256]{2,1,0:T(8,128)(2,1)S(1)}, bf16[8,64,256]{2,1,0:T(8,128)(2,1)S(1)}, u32[]{:S(2)}, u32[]{:S(2)}) collective-permute-start(bf16[8,64,256]{2,1,0:T(8,128)(2,1)S(1)} %get-tuple-element.279), channel_id=1, source_target_pairs={{0,16},{1,17},{2,18},{3,19},{4,20},{5,21},{6,22},{7,23},{8,24},{9,... | collective-permute-start | bytes 786440 | tf_op jit(solution)/shard_map/ppermute | solution.py:79
  186.6 14.8 %collective-permute-start.30 = (bf16[1,64,2560]{2,1,0:T(8,128)(2,1)S(1)}, bf16[1,64,2560]{2,1,0:T(8,128)(2,1)S(1)}, u32[]{:S(2)}, u32[]{:S(2)}) collective-permute-start(bf16[1,64,2560]{2,1,0:T(8,128)(2,1)S(1)} %get-tuple-element.284), channel_id=1, source_target_pairs={{0,2},{1,3},{2,0},{3,1},{4,6},{5,7},{6,4},{7,5},{8,10},{9,11},{10,... | collective-permute-start | bytes 983048 | tf_op jit(solution)/shard_map/ppermute | solution.py:79
  189.1 12.3 %collective-permute-start.29 = (bf16[1,64,2304]{2,1,0:T(8,128)(2,1)S(1)}, bf16[1,64,2304]{2,1,0:T(8,128)(2,1)S(1)}, u32[]{:S(2)}, u32[]{:S(2)}) collective-permute-start(bf16[1,64,2304]{2,1,0:T(8,128)(2,1)S(1)} %get-tuple-element.283), channel_id=1, source_target_pairs={{0,4},{1,5},{2,6},{3,7},{4,0},{5,1},{6,2},{7,3},{8,12},{9,13},{10,... | collective-permute-start | bytes 884744 | tf_op jit(solution)/shard_map/ppermute | solution.py:79
  201.5 9.8 %collective-permute-start.31 = (bf16[1,32,4864]{2,1,0:T(8,128)(2,1)S(1)}, bf16[1,32,4864]{2,1,0:T(8,128)(2,1)S(1)}, u32[]{:S(2)}, u32[]{:S(2)}) collective-permute-start(bf16[1,32,4864]{2,1,0:T(8,128)(2,1)S(1)} %get-tuple-element.289), channel_id=1, source_target_pairs={{0,8},{1,9},{2,10},{3,11},{4,12},{5,13},{6,14},{7,15},{8,0},{9,1},... | collective-permute-start | bytes 933896 | tf_op jit(solution)/shard_map/ppermute | solution.py:79
  203.9 12.5 %collective-permute-start.37 = (bf16[1,64,1664]{2,1,0:T(8,128)(2,1)S(1)}, bf16[1,64,1664]{2,1,0:T(8,128)(2,1)S(1)}, u32[]{:S(2)}, u32[]{:S(2)}) collective-permute-start(bf16[1,64,1664]{2,1,0:T(8,128)(2,1)S(1)} %get-tuple-element.300), channel_id=1, source_target_pairs={{0,6},{1,7},{2,4},{3,5},{4,2},{5,3},{6,0},{7,1},{8,14},{9,15},{10,... | collective-permute-start | bytes 638984 | tf_op jit(solution)/shard_map/ppermute | solution.py:79
  211.6 13.4 %collective-permute-start.32 = (bf16[1,16,4864]{2,1,0:T(8,128)(2,1)S(1)}, bf16[1,16,4864]{2,1,0:T(8,128)(2,1)S(1)}, u32[]{:S(2)}, u32[]{:S(2)}) collective-permute-start(bf16[1,16,4864]{2,1,0:T(8,128)(2,1)S(1)} %get-tuple-element.291), channel_id=1, source_target_pairs={{0,16},{1,17},{2,18},{3,19},{4,20},{5,21},{6,22},{7,23},{8,24},{9,... | collective-permute-start | bytes 466952 | tf_op jit(solution)/shard_map/ppermute | solution.py:79
  (67 other events, 864.3 us)
Sparse Core Ops, SparseCore 0:
  11.6 86.6 all-gather.1

commit v5 on v4

--- a/solution.py
+++ b/solution.py
@@ -161,7 +161,8 @@
     lead, rows, columns = keep.shape
     size = rows // radix
     if lead > 1:
-        steps, block, index = lead, (1, rows, columns), lambda i: (i, 0, 0)
+        group = 2 if held == bf16 else 1
+        steps, block, index = lead // group, (group, rows, columns), lambda i: (i, 0, 0)
     else:
         steps = 2 if columns % 256 == 0 else 1
         block, index = (1, rows, columns // steps), lambda i: (0, 0, i)
@@ -684,7 +685,7 @@
     sums[2:3, :] += column_sum(grad_normed * normal)
     sums[3:4, :] += column_sum(grad_normed)
     grad_first = grad_after + norm_back(normal, rstd, scales[2:3, :], grad_normed)
-    out_after[...] = grad_first
+    out_after[...] = grad_first.astype(bf16)
     sums[4:5, :] += column_sum(grad_first * branch_first[...].astype(f32))
     low_first = (grad_first * scales[4:5, :]).astype(bf16)
     grad_branch[rows, :] = low_first
@@ -726,7 +727,7 @@
         + [row(width), whole(scales.shape), whole(weights.shape)],
         out_specs=[row(width), row(width), whole((8, width))] + [whole(piece) for piece in pieces],
         out_shape=[
-            jax.ShapeDtypeStruct((count, width), f32),
+            jax.ShapeDtypeStruct((count, width), bf16),
             jax.ShapeDtypeStruct((count, width), bf16),
             jax.ShapeDtypeStruct((8, width), f32),
         ]
@@ -875,7 +876,7 @@
     normal, rstd = centre_rows(inputs[...].astype(f32))
     sums[0:1, :] += column_sum(grad * normal)
     sums[1:2, :] += column_sum(grad)
-    out[...] = grad_after[...] + norm_back(normal, rstd, scales[0:1, :], grad)
+    out[...] = grad_after[...].astype(f32) + norm_back(normal, rstd, scales[0:1, :], grad)
 
     store_flipped(dests, rowmap, normed[...], flipped, rows)
 

time: 245 us -> 244 us (level)
  transfers between devices with their start and end apart: 42 -> 42, of which waited for: 19 -> 20; matrix products, arithmetic and copies ran while one was open for 2% -> 2% of each run, Pallas kernels for 37% -> 36%
where the time goes in v5:
time: 244 us
  Pallas kernels  112 us (46%)
  starting transfers between devices  50.8 us (21%)
  waiting for transfers between devices  45.6 us (19%)
  between operations  15.7 us (6%)
  blocking collectives  9.18 us (4%)
  local copies, waits for them, and re-layouts  5.49 us (2%)
  other arithmetic  5.22 us (2%)
    ppermute x39, starting transfers between devices, swap(): return lax.ppermute(block, AXES, [(i, i ^ mask) for i in range(count)])  46.9 us
    ppermute x39, waiting for transfers between devices, swap(): return lax.ppermute(block, AXES, [(i, i ^ mask) for i in range(count)])  45.5 us
    pallas_call x1, Pallas kernels, backward_call(): pl.pallas_call(backward_kernel, grid=(count // ROWS,), in_specs=[smem(),...  21.5 us
    pallas_call x1, Pallas kernels, forward_call(): pl.pallas_call(forward_kernel, grid=(count // ROWS,), in_specs=[smem(), w...  16.5 us
    pallas_call x3, Pallas kernels, attend_back_call(): pl.pallas_call(lambda *refs: attend_back_kernel(pieces, *refs), grid=(blo...  16 us
    pallas_call x1, Pallas kernels, fetch_call(): pl.pallas_call(fetch_kernel, grid=(LEVELS,), in_specs=[smem(), whole(code...  12.9 us
    pallas_call x2, Pallas kernels, spread_call(): pl.pallas_call(lambda *refs: spread_kernel(first, *refs), grid=(levels,),...  10.2 us
    all_to_all x1, blocking collectives, body(): shared = lax.all_to_all(shared, AXES, 0, 0, tiled=True)  9.18 us
  transfers between devices with their start and end apart: 42, of which 20 were waited for; matrix products, arithmetic and copies ran while one was open for 2% of the time, Pallas kernels for 36%

profile of v5, /device:TPU:0, one launch (start us, length us, event | category | flops | bytes accessed | tf_op | source)
XLA Modules:
  0.0 244.0 jit_solution(4870681991454196483)
XLA Ops:
  9.2 3.1 %collective-permute-start = (bf16[16,1664]{1,0:T(8,128)(2,1)}, bf16[16,1664]{1,0:T(8,128)(2,1)S(1)}, u32[]{:S(2)}, u32[]{:S(2)}) collective-permute-start(bf16[16,1664]{1,0:T(8,128)(2,1)} %get-tuple-element.176.refs_0_), channel_id=1, source_target_pairs={{0,8},{1,9},{2,10},{3,11},{4,12},{5,13},{6,14},{7,15},{8,0},{9,1},... | collective-permute-start | bytes 159752 | tf_op jit(solution)/shard_map/ppermute | solution.py:79
  18.7 3.0 %collective-permute-done.2.refs_3_ = bf16[16,1664]{1,0:T(8,128)(2,1)S(1)} collective-permute-done((bf16[16,1664]{1,0:T(8,128)(2,1)}, bf16[16,1664]{1,0:T(8,128)(2,1)S(1)}, u32[]{:S(2)}, u32[]{:S(2)}) %collective-permute-start.2) | collective-permute-done | bytes 53280 | tf_op jit(solution)/shard_map/ppermute | solution.py:79
  31.3 3.3 %collective-permute-start.9 = (bf16[32,4864]{1,0:T(8,128)(2,1)S(1)}, bf16[32,4864]{1,0:T(8,128)(2,1)S(1)}, u32[]{:S(2)}, u32[]{:S(2)}) collective-permute-start(bf16[32,4864]{1,0:T(8,128)(2,1)S(1)} %join_rows.10.refs_0_), channel_id=1, source_target_pairs={{0,8},{1,9},{2,10},{3,11},{4,12},{5,13},{6,14},{7,15},{8,0},{9,1},... | collective-permute-start | bytes 933896 | tf_op jit(solution)/shard_map/ppermute | solution.py:79
  43.2 6.2 %project_rows.1 = (bf16[1024,512]{1,0:T(8,128)(2,1)S(1)}, bf16[1024,512]{1,0:T(8,128)(2,1)S(1)}, bf16[1280,512]{1,0:T(8,128)(2,1)S(1)}, bf16[1280,512]{1,0:T(8,1...) custom-call(s32[32]{0:T(128)S(1)} %get-tuple-element.184.starts, ...), custom_call_target="tpu_custom_call" | custom-call | flops 2000000000 | bytes 25165824 | tf_op jit(solution)/shard_map/project_rows/pallas_call | solution.py:415
  50.0 3.8 %collective-permute-done.10.refs_1_ = bf16[64,2048]{1,0:T(8,128)(2,1)S(1)} collective-permute-done((bf16[64,2048]{1,0:T(8,128)(2,1)S(1)}, bf16[64,2048]{1,0:T(8,128)(2,1)S(1)}, u32[]{:S(2)}, u32[]{:S(2)}) %collective-permute-start.10) | collective-permute-done | bytes 262176 | tf_op jit(solution)/shard_map/ppermute | solution.py:79
  57.7 8.5 %attend_rows.1 = (bf16[1024,512]{1,0:T(8,128)(2,1)S(1)}, f32[8,1024]{1,0:T(8,128)S(1)}) custom-call(bf16[1024,512]{1,0:T(8,128)(2,1)S(1)} %get-tuple-element.194.q.refs_4_.refs_6_, bf16[1280,512]{1,0:T(8,128)(2,1)S(1)} %get-tuple-element.203.k.refs_0_.refs_1_.refs_2_, bf16[1280,512]{1,0:T(8,128)(2,1)S(1)} %get-tuple-element.204.v.refs_2_.refs_3_.refs_4_.refs_5_, ...), custom_call_target="tpu_custom_call" | custom-call | flops 2000000000 | bytes 44040192 | tf_op jit(solution)/shard_map/attend_rows/pallas_call | solution.py:476
  66.2 5.9 %collective-permute-done.12.refs_1_ = bf16[128,2048]{1,0:T(8,128)(2,1)S(1)} collective-permute-done((bf16[128,2048]{1,0:T(8,128)(2,1)S(1)}, bf16[128,2048]{1,0:T(8,128)(2,1)S(1)}, u32[]{:S(2)}, u32[]{:S(2)}) %collective-permute-start.12) | collective-permute-done | bytes 524320 | tf_op jit(solution)/shard_map/ppermute | solution.py:79
  72.1 4.3 %collective-permute-done.13.refs_1_ = bf16[128,2816]{1,0:T(8,128)(2,1)S(1)} collective-permute-done((bf16[128,2816]{1,0:T(8,128)(2,1)S(1)}, bf16[128,2816]{1,0:T(8,128)(2,1)S(1)}, u32[]{:S(2)}, u32[]{:S(2)}) %collective-permute-start.13) | collective-permute-done | bytes 720928 | tf_op jit(solution)/shard_map/ppermute | solution.py:79
  78.0 3.4 %collective-permute-done.14.other_a = bf16[256,2048]{1,0:T(8,128)(2,1)S(1)} collective-permute-done((bf16[256,2048]{1,0:T(8,128)(2,1)S(1)}, bf16[256,2048]{1,0:T(8,128)(2,1)S(1)}, u32[]{:S(2)}, u32[]{:S(2)}) %collective-permute-start.14) | collective-permute-done | bytes 1048608 | tf_op jit(solution)/shard_map/ppermute | solution.py:79
  83.5 16.5 %feed_rows.1 = (bf16[1024,512]{1,0:T(8,128)(2,1)}, f32[1024,512]{1,0:T(8,128)}, bf16[1024,512]{1,0:T(8,128)(2,1)}, bf16[1024,2048]{1,0:T(8,128)(2,1)}, bf16[1024...) custom-call(s32[32]{0:T(128)} %get-tuple-element.180.starts_a, ...), custom_call_target="tpu_custom_call" | custom-call | flops 2000000000 | bytes 53477376 | tf_op jit(solution)/shard_map/feed_rows/pallas_call | solution.py:546
  101.2 12.9 %fetch_codes.1.refs_1_.carried = bf16[8,1024,256]{2,1,0:T(8,128)(2,1)S(1)} custom-call(s32[1]{0:T(128)S(6)} %copy.47.active, s32[16,1024]{1,0:T(8,128)S(1)} %pad_add_fusion.codes.refs_0_, f32[1024,256]{1,0:T(8,128)S(1)} %copy-done.20, bf16[8,2048,256]{2,1,0:T(8,128)(2,1)} %all-gather.2.cloned.1.call-done.book), custom_call_target="tpu_custom_call" | custom-call | flops 2000000000 | bytes 40894464 | tf_op jit(solution)/shard_map/fetch_codes/pallas_call | solution.py:602
  114.2 5.1 %spread_codes.2 = (bf16[4,1024,256]{2,1,0:T(8,128)(2,1)S(1)}, bf16[4,1024,256]{2,1,0:T(8,128)(2,1)S(1)}) custom-call(s32[16,1024]{1,0:T(8,128)S(1)} %pad_add_fusion.codes.refs_0_, bf16[8,1024,256]{2,1,0:T(8,128)(2,1)S(1)} %fetch_codes.1.refs_1_.carried), custom_call_target="tpu_custom_call" | custom-call | flops 500000000 | bytes 15728640 | tf_op jit(solution)/shard_map/spread_codes/pallas_call | solution.py:641
  119.5 5.1 %spread_codes.3 = (bf16[4,1024,256]{2,1,0:T(8,128)(2,1)S(1)}, bf16[4,1024,256]{2,1,0:T(8,128)(2,1)S(1)}) custom-call(s32[16,1024]{1,0:T(8,128)S(1)} %pad_add_fusion.codes.refs_0_, bf16[8,1024,256]{2,1,0:T(8,128)(2,1)S(1)} %fetch_codes.1.refs_1_.carried), custom_call_target="tpu_custom_call" | custom-call | flops 500000000 | bytes 15728640 | tf_op jit(solution)/shard_map/spread_codes/pallas_call | solution.py:641
  132.6 21.5 %feed_back.1 = (bf16[1024,512]{1,0:T(8,128)(2,1)}, bf16[1024,512]{1,0:T(8,128)(2,1)}, f32[8,512]{1,0:T(8,128)}, bf16[1,256,2304]{2,1,0:T(8,128)(2,1)}, bf16[1,25...) custom-call(s32[32]{0:T(128)} %get-tuple-element.189.dests_a, ...), custom_call_target="tpu_custom_call" | custom-call | flops 1000000000 | bytes 78643200 | tf_op jit(solution)/shard_map/feed_back/pallas_call | solution.py:721
  161.1 3.5 %attend_back.3 = (bf16[256,512]{1,0:T(8,128)(2,1)S(1)}, f32[512,512]{1,0:T(8,128)S(1)}, f32[512,512]{1,0:T(8,128)S(1)}, bf16[512,512]{1,0:T(8,128)(2,1)S(1)}) custom-call(bf16[1280,512]{1,0:T(8,128)(2,1)S(1)} %get-tuple-element.203.k.refs_0_.refs_1_.refs_2_, bf16[1280,512]{1,0:T(8,128)(2,1)S(1)} %get-tuple-element.203.k.refs_0_.refs_1_.refs_2_, ...), custom_call_target="tpu_custom_call" | custom-call | flops 4000000000 | bytes 12582912 | tf_op jit(solution)/shard_map/attend_back/pallas_call | solution.py:811
  166.9 4.3 %attend_back.4 = (bf16[256,512]{1,0:T(8,128)(2,1)S(1)}, f32[512,512]{1,0:T(8,128)S(1)}, f32[512,512]{1,0:T(8,128)S(1)}, bf16[512,512]{1,0:T(8,128)(2,1)}) custom-call(bf16[1280,512]{1,0:T(8,128)(2,1)S(1)} %get-tuple-element.203.k.refs_0_.refs_1_.refs_2_, bf16[1280,512]{1,0:T(8,128)(2,1)S(1)} %get-tuple-element.203.k.refs_0_.refs_1_.refs_2_, ...), custom_call_target="tpu_custom_call" | custom-call | bytes 12582912 | tf_op jit(solution)/shard_map/attend_back/pallas_call | solution.py:811
  175.8 8.1 %attend_back.5 = (bf16[512,512]{1,0:T(8,128)(2,1)S(1)}, f32[768,512]{1,0:T(8,128)S(1)}, f32[768,512]{1,0:T(8,128)S(1)}, bf16[512,512]{1,0:T(8,128)(2,1)}) custom-call(bf16[1280,512]{1,0:T(8,128)(2,1)S(1)} %get-tuple-element.203.k.refs_0_.refs_1_.refs_2_, bf16[1280,512]{1,0:T(8,128)(2,1)S(1)} %get-tuple-element.203.k.refs_0_.refs_1_.refs_2_, ...), custom_call_target="tpu_custom_call" | custom-call | bytes 25165824 | tf_op jit(solution)/shard_map/attend_back/pallas_call | solution.py:811
  189.7 7.9 %finish_rows.1 = (f32[1024,512]{1,0:T(8,128)}, bf16[1,256,768]{2,1,0:T(8,128)(2,1)S(1)}, bf16[1,256,768]{2,1,0:T(8,128)(2,1)S(1)}, bf16[1,256,896]{2,1,0:T(8,128)(2,1)S(1)}, bf16[1,256,896]{2,1,0:T(8,128)(2,1)S(1)}) custom-call(s32[32]{0:T(128)S(1)} %get-tuple-element.188.dests, s32[1,128]{1,0:T(1,128)S(1)} %copy-done.31, bf16[1024,512]{1,0:T(8,128)(2,1)S(1)} %copy-done.11, ...), custom_call_target="tpu_custom_call" | custom-call | bytes 31457280 | tf_op jit(solution)/shard_map/finish_rows/pallas_call | solution.py:910
  197.7 2.7 %collective-permute-start.33 = (bf16[1,256,768]{2,1,0:T(8,128)(2,1)S(1)}, bf16[1,256,768]{2,1,0:T(8,128)(2,1)S(1)}, u32[]{:S(2)}, u32[]{:S(2)}) collective-permute-start(bf16[1,256,768]{2,1,0:T(8,128)(2,1)S(1)} %get-tuple-element.292), channel_id=1, source_target_pairs={{0,1},{1,0},{2,3},{3,2},{4,5},{5,4},{6,7},{7,6},{8,9},{9,8},{10,11... | collective-permute-start | bytes 1179656 | tf_op jit(solution)/shard_map/ppermute | solution.py:79
  203.5 2.7 %collective-permute-start.37 = (bf16[1,64,1664]{2,1,0:T(8,128)(2,1)S(1)}, bf16[1,64,1664]{2,1,0:T(8,128)(2,1)S(1)}, u32[]{:S(2)}, u32[]{:S(2)}) collective-permute-start(bf16[1,64,1664]{2,1,0:T(8,128)(2,1)S(1)} %get-tuple-element.300), channel_id=1, source_target_pairs={{0,6},{1,7},{2,4},{3,5},{4,2},{5,3},{6,0},{7,1},{8,14},{9,15},{10,... | collective-permute-start | bytes 638984 | tf_op jit(solution)/shard_map/ppermute | solution.py:79
  206.3 4.7 %collective-permute-done.31.refs_1_ = bf16[1,32,4864]{2,1,0:T(8,128)(2,1)S(1)} collective-permute-done((bf16[1,32,4864]{2,1,0:T(8,128)(2,1)S(1)}, bf16[1,32,4864]{2,1,0:T(8,128)(2,1)S(1)}, u32[]{:S(2)}, u32[]{:S(2)}) %collective-permute-start.31) | collective-permute-done | bytes 311328 | tf_op jit(solution)/shard_map/ppermute | solution.py:79
  211.5 4.5 %collective-permute-done.37.refs_3_ = bf16[1,64,1664]{2,1,0:T(8,128)(2,1)S(1)} collective-permute-done((bf16[1,64,1664]{2,1,0:T(8,128)(2,1)S(1)}, bf16[1,64,1664]{2,1,0:T(8,128)(2,1)S(1)}, u32[]{:S(2)}, u32[]{:S(2)}) %collective-permute-start.37) | collective-permute-done | bytes 213024 | tf_op jit(solution)/shard_map/ppermute | solution.py:79
  217.2 3.3 %collective-permute-start.40 = (bf16[1,16,1664]{2,1,0:T(8,128)(2,1)S(1)}, bf16[1,16,1664]{2,1,0:T(8,128)(2,1)S(1)}, u32[]{:S(2)}, u32[]{:S(2)}) collective-permute-start(bf16[1,16,1664]{2,1,0:T(8,128)(2,1)S(1)} %get-tuple-element.304), channel_id=1, source_target_pairs={{0,24},{1,25},{2,26},{3,27},{4,28},{5,29},{6,30},{7,31},{8,16},{9,... | collective-permute-start | bytes 159752 | tf_op jit(solution)/shard_map/ppermute | solution.py:79
  225.6 9.2 %all_to_all.11 = f32[32,1,128]{2,1,0:T(1,128)S(1)} all-to-all(f32[32,1,128]{2,1,0:T(1,128)S(1)} %bitcast.9), channel_id=1, replica_groups=mesh['clip'=8,'tm'=4] {'clip','tm'}, dimensions={0} | all-to-all | bytes 32768 | tf_op jit(solution)/shard_map/all_to_all | solution.py:1221
  (215 shorter events, 74.9 us)
Async XLA Ops:
  7.2 92.8 %all-gather.2.cloned.1.call-start = ((), (), s32[]{:S(2)}) async-start(), calls=%async_computation.1 | async-start | bytes 8650752 | tf_op jit(solution)/shard_map/all_gather | solution.py:1098
  14.9 16.4 %collective-permute-start.8 = (bf16[16,4864]{1,0:T(8,128)(2,1)}, bf16[16,4864]{1,0:T(8,128)(2,1)S(1)}, u32[]{:S(2)}, u32[]{:S(2)}) collective-permute-start(bf16[16,4864]{1,0:T(8,128)(2,1)} %get-tuple-element.196.refs_0_), channel_id=1, source_target_pairs={{0,16},{1,17},{2,18},{3,19},{4,20},{5,21},{6,22},{7,23},{8,24},{9,... | collective-permute-start | bytes 466952 | tf_op jit(solution)/shard_map/ppermute | solution.py:79
  22.5 12.1 %collective-permute-start.4 = (bf16[64,1664]{1,0:T(8,128)(2,1)S(1)}, bf16[64,1664]{1,0:T(8,128)(2,1)S(1)}, u32[]{:S(2)}, u32[]{:S(2)}) collective-permute-start(bf16[64,1664]{1,0:T(8,128)(2,1)S(1)} %join_rows.8.refs_0_), channel_id=1, source_target_pairs={{0,2},{1,3},{2,0},{3,1},{4,6},{5,7},{6,4},{7,5},{8,10},{9,11},{10,... | collective-permute-start | bytes 638984 | tf_op jit(solution)/shard_map/ppermute | solution.py:79
  24.1 10.5 %collective-permute-start.5 = (bf16[64,1664]{1,0:T(8,128)(2,1)S(1)}, bf16[64,1664]{1,0:T(8,128)(2,1)S(1)}, u32[]{:S(2)}, u32[]{:S(2)}) collective-permute-start(bf16[64,1664]{1,0:T(8,128)(2,1)S(1)} %join_rows.8.refs_0_), channel_id=1, source_target_pairs={{0,4},{1,5},{2,6},{3,7},{4,0},{5,1},{6,2},{7,3},{8,12},{9,13},{10,... | collective-permute-start | bytes 638984 | tf_op jit(solution)/shard_map/ppermute | solution.py:79
  40.5 13.3 %collective-permute-start.11 = (bf16[64,2816]{1,0:T(8,128)(2,1)S(1)}, bf16[64,2816]{1,0:T(8,128)(2,1)S(1)}, u32[]{:S(2)}, u32[]{:S(2)}) collective-permute-start(bf16[64,2816]{1,0:T(8,128)(2,1)S(1)} %get-tuple-element.200.refs_0_), channel_id=1, source_target_pairs={{0,2},{1,3},{2,0},{3,1},{4,6},{5,7},{6,4},{7,5},{8,10},{9,11},{10,... | collective-permute-start | bytes 1081352 | tf_op jit(solution)/shard_map/ppermute | solution.py:79
  42.0 11.8 %collective-permute-start.10 = (bf16[64,2048]{1,0:T(8,128)(2,1)S(1)}, bf16[64,2048]{1,0:T(8,128)(2,1)S(1)}, u32[]{:S(2)}, u32[]{:S(2)}) collective-permute-start(bf16[64,2048]{1,0:T(8,128)(2,1)S(1)} %get-tuple-element.199.refs_0_), channel_id=1, source_target_pairs={{0,4},{1,5},{2,6},{3,7},{4,0},{5,1},{6,2},{7,3},{8,12},{9,13},{10,... | collective-permute-start | bytes 786440 | tf_op jit(solution)/shard_map/ppermute | solution.py:79
  53.8 22.7 %collective-permute-start.13 = (bf16[128,2816]{1,0:T(8,128)(2,1)S(1)}, bf16[128,2816]{1,0:T(8,128)(2,1)S(1)}, u32[]{:S(2)}, u32[]{:S(2)}) collective-permute-start(bf16[128,2816]{1,0:T(8,128)(2,1)S(1)} %join_rows.13.refs_0_), channel_id=1, source_target_pairs={{0,4},{1,5},{2,6},{3,7},{4,0},{5,1},{6,2},{7,3},{8,12},{9,13},{10,... | collective-permute-start | bytes 2162696 | tf_op jit(solution)/shard_map/ppermute | solution.py:79
  56.0 16.1 %collective-permute-start.12 = (bf16[128,2048]{1,0:T(8,128)(2,1)S(1)}, bf16[128,2048]{1,0:T(8,128)(2,1)S(1)}, u32[]{:S(2)}, u32[]{:S(2)}) collective-permute-start(bf16[128,2048]{1,0:T(8,128)(2,1)S(1)} %join_rows.12.refs_0_), channel_id=1, source_target_pairs={{0,2},{1,3},{2,0},{3,1},{4,6},{5,7},{6,4},{7,5},{8,10},{9,11},{10,... | collective-permute-start | bytes 1572872 | tf_op jit(solution)/shard_map/ppermute | solution.py:79
  126.3 28.4 %collective-permute-start.19 = (bf16[4,512,256]{2,1,0:T(8,128)(2,1)}, bf16[4,512,256]{2,1,0:T(8,128)(2,1)S(1)}, u32[]{:S(2)}, u32[]{:S(2)}) collective-permute-start(bf16[4,512,256]{2,1,0:T(8,128)(2,1)} %get-tuple-element.233), channel_id=1, source_target_pairs={{0,4},{1,5},{2,6},{3,7},{4,0},{5,1},{6,2},{7,3},{8,12},{9,13},{10,... | collective-permute-start | bytes 3145736 | tf_op jit(solution)/shard_map/ppermute | solution.py:79
  130.1 26.4 %collective-permute-start.18 = (bf16[4,512,256]{2,1,0:T(8,128)(2,1)}, bf16[4,512,256]{2,1,0:T(8,128)(2,1)S(1)}, u32[]{:S(2)}, u32[]{:S(2)}) collective-permute-start(bf16[4,512,256]{2,1,0:T(8,128)(2,1)} %get-tuple-element.232), channel_id=1, source_target_pairs={{0,2},{1,3},{2,0},{3,1},{4,6},{5,7},{6,4},{7,5},{8,10},{9,11},{10,... | collective-permute-start | bytes 3145736 | tf_op jit(solution)/shard_map/ppermute | solution.py:79
  154.1 10.6 %collective-permute-start.21 = (bf16[1,256,2560]{2,1,0:T(8,128)(2,1)}, bf16[1,256,2560]{2,1,0:T(8,128)(2,1)S(1)}, u32[]{:S(2)}, u32[]{:S(2)}) collective-permute-start(bf16[1,256,2560]{2,1,0:T(8,128)(2,1)} %get-tuple-element.243), channel_id=1, source_target_pairs={{0,1},{1,0},{2,3},{3,2},{4,5},{5,4},{6,7},{7,6},{8,9},{9,8},{10,11... | collective-permute-start | bytes 3932168 | tf_op jit(solution)/shard_map/ppermute | solution.py:79
  154.3 10.4 %collective-permute-start.20 = (bf16[1,256,2304]{2,1,0:T(8,128)(2,1)}, bf16[1,256,2304]{2,1,0:T(8,128)(2,1)S(1)}, u32[]{:S(2)}, u32[]{:S(2)}) collective-permute-start(bf16[1,256,2304]{2,1,0:T(8,128)(2,1)} %get-tuple-element.242), channel_id=1, source_target_pairs={{0,1},{1,0},{2,3},{3,2},{4,5},{5,4},{6,7},{7,6},{8,9},{9,8},{10,11... | collective-permute-start | bytes 3538952 | tf_op jit(solution)/shard_map/ppermute | solution.py:79
  156.8 15.2 %collective-permute-start.22 = (bf16[4,256,256]{2,1,0:T(8,128)(2,1)S(1)}, bf16[4,256,256]{2,1,0:T(8,128)(2,1)S(1)}, u32[]{:S(2)}, u32[]{:S(2)}) collective-permute-start(bf16[4,256,256]{2,1,0:T(8,128)(2,1)S(1)} %get-tuple-element.253), channel_id=1, source_target_pairs={{0,4},{1,5},{2,6},{3,7},{4,0},{5,1},{6,2},{7,3},{8,12},{9,13},{10,... | collective-permute-start | bytes 1572872 | tf_op jit(solution)/shard_map/ppermute | solution.py:79
  159.3 14.9 %collective-permute-start.23 = (bf16[4,256,256]{2,1,0:T(8,128)(2,1)S(1)}, bf16[4,256,256]{2,1,0:T(8,128)(2,1)S(1)}, u32[]{:S(2)}, u32[]{:S(2)}) collective-permute-start(bf16[4,256,256]{2,1,0:T(8,128)(2,1)S(1)} %get-tuple-element.254), channel_id=1, source_target_pairs={{0,2},{1,3},{2,0},{3,1},{4,6},{5,7},{6,4},{7,5},{8,10},{9,11},{10,... | collective-permute-start | bytes 1572872 | tf_op jit(solution)/shard_map/ppermute | solution.py:79
  165.4 19.9 %collective-permute-start.26 = (bf16[1,128,2560]{2,1,0:T(8,128)(2,1)S(1)}, bf16[1,128,2560]{2,1,0:T(8,128)(2,1)S(1)}, u32[]{:S(2)}, u32[]{:S(2)}) collective-permute-start(bf16[1,128,2560]{2,1,0:T(8,128)(2,1)S(1)} %get-tuple-element.265), channel_id=1, source_target_pairs={{0,4},{1,5},{2,6},{3,7},{4,0},{5,1},{6,2},{7,3},{8,12},{9,13},{10,... | collective-permute-start | bytes 1966088 | tf_op jit(solution)/shard_map/ppermute | solution.py:79
  166.5 18.7 %collective-permute-start.25 = (bf16[1,128,2304]{2,1,0:T(8,128)(2,1)S(1)}, bf16[1,128,2304]{2,1,0:T(8,128)(2,1)S(1)}, u32[]{:S(2)}, u32[]{:S(2)}) collective-permute-start(bf16[1,128,2304]{2,1,0:T(8,128)(2,1)S(1)} %get-tuple-element.264), channel_id=1, source_target_pairs={{0,2},{1,3},{2,0},{3,1},{4,6},{5,7},{6,4},{7,5},{8,10},{9,11},{10,... | collective-permute-start | bytes 1769480 | tf_op jit(solution)/shard_map/ppermute | solution.py:79
  174.5 11.0 %collective-permute-start.24 = (bf16[8,128,256]{2,1,0:T(8,128)(2,1)S(1)}, bf16[8,128,256]{2,1,0:T(8,128)(2,1)S(1)}, u32[]{:S(2)}, u32[]{:S(2)}) collective-permute-start(bf16[8,128,256]{2,1,0:T(8,128)(2,1)S(1)} %get-tuple-element.263), channel_id=1, source_target_pairs={{0,8},{1,9},{2,10},{3,11},{4,12},{5,13},{6,14},{7,15},{8,0},{9,1},... | collective-permute-start | bytes 1572872 | tf_op jit(solution)/shard_map/ppermute | solution.py:79
  174.5 15.1 %collective-permute-start.27 = (bf16[512,512]{1,0:T(8,128)(2,1)S(1)}, bf16[512,512]{1,0:T(8,128)(2,1)S(1)}, u32[]{:S(2)}, u32[]{:S(2)}) collective-permute-start(bf16[512,512]{1,0:T(8,128)(2,1)S(1)} %get-tuple-element.274), channel_id=1, source_target_pairs={{1,0},{2,1},{3,2},{5,4},{6,5},{7,6},{9,8},{10,9},{11,10},{13,12},{... | collective-permute-start | bytes 1572872 | tf_op jit(solution)/shard_map/ppermute | solution.py:1182
  185.7 14.6 %collective-permute-start.28 = (bf16[8,64,256]{2,1,0:T(8,128)(2,1)S(1)}, bf16[8,64,256]{2,1,0:T(8,128)(2,1)S(1)}, u32[]{:S(2)}, u32[]{:S(2)}) collective-permute-start(bf16[8,64,256]{2,1,0:T(8,128)(2,1)S(1)} %get-tuple-element.279), channel_id=1, source_target_pairs={{0,16},{1,17},{2,18},{3,19},{4,20},{5,21},{6,22},{7,23},{8,24},{9,... | collective-permute-start | bytes 786440 | tf_op jit(solution)/shard_map/ppermute | solution.py:79
  186.2 14.9 %collective-permute-start.30 = (bf16[1,64,2560]{2,1,0:T(8,128)(2,1)S(1)}, bf16[1,64,2560]{2,1,0:T(8,128)(2,1)S(1)}, u32[]{:S(2)}, u32[]{:S(2)}) collective-permute-start(bf16[1,64,2560]{2,1,0:T(8,128)(2,1)S(1)} %get-tuple-element.284), channel_id=1, source_target_pairs={{0,2},{1,3},{2,0},{3,1},{4,6},{5,7},{6,4},{7,5},{8,10},{9,11},{10,... | collective-permute-start | bytes 983048 | tf_op jit(solution)/shard_map/ppermute | solution.py:79
  188.7 12.3 %collective-permute-start.29 = (bf16[1,64,2304]{2,1,0:T(8,128)(2,1)S(1)}, bf16[1,64,2304]{2,1,0:T(8,128)(2,1)S(1)}, u32[]{:S(2)}, u32[]{:S(2)}) collective-permute-start(bf16[1,64,2304]{2,1,0:T(8,128)(2,1)S(1)} %get-tuple-element.283), channel_id=1, source_target_pairs={{0,4},{1,5},{2,6},{3,7},{4,0},{5,1},{6,2},{7,3},{8,12},{9,13},{10,... | collective-permute-start | bytes 884744 | tf_op jit(solution)/shard_map/ppermute | solution.py:79
  201.2 9.8 %collective-permute-start.31 = (bf16[1,32,4864]{2,1,0:T(8,128)(2,1)S(1)}, bf16[1,32,4864]{2,1,0:T(8,128)(2,1)S(1)}, u32[]{:S(2)}, u32[]{:S(2)}) collective-permute-start(bf16[1,32,4864]{2,1,0:T(8,128)(2,1)S(1)} %get-tuple-element.289), channel_id=1, source_target_pairs={{0,8},{1,9},{2,10},{3,11},{4,12},{5,13},{6,14},{7,15},{8,0},{9,1},... | collective-permute-start | bytes 933896 | tf_op jit(solution)/shard_map/ppermute | solution.py:79
  203.5 12.5 %collective-permute-start.37 = (bf16[1,64,1664]{2,1,0:T(8,128)(2,1)S(1)}, bf16[1,64,1664]{2,1,0:T(8,128)(2,1)S(1)}, u32[]{:S(2)}, u32[]{:S(2)}) collective-permute-start(bf16[1,64,1664]{2,1,0:T(8,128)(2,1)S(1)} %get-tuple-element.300), channel_id=1, source_target_pairs={{0,6},{1,7},{2,4},{3,5},{4,2},{5,3},{6,0},{7,1},{8,14},{9,15},{10,... | collective-permute-start | bytes 638984 | tf_op jit(solution)/shard_map/ppermute | solution.py:79
  211.2 13.4 %collective-permute-start.32 = (bf16[1,16,4864]{2,1,0:T(8,128)(2,1)S(1)}, bf16[1,16,4864]{2,1,0:T(8,128)(2,1)S(1)}, u32[]{:S(2)}, u32[]{:S(2)}) collective-permute-start(bf16[1,16,4864]{2,1,0:T(8,128)(2,1)S(1)} %get-tuple-element.291), channel_id=1, source_target_pairs={{0,16},{1,17},{2,18},{3,19},{4,20},{5,21},{6,22},{7,23},{8,24},{9,... | collective-permute-start | bytes 466952 | tf_op jit(solution)/shard_map/ppermute | solution.py:79
  (67 other events, 855.9 us)
Sparse Core Ops, SparseCore 0:
  11.6 86.6 all-gather.1

commit v6 on v5

--- a/solution.py
+++ b/solution.py
@@ -161,7 +161,7 @@
     lead, rows, columns = keep.shape
     size = rows // radix
     if lead > 1:
-        group = 2 if held == bf16 else 1
+        group = lead if held == bf16 else 1
         steps, block, index = lead // group, (group, rows, columns), lambda i: (i, 0, 0)
     else:
         steps = 2 if columns % 256 == 0 else 1

time: 244 us -> 245 us (level)
  transfers between devices with their start and end apart: 42 -> 42, of which waited for: 20 -> 19; matrix products, arithmetic and copies ran while one was open for 2% -> 2% of each run, Pallas kernels for 36% -> 37%
where the time goes in v6:
time: 245 us; the launch traced here: 244 us
  Pallas kernels  112 us (46%)
  starting transfers between devices  50.8 us (21%)
  waiting for transfers between devices  45.5 us (19%)
  between operations  15.7 us (6%)
  blocking collectives  9.18 us (4%)
  local copies, waits for them, and re-layouts  5.49 us (2%)
  other arithmetic  5.22 us (2%)
    ppermute x39, starting transfers between devices, swap(): return lax.ppermute(block, AXES, [(i, i ^ mask) for i in range(count)])  46.9 us
    ppermute x39, waiting for transfers between devices, swap(): return lax.ppermute(block, AXES, [(i, i ^ mask) for i in range(count)])  45.4 us
    pallas_call x1, Pallas kernels, backward_call(): pl.pallas_call(backward_kernel, grid=(count // ROWS,), in_specs=[smem(),...  21.5 us
    pallas_call x1, Pallas kernels, forward_call(): pl.pallas_call(forward_kernel, grid=(count // ROWS,), in_specs=[smem(), w...  16.5 us
    pallas_call x3, Pallas kernels, attend_back_call(): pl.pallas_call(lambda *refs: attend_back_kernel(pieces, *refs), grid=(blo...  16 us
    pallas_call x1, Pallas kernels, fetch_call(): pl.pallas_call(fetch_kernel, grid=(LEVELS,), in_specs=[smem(), whole(code...  12.9 us
    pallas_call x2, Pallas kernels, spread_call(): pl.pallas_call(lambda *refs: spread_kernel(first, *refs), grid=(levels,),...  10.2 us
    all_to_all x1, blocking collectives, body(): shared = lax.all_to_all(shared, AXES, 0, 0, tiled=True)  9.18 us
  transfers between devices with their start and end apart: 42, of which 19 were waited for; matrix products, arithmetic and copies ran while one was open for 2% of the time, Pallas kernels for 37%

profile of v6, /device:TPU:0, one launch (start us, length us, event | category | flops | bytes accessed | tf_op | source)
XLA Modules:
  0.0 244.2 jit_solution(13894348296143550017)
XLA Ops:
  9.2 3.1 %collective-permute-start = (bf16[16,1664]{1,0:T(8,128)(2,1)}, bf16[16,1664]{1,0:T(8,128)(2,1)S(1)}, u32[]{:S(2)}, u32[]{:S(2)}) collective-permute-start(bf16[16,1664]{1,0:T(8,128)(2,1)} %get-tuple-element.176.refs_0_), channel_id=1, source_target_pairs={{0,8},{1,9},{2,10},{3,11},{4,12},{5,13},{6,14},{7,15},{8,0},{9,1},... | collective-permute-start | bytes 159752 | tf_op jit(solution)/shard_map/ppermute | solution.py:79
  18.7 3.0 %collective-permute-done.2.refs_3_ = bf16[16,1664]{1,0:T(8,128)(2,1)S(1)} collective-permute-done((bf16[16,1664]{1,0:T(8,128)(2,1)}, bf16[16,1664]{1,0:T(8,128)(2,1)S(1)}, u32[]{:S(2)}, u32[]{:S(2)}) %collective-permute-start.2) | collective-permute-done | bytes 53280 | tf_op jit(solution)/shard_map/ppermute | solution.py:79
  31.3 3.3 %collective-permute-start.9 = (bf16[32,4864]{1,0:T(8,128)(2,1)S(1)}, bf16[32,4864]{1,0:T(8,128)(2,1)S(1)}, u32[]{:S(2)}, u32[]{:S(2)}) collective-permute-start(bf16[32,4864]{1,0:T(8,128)(2,1)S(1)} %join_rows.10.refs_0_), channel_id=1, source_target_pairs={{0,8},{1,9},{2,10},{3,11},{4,12},{5,13},{6,14},{7,15},{8,0},{9,1},... | collective-permute-start | bytes 933896 | tf_op jit(solution)/shard_map/ppermute | solution.py:79
  37.8 2.6 %collective-permute-done.9.refs_1_ = bf16[32,4864]{1,0:T(8,128)(2,1)S(1)} collective-permute-done((bf16[32,4864]{1,0:T(8,128)(2,1)S(1)}, bf16[32,4864]{1,0:T(8,128)(2,1)S(1)}, u32[]{:S(2)}, u32[]{:S(2)}) %collective-permute-start.9) | collective-permute-done | bytes 311328 | tf_op jit(solution)/shard_map/ppermute | solution.py:79
  43.2 6.2 %project_rows.1 = (bf16[1024,512]{1,0:T(8,128)(2,1)S(1)}, bf16[1024,512]{1,0:T(8,128)(2,1)S(1)}, bf16[1280,512]{1,0:T(8,128)(2,1)S(1)}, bf16[1280,512]{1,0:T(8,1...) custom-call(s32[32]{0:T(128)S(1)} %get-tuple-element.184.starts, ...), custom_call_target="tpu_custom_call" | custom-call | flops 2000000000 | bytes 25165824 | tf_op jit(solution)/shard_map/project_rows/pallas_call | solution.py:415
  50.0 3.8 %collective-permute-done.10.refs_1_ = bf16[64,2048]{1,0:T(8,128)(2,1)S(1)} collective-permute-done((bf16[64,2048]{1,0:T(8,128)(2,1)S(1)}, bf16[64,2048]{1,0:T(8,128)(2,1)S(1)}, u32[]{:S(2)}, u32[]{:S(2)}) %collective-permute-start.10) | collective-permute-done | bytes 262176 | tf_op jit(solution)/shard_map/ppermute | solution.py:79
  57.7 8.5 %attend_rows.1 = (bf16[1024,512]{1,0:T(8,128)(2,1)S(1)}, f32[8,1024]{1,0:T(8,128)S(1)}) custom-call(bf16[1024,512]{1,0:T(8,128)(2,1)S(1)} %get-tuple-element.194.q.refs_4_.refs_6_, bf16[1280,512]{1,0:T(8,128)(2,1)S(1)} %get-tuple-element.203.k.refs_0_.refs_1_.refs_2_, bf16[1280,512]{1,0:T(8,128)(2,1)S(1)} %get-tuple-element.204.v.refs_2_.refs_3_.refs_4_.refs_5_, ...), custom_call_target="tpu_custom_call" | custom-call | flops 2000000000 | bytes 44040192 | tf_op jit(solution)/shard_map/attend_rows/pallas_call | solution.py:476
  66.2 5.9 %collective-permute-done.12.refs_1_ = bf16[128,2048]{1,0:T(8,128)(2,1)S(1)} collective-permute-done((bf16[128,2048]{1,0:T(8,128)(2,1)S(1)}, bf16[128,2048]{1,0:T(8,128)(2,1)S(1)}, u32[]{:S(2)}, u32[]{:S(2)}) %collective-permute-start.12) | collective-permute-done | bytes 524320 | tf_op jit(solution)/shard_map/ppermute | solution.py:79
  72.1 4.3 %collective-permute-done.13.refs_1_ = bf16[128,2816]{1,0:T(8,128)(2,1)S(1)} collective-permute-done((bf16[128,2816]{1,0:T(8,128)(2,1)S(1)}, bf16[128,2816]{1,0:T(8,128)(2,1)S(1)}, u32[]{:S(2)}, u32[]{:S(2)}) %collective-permute-start.13) | collective-permute-done | bytes 720928 | tf_op jit(solution)/shard_map/ppermute | solution.py:79
  78.0 3.4 %collective-permute-done.14.other_a = bf16[256,2048]{1,0:T(8,128)(2,1)S(1)} collective-permute-done((bf16[256,2048]{1,0:T(8,128)(2,1)S(1)}, bf16[256,2048]{1,0:T(8,128)(2,1)S(1)}, u32[]{:S(2)}, u32[]{:S(2)}) %collective-permute-start.14) | collective-permute-done | bytes 1048608 | tf_op jit(solution)/shard_map/ppermute | solution.py:79
  83.5 16.5 %feed_rows.1 = (bf16[1024,512]{1,0:T(8,128)(2,1)}, f32[1024,512]{1,0:T(8,128)}, bf16[1024,512]{1,0:T(8,128)(2,1)}, bf16[1024,2048]{1,0:T(8,128)(2,1)}, bf16[1024...) custom-call(s32[32]{0:T(128)} %get-tuple-element.180.starts_a, ...), custom_call_target="tpu_custom_call" | custom-call | flops 2000000000 | bytes 53477376 | tf_op jit(solution)/shard_map/feed_rows/pallas_call | solution.py:546
  101.2 12.9 %fetch_codes.1.refs_1_.carried = bf16[8,1024,256]{2,1,0:T(8,128)(2,1)S(1)} custom-call(s32[1]{0:T(128)S(6)} %copy.47.active, s32[16,1024]{1,0:T(8,128)S(1)} %pad_add_fusion.codes.refs_0_, f32[1024,256]{1,0:T(8,128)S(1)} %copy-done.20, bf16[8,2048,256]{2,1,0:T(8,128)(2,1)} %all-gather.2.cloned.1.call-done.book), custom_call_target="tpu_custom_call" | custom-call | flops 2000000000 | bytes 40894464 | tf_op jit(solution)/shard_map/fetch_codes/pallas_call | solution.py:602
  114.2 5.1 %spread_codes.2 = (bf16[4,1024,256]{2,1,0:T(8,128)(2,1)S(1)}, bf16[4,1024,256]{2,1,0:T(8,128)(2,1)S(1)}) custom-call(s32[16,1024]{1,0:T(8,128)S(1)} %pad_add_fusion.codes.refs_0_, bf16[8,1024,256]{2,1,0:T(8,128)(2,1)S(1)} %fetch_codes.1.refs_1_.carried), custom_call_target="tpu_custom_call" | custom-call | flops 500000000 | bytes 15728640 | tf_op jit(solution)/shard_map/spread_codes/pallas_call | solution.py:641
  119.5 5.1 %spread_codes.3 = (bf16[4,1024,256]{2,1,0:T(8,128)(2,1)S(1)}, bf16[4,1024,256]{2,1,0:T(8,128)(2,1)S(1)}) custom-call(s32[16,1024]{1,0:T(8,128)S(1)} %pad_add_fusion.codes.refs_0_, bf16[8,1024,256]{2,1,0:T(8,128)(2,1)S(1)} %fetch_codes.1.refs_1_.carried), custom_call_target="tpu_custom_call" | custom-call | flops 500000000 | bytes 15728640 | tf_op jit(solution)/shard_map/spread_codes/pallas_call | solution.py:641
  132.8 21.5 %feed_back.1 = (bf16[1024,512]{1,0:T(8,128)(2,1)}, bf16[1024,512]{1,0:T(8,128)(2,1)}, f32[8,512]{1,0:T(8,128)}, bf16[1,256,2304]{2,1,0:T(8,128)(2,1)}, bf16[1,25...) custom-call(s32[32]{0:T(128)} %get-tuple-element.189.dests_a, ...), custom_call_target="tpu_custom_call" | custom-call | flops 1000000000 | bytes 78643200 | tf_op jit(solution)/shard_map/feed_back/pallas_call | solution.py:721
  161.3 3.5 %attend_back.3 = (bf16[256,512]{1,0:T(8,128)(2,1)S(1)}, f32[512,512]{1,0:T(8,128)S(1)}, f32[512,512]{1,0:T(8,128)S(1)}, bf16[512,512]{1,0:T(8,128)(2,1)S(1)}) custom-call(bf16[1280,512]{1,0:T(8,128)(2,1)S(1)} %get-tuple-element.203.k.refs_0_.refs_1_.refs_2_, bf16[1280,512]{1,0:T(8,128)(2,1)S(1)} %get-tuple-element.203.k.refs_0_.refs_1_.refs_2_, ...), custom_call_target="tpu_custom_call" | custom-call | flops 4000000000 | bytes 12582912 | tf_op jit(solution)/shard_map/attend_back/pallas_call | solution.py:811
  167.1 4.3 %attend_back.4 = (bf16[256,512]{1,0:T(8,128)(2,1)S(1)}, f32[512,512]{1,0:T(8,128)S(1)}, f32[512,512]{1,0:T(8,128)S(1)}, bf16[512,512]{1,0:T(8,128)(2,1)}) custom-call(bf16[1280,512]{1,0:T(8,128)(2,1)S(1)} %get-tuple-element.203.k.refs_0_.refs_1_.refs_2_, bf16[1280,512]{1,0:T(8,128)(2,1)S(1)} %get-tuple-element.203.k.refs_0_.refs_1_.refs_2_, ...), custom_call_target="tpu_custom_call" | custom-call | bytes 12582912 | tf_op jit(solution)/shard_map/attend_back/pallas_call | solution.py:811
  176.0 8.1 %attend_back.5 = (bf16[512,512]{1,0:T(8,128)(2,1)S(1)}, f32[768,512]{1,0:T(8,128)S(1)}, f32[768,512]{1,0:T(8,128)S(1)}, bf16[512,512]{1,0:T(8,128)(2,1)}) custom-call(bf16[1280,512]{1,0:T(8,128)(2,1)S(1)} %get-tuple-element.203.k.refs_0_.refs_1_.refs_2_, bf16[1280,512]{1,0:T(8,128)(2,1)S(1)} %get-tuple-element.203.k.refs_0_.refs_1_.refs_2_, ...), custom_call_target="tpu_custom_call" | custom-call | bytes 25165824 | tf_op jit(solution)/shard_map/attend_back/pallas_call | solution.py:811
  189.9 7.9 %finish_rows.1 = (f32[1024,512]{1,0:T(8,128)}, bf16[1,256,768]{2,1,0:T(8,128)(2,1)S(1)}, bf16[1,256,768]{2,1,0:T(8,128)(2,1)S(1)}, bf16[1,256,896]{2,1,0:T(8,128)(2,1)S(1)}, bf16[1,256,896]{2,1,0:T(8,128)(2,1)S(1)}) custom-call(s32[32]{0:T(128)S(1)} %get-tuple-element.188.dests, s32[1,128]{1,0:T(1,128)S(1)} %copy-done.31, bf16[1024,512]{1,0:T(8,128)(2,1)S(1)} %copy-done.11, ...), custom_call_target="tpu_custom_call" | custom-call | bytes 31457280 | tf_op jit(solution)/shard_map/finish_rows/pallas_call | solution.py:910
  203.7 2.7 %collective-permute-start.37 = (bf16[1,64,1664]{2,1,0:T(8,128)(2,1)S(1)}, bf16[1,64,1664]{2,1,0:T(8,128)(2,1)S(1)}, u32[]{:S(2)}, u32[]{:S(2)}) collective-permute-start(bf16[1,64,1664]{2,1,0:T(8,128)(2,1)S(1)} %get-tuple-element.300), channel_id=1, source_target_pairs={{0,6},{1,7},{2,4},{3,5},{4,2},{5,3},{6,0},{7,1},{8,14},{9,15},{10,... | collective-permute-start | bytes 638984 | tf_op jit(solution)/shard_map/ppermute | solution.py:79
  206.4 4.7 %collective-permute-done.31.refs_1_ = bf16[1,32,4864]{2,1,0:T(8,128)(2,1)S(1)} collective-permute-done((bf16[1,32,4864]{2,1,0:T(8,128)(2,1)S(1)}, bf16[1,32,4864]{2,1,0:T(8,128)(2,1)S(1)}, u32[]{:S(2)}, u32[]{:S(2)}) %collective-permute-start.31) | collective-permute-done | bytes 311328 | tf_op jit(solution)/shard_map/ppermute | solution.py:79
  211.7 4.5 %collective-permute-done.37.refs_3_ = bf16[1,64,1664]{2,1,0:T(8,128)(2,1)S(1)} collective-permute-done((bf16[1,64,1664]{2,1,0:T(8,128)(2,1)S(1)}, bf16[1,64,1664]{2,1,0:T(8,128)(2,1)S(1)}, u32[]{:S(2)}, u32[]{:S(2)}) %collective-permute-start.37) | collective-permute-done | bytes 213024 | tf_op jit(solution)/shard_map/ppermute | solution.py:79
  217.4 3.3 %collective-permute-start.40 = (bf16[1,16,1664]{2,1,0:T(8,128)(2,1)S(1)}, bf16[1,16,1664]{2,1,0:T(8,128)(2,1)S(1)}, u32[]{:S(2)}, u32[]{:S(2)}) collective-permute-start(bf16[1,16,1664]{2,1,0:T(8,128)(2,1)S(1)} %get-tuple-element.304), channel_id=1, source_target_pairs={{0,24},{1,25},{2,26},{3,27},{4,28},{5,29},{6,30},{7,31},{8,16},{9,... | collective-permute-start | bytes 159752 | tf_op jit(solution)/shard_map/ppermute | solution.py:79
  225.7 9.2 %all_to_all.11 = f32[32,1,128]{2,1,0:T(1,128)S(1)} all-to-all(f32[32,1,128]{2,1,0:T(1,128)S(1)} %bitcast.9), channel_id=1, replica_groups=mesh['clip'=8,'tm'=4] {'clip','tm'}, dimensions={0} | all-to-all | bytes 32768 | tf_op jit(solution)/shard_map/all_to_all | solution.py:1221
  (215 shorter events, 75.1 us)
Async XLA Ops:
  7.2 92.8 %all-gather.2.cloned.1.call-start = ((), (), s32[]{:S(2)}) async-start(), calls=%async_computation.1 | async-start | bytes 8650752 | tf_op jit(solution)/shard_map/all_gather | solution.py:1098
  14.9 16.4 %collective-permute-start.8 = (bf16[16,4864]{1,0:T(8,128)(2,1)}, bf16[16,4864]{1,0:T(8,128)(2,1)S(1)}, u32[]{:S(2)}, u32[]{:S(2)}) collective-permute-start(bf16[16,4864]{1,0:T(8,128)(2,1)} %get-tuple-element.196.refs_0_), channel_id=1, source_target_pairs={{0,16},{1,17},{2,18},{3,19},{4,20},{5,21},{6,22},{7,23},{8,24},{9,... | collective-permute-start | bytes 466952 | tf_op jit(solution)/shard_map/ppermute | solution.py:79
  22.5 12.1 %collective-permute-start.4 = (bf16[64,1664]{1,0:T(8,128)(2,1)S(1)}, bf16[64,1664]{1,0:T(8,128)(2,1)S(1)}, u32[]{:S(2)}, u32[]{:S(2)}) collective-permute-start(bf16[64,1664]{1,0:T(8,128)(2,1)S(1)} %join_rows.8.refs_0_), channel_id=1, source_target_pairs={{0,2},{1,3},{2,0},{3,1},{4,6},{5,7},{6,4},{7,5},{8,10},{9,11},{10,... | collective-permute-start | bytes 638984 | tf_op jit(solution)/shard_map/ppermute | solution.py:79
  24.1 10.5 %collective-permute-start.5 = (bf16[64,1664]{1,0:T(8,128)(2,1)S(1)}, bf16[64,1664]{1,0:T(8,128)(2,1)S(1)}, u32[]{:S(2)}, u32[]{:S(2)}) collective-permute-start(bf16[64,1664]{1,0:T(8,128)(2,1)S(1)} %join_rows.8.refs_0_), channel_id=1, source_target_pairs={{0,4},{1,5},{2,6},{3,7},{4,0},{5,1},{6,2},{7,3},{8,12},{9,13},{10,... | collective-permute-start | bytes 638984 | tf_op jit(solution)/shard_map/ppermute | solution.py:79
  40.5 13.3 %collective-permute-start.11 = (bf16[64,2816]{1,0:T(8,128)(2,1)S(1)}, bf16[64,2816]{1,0:T(8,128)(2,1)S(1)}, u32[]{:S(2)}, u32[]{:S(2)}) collective-permute-start(bf16[64,2816]{1,0:T(8,128)(2,1)S(1)} %get-tuple-element.200.refs_0_), channel_id=1, source_target_pairs={{0,2},{1,3},{2,0},{3,1},{4,6},{5,7},{6,4},{7,5},{8,10},{9,11},{10,... | collective-permute-start | bytes 1081352 | tf_op jit(solution)/shard_map/ppermute | solution.py:79
  42.0 11.8 %collective-permute-start.10 = (bf16[64,2048]{1,0:T(8,128)(2,1)S(1)}, bf16[64,2048]{1,0:T(8,128)(2,1)S(1)}, u32[]{:S(2)}, u32[]{:S(2)}) collective-permute-start(bf16[64,2048]{1,0:T(8,128)(2,1)S(1)} %get-tuple-element.199.refs_0_), channel_id=1, source_target_pairs={{0,4},{1,5},{2,6},{3,7},{4,0},{5,1},{6,2},{7,3},{8,12},{9,13},{10,... | collective-permute-start | bytes 786440 | tf_op jit(solution)/shard_map/ppermute | solution.py:79
  53.8 22.7 %collective-permute-start.13 = (bf16[128,2816]{1,0:T(8,128)(2,1)S(1)}, bf16[128,2816]{1,0:T(8,128)(2,1)S(1)}, u32[]{:S(2)}, u32[]{:S(2)}) collective-permute-start(bf16[128,2816]{1,0:T(8,128)(2,1)S(1)} %join_rows.13.refs_0_), channel_id=1, source_target_pairs={{0,4},{1,5},{2,6},{3,7},{4,0},{5,1},{6,2},{7,3},{8,12},{9,13},{10,... | collective-permute-start | bytes 2162696 | tf_op jit(solution)/shard_map/ppermute | solution.py:79
  56.0 16.1 %collective-permute-start.12 = (bf16[128,2048]{1,0:T(8,128)(2,1)S(1)}, bf16[128,2048]{1,0:T(8,128)(2,1)S(1)}, u32[]{:S(2)}, u32[]{:S(2)}) collective-permute-start(bf16[128,2048]{1,0:T(8,128)(2,1)S(1)} %join_rows.12.refs_0_), channel_id=1, source_target_pairs={{0,2},{1,3},{2,0},{3,1},{4,6},{5,7},{6,4},{7,5},{8,10},{9,11},{10,... | collective-permute-start | bytes 1572872 | tf_op jit(solution)/shard_map/ppermute | solution.py:79
  126.4 28.5 %collective-permute-start.19 = (bf16[4,512,256]{2,1,0:T(8,128)(2,1)}, bf16[4,512,256]{2,1,0:T(8,128)(2,1)S(1)}, u32[]{:S(2)}, u32[]{:S(2)}) collective-permute-start(bf16[4,512,256]{2,1,0:T(8,128)(2,1)} %get-tuple-element.233), channel_id=1, source_target_pairs={{0,4},{1,5},{2,6},{3,7},{4,0},{5,1},{6,2},{7,3},{8,12},{9,13},{10,... | collective-permute-start | bytes 3145736 | tf_op jit(solution)/shard_map/ppermute | solution.py:79
  130.3 26.4 %collective-permute-start.18 = (bf16[4,512,256]{2,1,0:T(8,128)(2,1)}, bf16[4,512,256]{2,1,0:T(8,128)(2,1)S(1)}, u32[]{:S(2)}, u32[]{:S(2)}) collective-permute-start(bf16[4,512,256]{2,1,0:T(8,128)(2,1)} %get-tuple-element.232), channel_id=1, source_target_pairs={{0,2},{1,3},{2,0},{3,1},{4,6},{5,7},{6,4},{7,5},{8,10},{9,11},{10,... | collective-permute-start | bytes 3145736 | tf_op jit(solution)/shard_map/ppermute | solution.py:79
  154.3 10.5 %collective-permute-start.21 = (bf16[1,256,2560]{2,1,0:T(8,128)(2,1)}, bf16[1,256,2560]{2,1,0:T(8,128)(2,1)S(1)}, u32[]{:S(2)}, u32[]{:S(2)}) collective-permute-start(bf16[1,256,2560]{2,1,0:T(8,128)(2,1)} %get-tuple-element.243), channel_id=1, source_target_pairs={{0,1},{1,0},{2,3},{3,2},{4,5},{5,4},{6,7},{7,6},{8,9},{9,8},{10,11... | collective-permute-start | bytes 3932168 | tf_op jit(solution)/shard_map/ppermute | solution.py:79
  154.4 10.4 %collective-permute-start.20 = (bf16[1,256,2304]{2,1,0:T(8,128)(2,1)}, bf16[1,256,2304]{2,1,0:T(8,128)(2,1)S(1)}, u32[]{:S(2)}, u32[]{:S(2)}) collective-permute-start(bf16[1,256,2304]{2,1,0:T(8,128)(2,1)} %get-tuple-element.242), channel_id=1, source_target_pairs={{0,1},{1,0},{2,3},{3,2},{4,5},{5,4},{6,7},{7,6},{8,9},{9,8},{10,11... | collective-permute-start | bytes 3538952 | tf_op jit(solution)/shard_map/ppermute | solution.py:79
  157.0 15.2 %collective-permute-start.22 = (bf16[4,256,256]{2,1,0:T(8,128)(2,1)S(1)}, bf16[4,256,256]{2,1,0:T(8,128)(2,1)S(1)}, u32[]{:S(2)}, u32[]{:S(2)}) collective-permute-start(bf16[4,256,256]{2,1,0:T(8,128)(2,1)S(1)} %get-tuple-element.253), channel_id=1, source_target_pairs={{0,4},{1,5},{2,6},{3,7},{4,0},{5,1},{6,2},{7,3},{8,12},{9,13},{10,... | collective-permute-start | bytes 1572872 | tf_op jit(solution)/shard_map/ppermute | solution.py:79
  159.4 14.9 %collective-permute-start.23 = (bf16[4,256,256]{2,1,0:T(8,128)(2,1)S(1)}, bf16[4,256,256]{2,1,0:T(8,128)(2,1)S(1)}, u32[]{:S(2)}, u32[]{:S(2)}) collective-permute-start(bf16[4,256,256]{2,1,0:T(8,128)(2,1)S(1)} %get-tuple-element.254), channel_id=1, source_target_pairs={{0,2},{1,3},{2,0},{3,1},{4,6},{5,7},{6,4},{7,5},{8,10},{9,11},{10,... | collective-permute-start | bytes 1572872 | tf_op jit(solution)/shard_map/ppermute | solution.py:79
  165.5 19.9 %collective-permute-start.26 = (bf16[1,128,2560]{2,1,0:T(8,128)(2,1)S(1)}, bf16[1,128,2560]{2,1,0:T(8,128)(2,1)S(1)}, u32[]{:S(2)}, u32[]{:S(2)}) collective-permute-start(bf16[1,128,2560]{2,1,0:T(8,128)(2,1)S(1)} %get-tuple-element.265), channel_id=1, source_target_pairs={{0,4},{1,5},{2,6},{3,7},{4,0},{5,1},{6,2},{7,3},{8,12},{9,13},{10,... | collective-permute-start | bytes 1966088 | tf_op jit(solution)/shard_map/ppermute | solution.py:79
  166.7 18.7 %collective-permute-start.25 = (bf16[1,128,2304]{2,1,0:T(8,128)(2,1)S(1)}, bf16[1,128,2304]{2,1,0:T(8,128)(2,1)S(1)}, u32[]{:S(2)}, u32[]{:S(2)}) collective-permute-start(bf16[1,128,2304]{2,1,0:T(8,128)(2,1)S(1)} %get-tuple-element.264), channel_id=1, source_target_pairs={{0,2},{1,3},{2,0},{3,1},{4,6},{5,7},{6,4},{7,5},{8,10},{9,11},{10,... | collective-permute-start | bytes 1769480 | tf_op jit(solution)/shard_map/ppermute | solution.py:79
  174.6 11.0 %collective-permute-start.24 = (bf16[8,128,256]{2,1,0:T(8,128)(2,1)S(1)}, bf16[8,128,256]{2,1,0:T(8,128)(2,1)S(1)}, u32[]{:S(2)}, u32[]{:S(2)}) collective-permute-start(bf16[8,128,256]{2,1,0:T(8,128)(2,1)S(1)} %get-tuple-element.263), channel_id=1, source_target_pairs={{0,8},{1,9},{2,10},{3,11},{4,12},{5,13},{6,14},{7,15},{8,0},{9,1},... | collective-permute-start | bytes 1572872 | tf_op jit(solution)/shard_map/ppermute | solution.py:79
  174.7 15.1 %collective-permute-start.27 = (bf16[512,512]{1,0:T(8,128)(2,1)S(1)}, bf16[512,512]{1,0:T(8,128)(2,1)S(1)}, u32[]{:S(2)}, u32[]{:S(2)}) collective-permute-start(bf16[512,512]{1,0:T(8,128)(2,1)S(1)} %get-tuple-element.274), channel_id=1, source_target_pairs={{1,0},{2,1},{3,2},{5,4},{6,5},{7,6},{9,8},{10,9},{11,10},{13,12},{... | collective-permute-start | bytes 1572872 | tf_op jit(solution)/shard_map/ppermute | solution.py:1182
  185.9 14.6 %collective-permute-start.28 = (bf16[8,64,256]{2,1,0:T(8,128)(2,1)S(1)}, bf16[8,64,256]{2,1,0:T(8,128)(2,1)S(1)}, u32[]{:S(2)}, u32[]{:S(2)}) collective-permute-start(bf16[8,64,256]{2,1,0:T(8,128)(2,1)S(1)} %get-tuple-element.279), channel_id=1, source_target_pairs={{0,16},{1,17},{2,18},{3,19},{4,20},{5,21},{6,22},{7,23},{8,24},{9,... | collective-permute-start | bytes 786440 | tf_op jit(solution)/shard_map/ppermute | solution.py:79
  186.4 14.8 %collective-permute-start.30 = (bf16[1,64,2560]{2,1,0:T(8,128)(2,1)S(1)}, bf16[1,64,2560]{2,1,0:T(8,128)(2,1)S(1)}, u32[]{:S(2)}, u32[]{:S(2)}) collective-permute-start(bf16[1,64,2560]{2,1,0:T(8,128)(2,1)S(1)} %get-tuple-element.284), channel_id=1, source_target_pairs={{0,2},{1,3},{2,0},{3,1},{4,6},{5,7},{6,4},{7,5},{8,10},{9,11},{10,... | collective-permute-start | bytes 983048 | tf_op jit(solution)/shard_map/ppermute | solution.py:79
  188.9 12.3 %collective-permute-start.29 = (bf16[1,64,2304]{2,1,0:T(8,128)(2,1)S(1)}, bf16[1,64,2304]{2,1,0:T(8,128)(2,1)S(1)}, u32[]{:S(2)}, u32[]{:S(2)}) collective-permute-start(bf16[1,64,2304]{2,1,0:T(8,128)(2,1)S(1)} %get-tuple-element.283), channel_id=1, source_target_pairs={{0,4},{1,5},{2,6},{3,7},{4,0},{5,1},{6,2},{7,3},{8,12},{9,13},{10,... | collective-permute-start | bytes 884744 | tf_op jit(solution)/shard_map/ppermute | solution.py:79
  201.3 9.8 %collective-permute-start.31 = (bf16[1,32,4864]{2,1,0:T(8,128)(2,1)S(1)}, bf16[1,32,4864]{2,1,0:T(8,128)(2,1)S(1)}, u32[]{:S(2)}, u32[]{:S(2)}) collective-permute-start(bf16[1,32,4864]{2,1,0:T(8,128)(2,1)S(1)} %get-tuple-element.289), channel_id=1, source_target_pairs={{0,8},{1,9},{2,10},{3,11},{4,12},{5,13},{6,14},{7,15},{8,0},{9,1},... | collective-permute-start | bytes 933896 | tf_op jit(solution)/shard_map/ppermute | solution.py:79
  203.7 12.5 %collective-permute-start.37 = (bf16[1,64,1664]{2,1,0:T(8,128)(2,1)S(1)}, bf16[1,64,1664]{2,1,0:T(8,128)(2,1)S(1)}, u32[]{:S(2)}, u32[]{:S(2)}) collective-permute-start(bf16[1,64,1664]{2,1,0:T(8,128)(2,1)S(1)} %get-tuple-element.300), channel_id=1, source_target_pairs={{0,6},{1,7},{2,4},{3,5},{4,2},{5,3},{6,0},{7,1},{8,14},{9,15},{10,... | collective-permute-start | bytes 638984 | tf_op jit(solution)/shard_map/ppermute | solution.py:79
  211.4 13.4 %collective-permute-start.32 = (bf16[1,16,4864]{2,1,0:T(8,128)(2,1)S(1)}, bf16[1,16,4864]{2,1,0:T(8,128)(2,1)S(1)}, u32[]{:S(2)}, u32[]{:S(2)}) collective-permute-start(bf16[1,16,4864]{2,1,0:T(8,128)(2,1)S(1)} %get-tuple-element.291), channel_id=1, source_target_pairs={{0,16},{1,17},{2,18},{3,19},{4,20},{5,21},{6,22},{7,23},{8,24},{9,... | collective-permute-start | bytes 466952 | tf_op jit(solution)/shard_map/ppermute | solution.py:79
  (67 other events, 855.8 us)
Sparse Core Ops, SparseCore 0:
  11.6 86.6 all-gather.1
